TPU v7x, 32 devices: a whole 2x2x4 slice. The times are simulated.
32 devices in a mesh: blk: 2 (over x), seq: 16 (over z, y, core).
Axes of the slice: x: 2, y: 2, z: 4, core: 2. Of those that a mesh axis runs over, the one named last changes fastest.
Arguments:
- byte_ids: int32 [64, 1032], P('seq'), may hold values from 0 to 258
- lengths: int32 [64], P('seq'), may hold values from 1 to 1032, 49536 in all
- lang_ids: int32 [64], P('seq'), may hold values from 0 to 7
- owners: int32 [3], replicated, may hold values from 0 to 15
- table: float32 [259, 768], replicated, may hold values from -6 to 6
- conv_w: float32 [5, 768], replicated, may hold values from -3 to 3
- score_w: float32 [8, 768], replicated, may hold values from -0.4375 to 0.4375
- cotangent: bfloat16 [64, 516, 768], P('seq', None, 'blk'), may hold values from -6 to 6
- table_m: float32 [259, 768], P(None, 'blk'), may hold values from -6 to 6
- table_v: float32 [259, 768], P(None, 'blk'), may hold values from 0.01719 to 0.06876
- convolution_first_moment: float32 [5, 768], P(None, 'blk'), may hold values from -40 to 40
- convolution_second_moment: float32 [5, 768], P(None, 'blk'), may hold values from 4.45824 to 17.83296
- score_m: float32 [8, 768], P(None, 'blk'), may hold values from -6 to 6
- score_v: float32 [8, 768], P(None, 'blk'), may hold values from 0.06192 to 0.24768
Outputs:
- pooled_rows: bfloat16 [64, 516, 768], P('seq', None, 'blk')
- table_m_new: float32 [16, 259, 768], P('seq', None, 'blk')
- table_v_new: float32 [16, 259, 768], P('seq', None, 'blk')
- table_new: float32 [16, 259, 768], P('seq', None, 'blk')
- conv_m_new: float32 [16, 5, 768], P('seq', None, 'blk')
- conv_v_new: float32 [16, 5, 768], P('seq', None, 'blk')
- conv_new: float32 [16, 5, 768], P('seq', None, 'blk')
- score_m_new: float32 [16, 8, 768], P('seq', None, 'blk')
- score_v_new: float32 [16, 8, 768], P('seq', None, 'blk')
- score_new: float32 [16, 8, 768], P('seq', None, 'blk')
Inputs may be any that keep to these rules, and one draw needn't show every extreme that they name: `lengths`: the longest sequence has exactly 1032 live positions.
All inputs are finite; a program needn't handle non-finite values. No bound on the sum of `lengths` on one device may be relied on, other than what follows from the above.
Results may differ from a plain program's by a relative error of at most 0.0049.
The roundings to bfloat16 on the way count: a program that leaves them out, or rounds other values in their place, can miss the bound.
Values may be sent and summed in bfloat16 or wider, within the bound.
No kernel may reach another device: no remote copies, remote signals or barrier semaphores. Data moves between devices by JAX's collectives and lax.ppermute only.
A program may use at most 384 MiB of HBM per device.

v0:
```python
import functools

import jax
import jax.numpy as jnp
from jax import lax
from jax.sharding import PartitionSpec as P

STEP_NUMBER = 5


def shifted_rows(field, offset):
    slot_len = field.shape[1]
    if offset == 0:
        return field
    if offset > 0:
        widths = [(0, 0)] * field.ndim
        widths[1] = (0, offset)
        return jnp.pad(field, widths)[:, offset : offset + slot_len]
    widths = [(0, 0)] * field.ndim
    widths[1] = (-offset, 0)
    return jnp.pad(field, widths)[:, :slot_len]


def block_total(field, size_val):
    slot_len = field.shape[1]
    within = jnp.arange(slot_len, dtype=jnp.int32) % size_val
    total = jnp.zeros_like(field)
    for offset in range(-(size_val - 1), size_val):
        keep = (within + offset >= 0) & (within + offset < size_val)
        keep = keep.astype(field.dtype)
        if field.ndim == 3:
            keep = keep[:, None]
        total = total + keep * shifted_rows(field, offset)
    return total


def pool_size(field, live_mask, size_val):
    totals = block_total(field * live_mask[..., None], size_val)
    tallied_count = block_total(live_mask, size_val)
    return totals / jnp.maximum(tallied_count, 1.0)[..., None]


def unpool_size(grad, live_mask, size_val):
    totals = block_total(grad, size_val)
    tallied_count = block_total(live_mask, size_val)
    return totals / jnp.maximum(tallied_count, 1.0)[..., None] * live_mask[..., None]


def by_size(blk_index, size_slot, compute):
    return lax.switch(
        blk_index,
        [functools.partial(compute, 2 * blk_level + size_slot + 1) for blk_level in range(2)],
    )


def convolve(embedded, taps):
    result = taps[4] + jnp.zeros_like(embedded)
    for tap_index in range(4):
        shifted = jnp.pad(embedded, ((0, 0), (tap_index, 0), (0, 0)))[:, : embedded.shape[1]]
        result = result + taps[tap_index] * shifted
    return result


def conv_backward(grad_conv, embedded, taps):
    slot_len = grad_conv.shape[1]
    grad_embedded = jnp.zeros_like(grad_conv)
    tap_grads = []
    for tap_index in range(4):
        ahead = jnp.pad(grad_conv, ((0, 0), (0, tap_index), (0, 0)))[:, tap_index:]
        grad_embedded = grad_embedded + taps[tap_index] * ahead
        behind = jnp.pad(embedded, ((0, 0), (tap_index, 0), (0, 0)))[:, :slot_len]
        tap_grads.append(jnp.sum(grad_conv * behind, axis=(0, 1)))
    tap_grads.append(jnp.sum(grad_conv, axis=(0, 1)))
    return (grad_embedded, jnp.stack(tap_grads))


def table_grad(indicator_rows, grad_embedded, live_mask, vocab):
    rounded = (grad_embedded * live_mask[..., None]).astype(jnp.bfloat16)
    flat = rounded.reshape(-1, rounded.shape[2])
    summed = jnp.dot(indicator_rows, flat, preferred_element_type=jnp.float32)
    return summed[:vocab]


def adamw(weight, grad, moment, second, rate):
    new_m = 0.9 * moment + 0.1 * grad
    new_v = 0.999 * second + 0.001 * grad * grad
    m_hat = new_m / (1.0 - 0.9**STEP_NUMBER)
    v_hat = new_v / (1.0 - 0.999**STEP_NUMBER)
    new_w = weight - rate * (m_hat / (jnp.sqrt(v_hat) + 1e-08) + 0.01 * weight)
    return (new_m, new_v, new_w)


def local(
    byte_ids,
    lengths,
    lang_ids,
    owners,
    table,
    conv_w,
    score_w,
    cotangent,
    table_m,
    table_v,
    convolution_first_moment,
    convolution_second_moment,
    score_m,
    score_v,
):
    seq_count, slot_len = byte_ids.shape
    vocab, channels = table.shape
    half_width = channels // 2
    blk_index = lax.axis_index("blk")
    seq_index = lax.axis_index("seq")
    places = jnp.arange(slot_len, dtype=jnp.int32)
    live_mask = (places[None, :] < lengths[:, None]).astype(jnp.float32)
    table_rows = (vocab + 127) // 128 * 128
    indicator_rows = (
        jnp.arange(table_rows, dtype=jnp.int32)[:, None]
        == byte_ids.reshape(1, seq_count * slot_len)
    ).astype(jnp.bfloat16)
    table_low = table.astype(jnp.bfloat16)
    lang_hot = (lang_ids[:, None] == jnp.arange(score_w.shape[0], dtype=jnp.int32)).astype(
        jnp.float32
    )
    fetched_rows = jnp.take(table_low, byte_ids, axis=0).astype(jnp.float32)
    embedded = fetched_rows * live_mask[..., None]
    convolved = convolve(embedded, conv_w)
    score_vec = jnp.dot(lang_hot, score_w, precision=lax.Precision.HIGHEST)

    def pooled_for(size_val):
        return pool_size(convolved, live_mask, size_val)

    pooled = [by_size(blk_index, size_slot, pooled_for) for size_slot in (0, 1)]
    my_scores = jnp.stack([jnp.sum(entry * score_vec[:, None, :], axis=-1) for entry in pooled])
    all_scores = lax.all_gather(my_scores, "blk", axis=0, tiled=True)
    soft = jax.nn.softmax(all_scores, axis=0)
    mine = lax.dynamic_slice_in_dim(soft, blk_index * 2, 2, 0)
    partial_mix = (mine[0][..., None] * pooled[0] + mine[1][..., None] * pooled[1]) * live_mask[
        ..., None
    ]
    down_part = 0.5 * jnp.sum(partial_mix.reshape(seq_count, slot_len // 2, 2, channels), axis=2)
    pooled_rows = lax.psum_scatter(down_part, "blk", scatter_dimension=2, tiled=True).astype(
        jnp.bfloat16
    )
    cot_full = lax.all_gather(cotangent, "blk", axis=2, tiled=True).astype(jnp.float32)
    grad_mixed = 0.5 * jnp.repeat(cot_full, 2, axis=1) * live_mask[..., None]
    inner = [jnp.sum(grad_mixed * entry, axis=-1) for entry in pooled]
    weighted = lax.psum(mine[0] * inner[0] + mine[1] * inner[1], "blk")
    grad_scores = [mine[size_slot] * (inner[size_slot] - weighted) for size_slot in (0, 1)]
    grad_pooled = [
        mine[size_slot][..., None] * grad_mixed
        + grad_scores[size_slot][..., None] * score_vec[:, None, :]
        for size_slot in (0, 1)
    ]
    score_seq = jnp.sum(
        grad_scores[0][..., None] * pooled[0] + grad_scores[1][..., None] * pooled[1], axis=1
    )
    score_part = jnp.dot(lang_hot.T, score_seq, precision=lax.Precision.HIGHEST)

    def unpool_first(size_val):
        return unpool_size(grad_pooled[0], live_mask, size_val)

    def unpool_second(size_val):
        return unpool_size(grad_pooled[1], live_mask, size_val)

    grad_conv = by_size(blk_index, 0, unpool_first) + by_size(blk_index, 1, unpool_second)
    flat_grad = grad_conv.reshape(seq_count * slot_len, channels)
    whole_grad, score_whole = lax.psum((flat_grad, score_part), "blk")
    grad_embedded, tap_whole = conv_backward(
        whole_grad.reshape(seq_count, slot_len, channels), embedded, conv_w
    )
    table_whole = table_grad(indicator_rows, grad_embedded, live_mask, vocab)
    table_local = lax.dynamic_slice_in_dim(table_whole, blk_index * half_width, half_width, 1)
    tap_local = lax.dynamic_slice_in_dim(tap_whole, blk_index * half_width, half_width, 1)
    score_local = lax.dynamic_slice_in_dim(score_whole, blk_index * half_width, half_width, 1)
    table_sum, tap_sum, score_sum = lax.psum((table_local, tap_local, score_local), "seq")
    output_values = [pooled_rows]
    for weight, grad, moment, second, rate, owner in (
        (table, table_sum, table_m, table_v, 0.5, owners[0]),
        (conv_w, tap_sum, convolution_first_moment, convolution_second_moment, 0.3, owners[1]),
        (score_w, score_sum, score_m, score_v, 0.05, owners[2]),
    ):
        weight_half = lax.dynamic_slice_in_dim(weight, blk_index * half_width, half_width, 1)
        new_m, new_v, new_w = adamw(weight_half, grad, moment, second, rate)
        hit = (seq_index == owner).astype(jnp.float32)
        output_values = output_values + [hit * new_m[None], hit * new_v[None], hit * new_w[None]]
    return (
        output_values[0],
        output_values[1],
        output_values[2],
        output_values[3],
        output_values[4],
        output_values[5],
        output_values[6],
        output_values[7],
        output_values[8],
        output_values[9],
    )


def solution(mesh):
    return jax.shard_map(
        local,
        mesh=mesh,
        in_specs=(
            P("seq", None),
            P("seq"),
            P("seq"),
            P(),
            P(),
            P(),
            P(),
            P("seq", None, "blk"),
            P(None, "blk"),
            P(None, "blk"),
            P(None, "blk"),
            P(None, "blk"),
            P(None, "blk"),
            P(None, "blk"),
        ),
        out_specs=(
            P("seq", None, "blk"),
            P("seq", None, "blk"),
            P("seq", None, "blk"),
            P("seq", None, "blk"),
            P("seq", None, "blk"),
            P("seq", None, "blk"),
            P("seq", None, "blk"),
            P("seq", None, "blk"),
            P("seq", None, "blk"),
            P("seq", None, "blk"),
        ),
        check_vma=False,
    )
```

profile of v0, /device:TPU:0, one launch (start us, length us, event | category | flops | bytes accessed | tf_op | source)
XLA Modules:
  0.0 799.9 jit_solution(15969820804139954129)
XLA Ops:
  11.8 13.6 %gather_fusion = bf16[4128,768]{1,0:T(8,128)(2,1)} fusion(bf16[259,768]{1,0:T(8,128)(2,1)S(1)} %convert_element_type.549, s32[5120]{0:T(1024)S(1)} %pad_clamp_fusion), kind=kCustom, calls=%fused_computation | custom fusion | bytes 12697728 | tf_op jit(solution)/shard_map/jit(_take)/gather | solution.py:125
  25.4 5.2 convert_multiply_fusion
  30.7 8.7 %multiply_add_fusion.5 = f32[4,1032,768]{2,1,0:T(8,128)} fusion(f32[4,1032,768]{2,1,0:T(8,128)S(1)} %convert_multiply_fusion, f32[768]{0:T(1024)S(1)} %get-tuple-element.125, f32[768]{0:T(1024)S(1)} %get-tuple-element.122, f32[768]{0:T(1024)S(1)} %get-tuple-element.123, f32[768]{0:T(1024)S(1)} %get-tuple-element.124, f32[768]{0:T(1024)S(1)} %get-tuple-element.121), kind=kLoop, calls=%fused_computation.290 | loop fusion | flops 25362432 | bytes 25377792 | tf_op jit(solution)/shard_map/add | solution.py:60
  39.4 29.0 %conditional.5 = (f32[4,1032,768]{2,1,0:T(8,128)}) conditional(s32[]{:T(128)} %clamp.2, (f32[4,1032]{1,0:T(4,128)S(1)}, f32[4,1032,768]{2,1,0:T(8,128)}) %tuple.46, (f32[4,1032]{1,0:T(4,128)S(1)}, f32[4,1032,768]{2,1,0:T(8,128)}) %tuple.46), branch_computations={%region_3.4_spmd, %region_4.5_spmd} | conditional | flops 47672208 | bytes 50877608 | solution.py:50
  39.4 10.0 %broadcast_multiply_fusion.2 = f32[4,1032,768]{2,1,0:T(8,128)} fusion(f32[4,1032,768]{2,1,0:T(8,128)} %get-tuple-element.60, f32[4,1032]{1,0:T(4,128)S(1)} %get-tuple-element.61), kind=kLoop, calls=%fused_computation.52 | loop fusion | flops 3170304 | bytes 25378944 | tf_op jit(solution)/shard_map/cond/branch_0_fun/mul | solution.py:38
  49.5 18.9 %fusion.38 = f32[4,1032,768]{2,1,0:T(8,128)} fusion(f32[4,1032,768]{2,1,0:T(8,128)} %broadcast_multiply_fusion.2, f32[4,1032]{1,0:T(4,128)S(1)} %add_maximum_fusion, f32[1032]{0:T(1024)S(1)} %get-tuple-element.134, f32[1032]{0:T(1024)S(1)} %fusion.55, f32[1032]{0:T(1024)S(1)} %get-tuple-element.135), kind=kLoop, calls=%fused_computation.50 | loop fusion | flops 19021824 | bytes 25391328 | tf_op jit(solution)/shard_map/cond/branch_0_fun/div | solution.py:40
  68.4 10.2 %conditional.4 = (f32[4,1032,768]{2,1,0:T(8,128)}, f32[4,1032]{1,0:T(4,128)S(1)}) conditional(s32[]{:T(128)} %clamp.2, (f32[4,1032]{1,0:T(4,128)S(1)}, f32[4,1032,768]{2,1,0:T(8,128)}) %tuple.46, (f32[4,1032]{1,0:T(4,128)S(1)}, f32[4,1032,768]{2,1,0:T(8,128)}) %tuple.46), branch_computations={%region_0.1_spmd, %region_1.2_spmd} | conditional | flops 31783536 | bytes 50836336 | solution.py:50
  68.4 10.0 %broadcast_multiply_fusion = f32[4,1032,768]{2,1,0:T(8,128)} fusion(f32[4,1032,768]{2,1,0:T(8,128)} %get-tuple-element.56, f32[4,1032]{1,0:T(4,128)S(1)} %get-tuple-element.180), kind=kLoop, calls=%fused_computation.1 | loop fusion | flops 3170304 | bytes 25378944 | tf_op jit(solution)/shard_map/cond/branch_0_fun/mul | solution.py:38
  78.9 2.4 copy.29
  81.3 6.8 broadcast_in_dim.27
  88.1 15.8 %reshape.603 = f32[4,1032,768]{2,1,0:T(8,128)} reshape(f32[4,516,2,768]{3,2,1,0:T(2,128)} %broadcast_in_dim.27) | data formatting | bytes 25362432 | tf_op jit(solution)/shard_map/reshape | solution.py:146
  103.9 13.6 %multiply_reduce_fusion.5 = (f32[4,1032]{1,0:T(4,128)S(1)}, f32[4,1032]{1,0:T(4,128)S(1)}, f32[4,1032]{1,0:T(4,128)S(1)}, f32[4,1032]{1,0:T(4,128)S(1)}) fusion(f32[4,1032,768]{2,1,0:T(8,128)} %reshape.603, f32[4,1032]{1,0:T(4,128)S(1)} %fusion.228, f32[4,1032,768]{2,1,0:T(8,128)} %get-tuple-element.87, f32[4,1032]{1,0:T(4,128)S(1)} %broadcast_maximum_fusion.1, ...), kind=kLoop, calls=%fused_computation.286 | loop fusion | flops 31686528 | bytes 38155008 | tf_op jit(solution)/shard_map/reduce_sum | solution.py:147
  117.5 49.0 %all_gather.6 = f32[4,4,1032]{2,1,0:T(4,128)S(1)} all-gather(f32[2,4,1032]{2,1,0:T(4,128)S(1)} %pad_maximum_fusion), channel_id=1, replica_groups=mesh['blk'=2,'seq'=16] {'blk'}, dimensions={0}, use_global_device_ids=true | all-gather | bytes 99072 | tf_op jit(solution)/shard_map/all_gather | solution.py:135
  166.6 8.8 %psum.42 = f32[4,1032]{1,0:T(4,128)S(1)} all-reduce(f32[4,1032]{1,0:T(4,128)S(1)} %multiply_add_fusion.7), channel_id=1, replica_groups=mesh['blk'=2,'seq'=16] {'blk'}, use_global_device_ids=true, to_apply=%region_12.13 | all-reduce | flops 4128 | bytes 33024 | tf_op jit(solution)/shard_map/psum | solution.py:148
  175.4 29.9 %multiply_add_fusion.4 = (f32[4,1032,768]{2,1,0:T(8,128)}, f32[4,1032,768]{2,1,0:T(8,128)}, f32[4,1032,768]{2,1,0:T(8,128)}, f32[4,768]{1,0:T(4,128)}) fusion(f32[4,1032,768]{2,1,0:T(8,128)} %reshape.603, f32[4,1032]{1,0:T(4,128)S(1)} %get-tuple-element.164, f32[4,1032]{1,0:T(4,128)S(1)} %fusion.228, f32[4,1032]{1,0:T(4,128)S(1)} %get-tuple-element.166, ...), kind=kLoop, calls=%fused_computation.284 | loop fusion | flops 50721792 | bytes 76227456 | tf_op jit(solution)/shard_map/add | solution.py:151
  205.3 19.3 %conditional.7 = (f32[4,1032,768]{2,1,0:T(8,128)}) conditional(s32[]{:T(128)} %clamp.2, (f32[4,1032,768]{2,1,0:T(8,128)}, f32[4,1032]{1,0:T(4,128)S(1)}) %tuple.48, (f32[4,1032,768]{2,1,0:T(8,128)}, f32[4,1032]{1,0:T(4,128)S(1)}) %tuple.48), branch_computations={%region_15.16_spmd, %region_16.17_spmd} | conditional | flops 47672208 | bytes 25515176 | solution.py:50
  205.4 19.0 %fusion.146 = f32[4,1032,768]{2,1,0:T(8,128)} fusion(f32[4,1032,768]{2,1,0:T(8,128)} %get-tuple-element.68, f32[4,1032]{1,0:T(4,128)S(1)} %get-tuple-element.69, f32[4,1032]{1,0:T(4,128)S(1)} %add_maximum_fusion.2, f32[1032]{0:T(1024)S(1)} %get-tuple-element.146, f32[1032]{0:T(1024)S(1)} %fusion.163, f32[1032]{0:T(1024)S(1)} %get-tuple-element.147), kind=kLoop, calls=%fused_computation.181 | loop fusion | flops 22192128 | bytes 25407840 | tf_op jit(solution)/shard_map/cond/branch_0_fun/mul | solution.py:46
  224.7 14.1 %multiply_add_fusion.3 = f32[4,1032,768]{2,1,0:T(8,128)} fusion(f32[4,1032,768]{2,1,0:T(8,128)} %get-tuple-element.190, f32[4,1032,768]{2,1,0:T(8,128)} %get-tuple-element.89, f32[4,1032]{1,0:T(4,128)S(1)} %get-tuple-element.91, f32[4,1032]{1,0:T(4,128)S(1)} %broadcast_maximum_fusion), kind=kLoop, calls=%fused_computation.283 | loop fusion | flops 9510912 | bytes 38076672 | tf_op jit(solution)/shard_map/add | solution.py:166
  238.9 15.4 %reshape.602 = f32[4,516,2,768]{3,2,1,0:T(2,128)} reshape(f32[4,1032,768]{2,1,0:T(8,128)} %get-tuple-element.162) | data formatting | bytes 25362432 | tf_op jit(solution)/shard_map/reshape | solution.py:141
  254.3 19.0 %reduce_sum.111 = f32[4,516,768]{2,1,0:T(8,128)} reduce(f32[4,516,2,768]{3,2,1,0:T(2,128)} %reshape.602, f32[]{:T(128)} %constant.313.clone.1), dimensions={2}, to_apply=%region_8.9 | reduce | flops 1585152 | bytes 19021828 | tf_op jit(solution)/shard_map/reduce_sum | solution.py:141
  273.3 6.0 broadcast_multiply_fusion.4
  279.3 96.2 %copy.33 = f32[4,516,768]{0,1,2:T(8,128)} copy(f32[4,516,768]{2,1,0:T(8,128)} %broadcast_multiply_fusion.4) | data formatting | bytes 12681216
  375.5 117.1 %reshape.619 = f32[768,2064]{1,0:T(8,128)} reshape(f32[768,516,4]{2,1,0:T(8,128)} %bitcast.18) | data formatting | bytes 12681216
  495.9 61.4 %psum.46 = f32[8,768]{1,0:T(8,128)S(1)} all-reduce(f32[8,768]{1,0:T(8,128)S(1)} %fusion.232), channel_id=1, replica_groups=mesh['blk'=2,'seq'=16] {'blk'}, use_global_device_ids=true, to_apply=%region_26.27 | all-reduce | flops 6144 | bytes 49152 | tf_op jit(solution)/shard_map/psum | solution.py:168
  557.3 25.3 %all-reduce.58.cloned.1.call-done = f32[4128,768]{1,0:T(8,128)} async-done(((f32[4128,768]{1,0:T(8,128)}), f32[4128,768]{1,0:T(8,128)}) %all-reduce.58.cloned.1.call-update) | async-done | bytes 12681232 | tf_op jit(solution)/shard_map/psum | solution.py:168
  582.6 8.0 fusion.237
  590.7 37.9 %multiply_reduce_fusion = (f32[768]{0:T(1024)S(1)}, f32[768]{0:T(1024)S(1)}, f32[768]{0:T(1024)S(1)}, bf16[4,1032,768]{2,1,0:T(8,128)(2,1)}) fusion(f32[4,1032,768]{2,1,0:T(8,128)} %bitcast.42, f32[4,1032,768]{2,1,0:T(8,128)} %copy-done, f32[4,1032]{1,0:T(4,128)S(1)} %get-tuple-element.91, f32[768]{0:T(1024)S(1)} %copy-done.14, f32[768]{0:T(1024)S(1)} %copy-done.8, ...), kind=kLoop, calls=%fused_computation.278 | loop fusion | flops 47552256 | bytes 31741056 | tf_op jit(solution)/shard_map/reduce_sum | solution.py:72
  628.6 61.2 %all-reduce.54 = (f32[5,384]{1,0:T(8,128)S(1)}, f32[8,384]{1,0:T(8,128)S(1)}) all-reduce(f32[5,384]{1,0:T(8,128)S(1)} %constant_dynamic-slice_fusion.1, f32[8,384]{1,0:T(8,128)S(1)} %constant_dynamic-slice_fusion), channel_id=1, replica_groups=mesh['blk'=2,'seq'=16] {'seq'}, use_global_device_ids=true, to_apply=%region_24.25 | all-reduce | flops 4992 | bytes 39936 | tf_op jit(solution)/shard_map/psum | solution.py:176
  691.7 4.9 fusion.224
  697.4 44.7 %reshape.620 = bf16[384,516,4]{2,1,0:T(8,128)(2,1)} reshape(f32[384,2064]{1,0:T(8,128)} %reduce-scatter.4.cloned.1.call-done) | data formatting | bytes 4755456
  742.1 45.3 %copy.34 = bf16[4,516,384]{2,0,1:T(4,128)(2,1)} copy(bf16[4,516,384]{0,1,2:T(8,128)(2,1)} %bitcast.39) | data formatting | bytes 3170304
  788.1 1.4 multiply_bitcast_fusion
  (113 shorter events, 13.4 us)
Async XLA Ops:
  7.2 71.8 %all-gather.2.cloned.1.call-start = ((), (), s32[]{:S(2)}) async-start(), calls=%async_computation.1 | async-start | bytes 4755456 | tf_op jit(solution)/shard_map/all_gather | solution.py:145
  7.9 574.7 %all-reduce.58.cloned.1.call-start = ((), (), s32[]{:S(2)}) async-start(), calls=%async_computation.2 | async-start | bytes 25362432 | tf_op jit(solution)/shard_map/psum | solution.py:168
  9.8 20.9 %copy-start.7 = (f32[768]{0:T(1024)}, f32[768]{0:T(1024)S(1)}, u32[]{:S(2)}) copy-start(f32[768]{0:T(1024)S(1)} %get-tuple-element.122) | copy-start | bytes 9220
  9.8 20.9 %copy-start.9 = (f32[768]{0:T(1024)}, f32[768]{0:T(1024)S(1)}, u32[]{:S(2)}) copy-start(f32[768]{0:T(1024)S(1)} %get-tuple-element.123) | copy-start | bytes 9220
  9.8 20.9 %copy-start.11 = (f32[768]{0:T(1024)}, f32[768]{0:T(1024)S(1)}, u32[]{:S(2)}) copy-start(f32[768]{0:T(1024)S(1)} %get-tuple-element.124) | copy-start | bytes 9220
  9.8 20.9 %copy-start.13 = (f32[768]{0:T(1024)}, f32[768]{0:T(1024)S(1)}, u32[]{:S(2)}) copy-start(f32[768]{0:T(1024)S(1)} %get-tuple-element.125) | copy-start | bytes 9220
  10.6 14.8 %copy-start.5 = (pred[4,1032]{1,0:T(4,128)(4,1)}, pred[4,1032]{1,0:T(4,128)(4,1)S(1)}, u32[]{:S(2)}) copy-start(pred[4,1032]{1,0:T(4,128)(4,1)S(1)} %get-tuple-element.178) | copy-start | bytes 12388
  30.6 8.8 %copy-start = (f32[4,1032,768]{2,1,0:T(8,128)}, f32[4,1032,768]{2,1,0:T(8,128)S(1)}, u32[]{:S(2)}) copy-start(f32[4,1032,768]{2,1,0:T(8,128)S(1)} %convert_multiply_fusion) | copy-start | bytes 38043652
  68.4 10.2 %copy-start.21 = (f32[8,768]{1,0:T(8,128)S(1)}, f32[8,768]{1,0:T(8,128)}, u32[]{:S(2)}) copy-start(f32[8,768]{1,0:T(8,128)} %param.28) | copy-start | bytes 73732
  68.4 10.2 %copy-start.25 = (s32[4]{0:T(128)S(1)}, s32[4]{0:T(128)}, u32[]{:S(2)}) copy-start(s32[4]{0:T(128)} %param.24) | copy-start | bytes 52
  68.4 10.4 %copy-start.24 = (s32[4]{0:T(128)S(1)}, s32[4]{0:T(128)}, u32[]{:S(2)}) copy-start(s32[4]{0:T(128)} %param.23) | copy-start | bytes 52
  238.8 458.5 %reduce-scatter.4.cloned.1.call-start = ((), (), s32[]{:S(2)}) async-start(), calls=%async_computation.4 | async-start | bytes 10027008
  375.5 117.2 %copy-start.4 = (s32[4,1032]{1,0:T(4,128)S(1)}, s32[4,1032]{1,0:T(4,128)}, u32[]{:S(2)}) copy-start(s32[4,1032]{1,0:T(4,128)} %param.22) | copy-start | bytes 49540
  375.5 117.3 %copy-start.6 = (pred[4,1032]{1,0:T(4,128)(4,1)S(1)}, pred[4,1032]{1,0:T(4,128)(4,1)}, u32[]{:S(2)}) copy-start(pred[4,1032]{1,0:T(4,128)(4,1)} %copy-done.5) | copy-start | bytes 12388
  375.5 117.5 %copy-start.23 = (s32[3]{0:T(128)S(1)}, s32[3]{0:T(128)}, u32[]{:S(2)}) copy-start(s32[3]{0:T(128)} %param.25) | copy-start | bytes 40
  375.5 120.1 %copy-start.20 = (f32[4,768]{1,0:T(4,128)S(1)}, f32[4,768]{1,0:T(4,128)}, u32[]{:S(2)}) copy-start(f32[4,768]{1,0:T(4,128)} %get-tuple-element.163) | copy-start | bytes 36868
  375.5 120.1 %copy-start.26 = (s32[4]{0:T(128)S(1)}, s32[4]{0:T(128)}, u32[]{:S(2)}) copy-start(s32[4]{0:T(128)} %param.24) | copy-start | bytes 52
  492.7 97.9 %copy-start.8 = (f32[768]{0:T(1024)S(1)}, f32[768]{0:T(1024)}, u32[]{:S(2)}) copy-start(f32[768]{0:T(1024)} %copy-done.7) | copy-start | bytes 9220
  492.7 97.9 %copy-start.10 = (f32[768]{0:T(1024)S(1)}, f32[768]{0:T(1024)}, u32[]{:S(2)}) copy-start(f32[768]{0:T(1024)} %copy-done.9) | copy-start | bytes 9220
  492.7 97.9 %copy-start.12 = (f32[768]{0:T(1024)S(1)}, f32[768]{0:T(1024)}, u32[]{:S(2)}) copy-start(f32[768]{0:T(1024)} %copy-done.11) | copy-start | bytes 9220
  492.7 98.0 %copy-start.14 = (f32[768]{0:T(1024)S(1)}, f32[768]{0:T(1024)}, u32[]{:S(2)}) copy-start(f32[768]{0:T(1024)} %copy-done.13) | copy-start | bytes 9220
  492.7 295.3 %all-reduce.60.cloned.1.call-start = ((), (), s32[]{:S(2)}) async-start(), calls=%async_computation.3 | async-start | bytes 811008 | tf_op jit(solution)/shard_map/psum | solution.py:176
  590.6 99.2 %copy-start.15 = (f32[5,768]{1,0:T(8,128)S(1)}, f32[5,768]{1,0:T(8,128)}, u32[]{:S(2)}) copy-start(f32[5,768]{1,0:T(8,128)} %param.27) | copy-start | bytes 46084
  590.6 99.2 %copy-start.16 = (f32[5,384]{1,0:T(8,128)S(1)}, f32[5,384]{1,0:T(8,128)}, u32[]{:S(2)}) copy-start(f32[5,384]{1,0:T(8,128)} %param.32) | copy-start | bytes 23044
  590.6 99.2 %copy-start.17 = (f32[5,384]{1,0:T(8,128)S(1)}, f32[5,384]{1,0:T(8,128)}, u32[]{:S(2)}) copy-start(f32[5,384]{1,0:T(8,128)} %param.33) | copy-start | bytes 23044
  742.1 45.3 %copy-start.18 = (f32[8,384]{1,0:T(8,128)S(1)}, f32[8,384]{1,0:T(8,128)}, u32[]{:S(2)}) copy-start(f32[8,384]{1,0:T(8,128)} %param.34) | copy-start | bytes 36868
  742.1 45.3 %copy-start.19 = (f32[8,384]{1,0:T(8,128)S(1)}, f32[8,384]{1,0:T(8,128)}, u32[]{:S(2)}) copy-start(f32[8,384]{1,0:T(8,128)} %param.35) | copy-start | bytes 36868
  742.1 45.3 %copy-start.22 = (f32[8,768]{1,0:T(8,128)S(1)}, f32[8,768]{1,0:T(8,128)}, u32[]{:S(2)}) copy-start(f32[8,768]{1,0:T(8,128)} %param.28) | copy-start | bytes 73732
  742.1 46.0 %copy-start.1 = (f32[259,768]{1,0:T(8,128)S(1)}, f32[259,768]{1,0:T(8,128)}, u32[]{:S(2)}) copy-start(f32[259,768]{1,0:T(8,128)} %param.26) | copy-start | bytes 2386948
  742.1 46.0 %copy-start.2 = (f32[259,384]{1,0:T(8,128)S(1)}, f32[259,384]{1,0:T(8,128)}, u32[]{:S(2)}) copy-start(f32[259,384]{1,0:T(8,128)} %param.30) | copy-start | bytes 1193476
  742.1 45.9 %copy-start.3 = (f32[259,384]{1,0:T(8,128)S(1)}, f32[259,384]{1,0:T(8,128)}, u32[]{:S(2)}) copy-start(f32[259,384]{1,0:T(8,128)} %param.31) | copy-start | bytes 1193476
Sparse Core Ops, SparseCore 0:
  9.5 47.8 all-gather.1
  238.9 343.6 all-reduce.57
  585.0 82.0 reduce-scatter.3
  697.5 86.0 all-reduce.59
where the time goes:
time: 815 us; the launch traced here: 800 us
  local copies, waits for them, and re-layouts  365 us (45%)
  other arithmetic  205 us (25%)
  blocking collectives  180 us (22%)
  waiting for transfers between devices  26.1 us (3%)
  between operations  16.6 us (2%)
    unnamed x61, local copies, waits for them, and re-layouts  307 us
    psum x1, blocking collectives, local(): whole_grad, score_whole = lax.psum((flat_grad, score_part), 'blk')  61.4 us
    psum x1, blocking collectives, local(): lax.psum((table_local, tap_local, score_local), 'seq')  61.2 us
    all_gather x1, blocking collectives, local(): all_scores = lax.all_gather(my_scores, 'blk', axis=0, tiled=True)  49 us
    reduce_sum x1, other arithmetic, conv_backward(): tap_grads.append(jnp.sum(grad_conv * behind, axis=(0, 1)))  37.9 us
    add x1, other arithmetic, local(): mine[size_slot][..., None] * grad_mixed  29.9 us
    psum x1, waiting for transfers between devices, local(): whole_grad, score_whole = lax.psum((flat_grad, score_part), 'blk')  25.3 us
    mul x2, other arithmetic, pool_size(): totals = block_total(field * live_mask[..., None], size_val)  20 us
  transfers between devices with their start and end apart: 4, of which 1 were waited for; matrix products, arithmetic and copies ran while one was open for 59% of the time, Pallas kernels for 0%

commit v1 on v0

v1 whole, which is shorter than its diff:
```python
import functools

import jax
import jax.numpy as jnp
from jax import lax
from jax.experimental import pallas as pl
from jax.experimental.pallas import tpu as pltpu
from jax.sharding import PartitionSpec as P

STEP_NUMBER = 5
F32, BF16 = jnp.float32, jnp.bfloat16
TJ = 96
NO_ID = 511.0
VP = 272
NN = (((1,), (0,)), ((), ()))
NT = (((1,), (1,)), ((), ()))
TN = (((0,), (0,)), ((), ()))


def dot(a, b, dims=NN):
    return lax.dot_general(a, b, dims, preferred_element_type=F32)


def iota(shape, dim):
    return lax.broadcasted_iota(jnp.int32, shape, dim)


def split2(x):
    high = x.astype(BF16)
    return high, (x - high.astype(F32)).astype(BF16)


def split3(x):
    high = x.astype(BF16)
    rest = x - high.astype(F32)
    mid = rest.astype(BF16)
    return high, mid, (rest - mid.astype(F32)).astype(BF16)


def block_masks():
    ju, jt = iota((TJ, TJ), 0), iota((TJ, TJ), 1)
    one = lambda cond: jnp.where(cond, 1.0, 0.0).astype(F32)
    third = lambda j, par: (2 * j + par) // 3
    return [
        one(ju == jt),
        one(ju // 2 == jt // 2),
        one(third(ju, 0) == third(jt, 0)),
        one(third(ju, 0) == third(jt, 1)),
        one(third(ju, 1) == third(jt, 0)),
        one(third(ju, 1) == third(jt, 1)),
    ]


def pick_row(x, index):
    return jnp.sum(jnp.where(iota(x.shape, 0) == index, x, 0.0), axis=0, keepdims=True)


def store_masks(mask_ref, wide):
    for k, mask in enumerate(block_masks()):
        if wide:
            mask_ref[k] = jnp.zeros(mask_ref.shape[1:], F32)
        mask_ref[k, :, :TJ] = mask


def load_table(table_ref, tail_ref, tab_ref):
    vocab = table_ref.shape[0]
    whole = vocab // 128 * 128
    tab_ref[:whole, :] = table_ref[:whole, :].astype(BF16)
    tail_ref[...] = jnp.zeros(tail_ref.shape, F32)
    tail_ref[: vocab - whole, :] = table_ref[whole:, :]
    tab_ref[whole:, :] = tail_ref[...].astype(BF16)


def load_cot_rows(cot_ref, first, rows):
    have = cot_ref.shape[1]
    if first + rows <= have:
        return cot_ref[0, first : first + rows, :]
    whole = (have - first) // 16 * 16
    parts = [cot_ref[0, first : first + whole, :]]
    left = have - first - whole
    if left:
        last = cot_ref[0, first + whole :, :].astype(F32)
        pad = jnp.zeros((16 - left, last.shape[1]), F32)
        parts.append(jnp.concatenate([last, pad], axis=0).astype(BF16))
        whole += 16
    if rows > whole:
        parts.append(jnp.zeros((rows - whole, cot_ref.shape[2]), BF16))
    return jnp.concatenate(parts, axis=0)


def forward_kernel(
    half_ref, len_ref, ids_ref, cot_ref, table_ref, conv_ref,
    emb_out, conv_out, inner_out, rows_out,
    xs, cs, idc, tail, tab, emb, masks,
):
    s = pl.program_id(0)
    seqs, slot = ids_ref.shape
    chans = cot_ref.shape[2]
    tiles = emb_out.shape[2] // TJ
    pairs = tiles * TJ

    @pl.when(s == 0)
    def _():
        xs[...] = jnp.full(xs.shape, NO_ID, F32)
        xs[:seqs, :slot] = ids_ref[...].astype(F32)
        for i in range(xs.shape[1] // 128):
            cs[128 * i : 128 * (i + 1), :] = xs[:, 128 * i : 128 * (i + 1)].T
        rows_out[...] = jnp.full(rows_out.shape, NO_ID, F32)
        for par in range(2):
            cols = cs[pl.ds(par, pairs, stride=2), :]
            for k in range(seqs):
                idc[k, par] = jnp.broadcast_to(cols[:, k : k + 1], (pairs, 128))
            for i in range(tiles):
                flipped = cols[TJ * i : TJ * (i + 1), :].T
                for k in range(seqs):
                    rows_out[k, par : par + 1, 128 * i : 128 * i + TJ] = flipped[k : k + 1, :]
        load_table(table_ref, tail, tab)
        emb[:, :8, :] = jnp.zeros((2, 8, chans), F32)
        store_masks(masks, False)

    inner_out[...] = jnp.zeros(inner_out.shape, F32)
    lane = iota((2 * TJ, 128), 1).astype(F32)
    length = len_ref[s]
    taps = [conv_ref[k : k + 1, :] for k in range(5)]
    for i in range(tiles):
        r = TJ * i
        ids = jnp.concatenate([idc[s, 0, r : r + TJ, :], idc[s, 1, r : r + TJ, :]], axis=0)
        hot = jnp.concatenate(
            [jnp.where(ids == lane + 128.0 * k, 1.0, 0.0).astype(BF16) for k in range(3)], axis=1
        )
        rows = dot(hot, tab[...])
        for par in range(2):
            emb[par, 8 + r : 8 + r + TJ, :] = rows[par * TJ : (par + 1) * TJ]
            emb_out[0, par, r : r + TJ, :] = rows[par * TJ : (par + 1) * TJ].astype(BF16)
        even, odd = rows[:TJ], rows[TJ:]
        even1 = emb[0, 7 + r : 7 + r + TJ, :]
        odd1 = emb[1, 7 + r : 7 + r + TJ, :]
        odd2 = emb[1, 6 + r : 6 + r + TJ, :]
        conv_even = taps[4] + taps[0] * even + taps[1] * odd1 + taps[2] * even1 + taps[3] * odd2
        conv_odd = taps[4] + taps[0] * odd + taps[1] * even + taps[2] * odd1 + taps[3] * even1
        high, low = split2(jnp.concatenate([conv_even, conv_odd], axis=0))
        conv_out[0, i] = high
        cot = load_cot_rows(cot_ref, r, TJ)
        prod = dot(high, cot, NT) + dot(low, cot, NT)
        place = 2 * (r + iota((TJ, TJ), 0))
        pe = jnp.where(place < length, prod[:TJ], 0.0)
        po = jnp.where(place + 1 < length, prod[TJ:], 0.0)
        total = lambda x: jnp.sum(x, axis=0, keepdims=True)
        sums = [
            total(masks[0] * pe),
            total(masks[0] * po),
            total(masks[1] * (pe + po)),
            total(masks[2] * pe + masks[4] * po),
            total(masks[3] * pe + masks[5] * po),
        ]
        for k, row in enumerate(sums):
            inner_out[0, k : k + 1, 128 * i : 128 * i + TJ] = row


def lane_facts(width):
    lane = iota((8, width), 1)
    within = lane % 128
    pair = TJ * (lane // 128) + within
    return within, pair


def shift_right(x, n):
    width = x.shape[1]
    within, pair = lane_facts(width)
    inside = pltpu.roll(x, n, 1)
    across = pltpu.roll(x, n + 128 - TJ, 1)
    return jnp.where(pair < n, 0.0, jnp.where(within < n, across, inside))


def shift_left(x, n):
    width = x.shape[1]
    within, pair = lane_facts(width)
    inside = pltpu.roll(x, width - n, 1)
    across = pltpu.roll(x, width - n - (128 - TJ), 1)
    last = TJ * (width // 128)
    return jnp.where(pair >= last - n, 0.0, jnp.where(within >= TJ - n, across, inside))


def block_sums(even, odd):
    width = even.shape[1]
    _, pair = lane_facts(width)
    after = lambda x: pltpu.roll(x, width - 1, 1)
    before = lambda x: pltpu.roll(x, 1, 1)
    two = even + odd
    four = two + jnp.where(pair % 2 == 0, after(two), before(two))
    third = pair % 3
    en, on, ep, op = after(even), after(odd), before(even), before(odd)
    first, last = two + en, op + two
    three_even = jnp.where(third == 0, first, jnp.where(third == 1, ep + op + even, last))
    three_odd = jnp.where(third == 0, first, jnp.where(third == 1, odd + en + on, last))
    return [even, two, three_even, four], [odd, two, three_odd, four]


def live_rows(len_ref, seqs, width):
    within, pair = lane_facts(width)
    sub = iota((8, width), 0)
    length = jnp.zeros((8, width), jnp.int32)
    for s in range(seqs):
        length = jnp.where(sub == s, len_ref[s], length)
    length = jnp.where(within < TJ, length, 0)
    return [jnp.where(2 * pair + par < length, 1.0, 0.0).astype(F32) for par in range(2)]


def inverse_counts(live):
    return [[1.0 / jnp.maximum(c, 1.0) for c in side] for side in block_sums(*live)]


def band(mask_ref, rows, seq, tile_start, length):
    r = [rows[k : k + 1, :] for k in range(5)]
    four = mask_ref[1] * r[4]
    even = mask_ref[0] * r[0] + mask_ref[2] * r[2] + mask_ref[3] * r[3] + four
    odd = mask_ref[0] * r[1] + mask_ref[4] * r[2] + mask_ref[5] * r[3] + four
    place = 2 * (tile_start + iota((TJ, 128), 0))
    even = jnp.where(place < length, even, 0.0)
    odd = jnp.where(place + 1 < length, odd, 0.0)
    return jnp.concatenate([even, odd], axis=0)


def pooled_kernel(
    len_ref, lang_ref, rows_ref, table_ref, convw_ref, score_ref, conv_ref,
    out_ref, prob_out, band_out,
    tail, tab, lookups, bias, masks,
):
    s = pl.program_id(0)
    seqs = len_ref.shape[0]
    width = rows_ref.shape[2]
    tiles = width // 128

    @pl.when(s == 0)
    def _():
        load_table(table_ref, tail, tab)
        store_masks(masks, True)
        scores = score_ref[...]
        mixed = jnp.concatenate([convw_ref[k : k + 1, :] * scores for k in range(4)], axis=0)
        small = dot(jnp.concatenate(split3(mixed), axis=0), tab[...], NT)
        small = small[:32] + small[32:64] + small[64:96]
        small = jnp.concatenate(split3(small), axis=0)
        constant = jnp.sum(convw_ref[4:5, :] * scores, axis=1, keepdims=True)
        constant = jnp.broadcast_to(constant, (8, width))
        for k in range(seqs):
            bias[k : k + 1, :] = pick_row(constant, lang_ref[k])
        bias[seqs:, :] = jnp.zeros((8 - seqs, width), F32)
        lookups[...] = jnp.zeros(lookups.shape, F32)
        for par in range(2):
            for k in range(seqs):
                sub = iota((VP, width), 0).astype(F32)
                hot = jnp.where(rows_ref[k, par : par + 1, :] == sub, 1.0, 0.0).astype(BF16)
                hot = jnp.concatenate([hot, jnp.zeros((384 - VP, width), BF16)], axis=0)
                got = dot(small, hot)
                got = got[:32] + got[32:64] + got[64:96]
                for tap in range(4):
                    lookups[par, tap, k : k + 1, :] = pick_row(got[8 * tap : 8 * tap + 8], lang_ref[k])
        look = lambda par, tap: lookups[par, tap]
        shift = shift_right
        even = bias[...] + look(0, 0) + shift(look(1, 1), 1) + shift(look(0, 2), 1) + shift(look(1, 3), 2)
        odd = bias[...] + look(1, 0) + look(0, 1) + shift(look(1, 2), 1) + shift(look(0, 3), 1)
        live = live_rows(len_ref, seqs, width)
        inverse = inverse_counts(live)
        totals = block_sums(jnp.where(live[0] > 0, even, 0.0), jnp.where(live[1] > 0, odd, 0.0))
        weights = []
        for par in range(2):
            score = [t * c for t, c in zip(totals[par], inverse[par])]
            top = functools.reduce(jnp.maximum, score)
            grown = [jnp.exp(x - top) for x in score]
            scale = 1.0 / functools.reduce(jnp.add, grown)
            prob = [x * scale for x in grown]
            for size in range(4):
                prob_out[par, size] = prob[size]
            weights.append([0.5 * live[par] * p * c for p, c in zip(prob, inverse[par])])
        (e1, e2, e3, e4), (o1, o2, o3, o4) = weights
        for k, row in enumerate([e1 + e2 + o2, o1 + e2 + o2, e3, o3, e4 + o4]):
            for q in range(seqs):
                band_out[q, k : k + 1, :] = row[q : q + 1, :]

    length = len_ref[s]
    have = out_ref.shape[1]
    for i in range(tiles):
        weights = band(masks, band_out[s, :, 128 * i : 128 * (i + 1)], s, TJ * i, length)
        got = dot(weights.astype(BF16), conv_ref[0, i], TN)
        rows = min(TJ, have - TJ * i)
        out_ref[0, TJ * i : TJ * i + rows, :] = got[:rows].astype(BF16)


def backward_kernel(
    half_ref, len_ref, lang_ref, core_ref, rows_ref, cot_ref, table_ref, convw_ref, score_ref,
    emb_ref, prob_ref, band_ref, inner_ref, other_ref,
    keep_out, send_out,
    tail, tab, masks, pulls, shifted, sums, emb, grad, gemb, hots, hist, acc, taps_acc, flat,
):
    s = pl.program_id(0)
    seqs = len_ref.shape[0]
    width = rows_ref.shape[2]
    tiles = width // 128
    pairs = tiles * TJ
    chans = cot_ref.shape[2]

    @pl.when(s == 0)
    def _():
        load_table(table_ref, tail, tab)
        store_masks(masks, True)
        pulls[...] = jnp.zeros(pulls.shape, F32)
        for q in range(seqs):
            both = inner_ref[q] + other_ref[q]
            for k in range(5):
                pulls[k, q : q + 1, :] = both[k : k + 1, :]
        live = live_rows(len_ref, seqs, width)
        inverse = inverse_counts(live)
        one_e, one_o, four, three_e, three_o = [pulls[k] for k in range(5)]
        two = one_e + one_o
        dots = [[one_e, two, three_e, four], [one_o, two, three_o, four]]
        parts = [[], []]
        for par in range(2):
            inner = [
                0.5 * jnp.where(live[par] > 0, d, 0.0) * c for d, c in zip(dots[par], inverse[par])
            ]
            prob = [prob_ref[par, size] for size in range(4)]
            mean = functools.reduce(jnp.add, [p * x for p, x in zip(prob, inner)])
            parts[par] = [p * (x - mean) * c for p, x, c in zip(prob, inner, inverse[par])]
        pull = [0.0, 0.0]
        for size in range(4):
            totals = block_sums(parts[0][size], parts[1][size])
            pull = [pull[par] + totals[par][size] for par in range(2)]
        pe, po = [live[par] * pull[par] for par in range(2)]
        sums[...] = jnp.broadcast_to(jnp.sum(pe + po, axis=1, keepdims=True), sums.shape)
        ahead = [
            [pe, po, shift_left(pe, 1), shift_left(po, 1)],
            [po, shift_left(pe, 1), shift_left(po, 1), shift_left(pe, 2)],
        ]
        for par in range(2):
            for k in range(4):
                high = ahead[par][k].astype(BF16).astype(F32)
                low = ahead[par][k] - high
                for q in range(seqs):
                    shifted[q, par, k : k + 1, :] = high[q : q + 1, :]
                    shifted[q, par, 4 + k : 5 + k, :] = low[q : q + 1, :]
        emb[:, :8, :] = jnp.zeros((2, 8, chans), F32)
        grad[:, pairs:, :] = jnp.zeros((2, 8, chans), F32)
        acc[...] = jnp.zeros(acc.shape, F32)
        taps_acc[...] = jnp.zeros(taps_acc.shape, F32)

    length = len_ref[s]
    lang = lang_ref[s]
    score = pick_row(score_ref[...], lang)
    high = score.astype(BF16).astype(F32)
    sub = iota((128 - TJ, chans), 0)
    gap = jnp.where(sub == 0, high, jnp.where(sub == 1, score - high, 0.0)).astype(BF16)
    lane = iota((TJ, 128), 1)
    extra = (lane == TJ) | (lane == TJ + 1)
    blank = jnp.zeros((120, 128), F32)
    for i in range(tiles):
        r = TJ * i
        cot = jnp.concatenate([load_cot_rows(cot_ref, r, TJ), gap], axis=0)
        lanes = slice(128 * i, 128 * (i + 1))
        weights = band(masks, band_ref[s, :, lanes], s, r, length)
        columns = []
        for par in range(2):
            both = jnp.concatenate([shifted[s, par, :, lanes], blank], axis=0).T
            gemb[256 * i + 128 * par : 256 * i + 128 * (par + 1), chans:] = both.astype(BF16)
            columns.append(jnp.where(extra, both[:TJ, 0:1] + both[:TJ, 4:5], weights[par * TJ : (par + 1) * TJ]))
        wide = jnp.concatenate(split2(jnp.concatenate(columns, axis=0)), axis=1)
        got = dot(wide, jnp.concatenate([cot, cot], axis=0))
        for par in range(2):
            grad[par, r : r + TJ, :] = got[par * TJ : (par + 1) * TJ]
            emb[par, 8 + r : 8 + r + TJ, :] = emb_ref[0, par, r : r + TJ, :].astype(F32)
            sub = iota((VP, 128), 0).astype(F32)
            hots[:, 256 * i + 128 * par : 256 * i + 128 * (par + 1)] = jnp.where(
                rows_ref[s, par : par + 1, lanes] == sub, 1.0, 0.0
            ).astype(BF16)
    taps = [convw_ref[k : k + 1, :] for k in range(4)]
    fold = lambda x: jnp.sum(x.reshape(TJ // 8, 8, chans), axis=0)
    for i in range(tiles):
        r = TJ * i
        ge, go = grad[0, r : r + TJ, :], grad[1, r : r + TJ, :]
        ge1, go1 = grad[0, r + 1 : r + 1 + TJ, :], grad[1, r + 1 : r + 1 + TJ, :]
        ge2 = grad[0, r + 2 : r + 2 + TJ, :]
        ee, eo = emb[0, 8 + r : 8 + r + TJ, :], emb[1, 8 + r : 8 + r + TJ, :]
        ee1, eo1 = emb[0, 7 + r : 7 + r + TJ, :], emb[1, 7 + r : 7 + r + TJ, :]
        eo2 = emb[1, 6 + r : 6 + r + TJ, :]
        back_e = taps[0] * ge + taps[1] * go + taps[2] * ge1 + taps[3] * go1
        back_o = taps[0] * go + taps[1] * ge1 + taps[2] * go1 + taps[3] * ge2
        zeros = jnp.zeros((128 - TJ, chans), BF16)
        gemb[256 * i : 256 * (i + 1), :chans] = jnp.concatenate(
            [back_e.astype(BF16), zeros, back_o.astype(BF16), zeros], axis=0
        )
        for k, part in enumerate(
            [ge * ee + go * eo, ge * eo1 + go * ee, ge * ee1 + go * eo1, ge * eo2 + go * ee1, ge + go]
        ):
            taps_acc[k] += fold(part)
    got = dot(hots[...], gemb[...])
    acc[...] += got[:, :chans]
    hist[...] = jnp.zeros(hist.shape, F32)
    hist[:VP, :] = got[:, chans:]
    counts = hist[...].T[:8]
    counts = jnp.concatenate(split3(jnp.concatenate([counts[:4] + counts[4:], jnp.zeros((12, 384), F32)], axis=0)), axis=0)
    from_table = dot(counts, tab[...])
    from_table = from_table[:16] + from_table[16:32] + from_table[32:]
    part = convw_ref[4:5, :] * pick_row(sums[:, :chans], s)
    for k in range(4):
        part = part + taps[k] * from_table[k : k + 1, :]
    groups = score_ref.shape[0]
    acc[VP - groups : VP, :] += jnp.where(iota((groups, chans), 0) == lang, part, 0.0)

    @pl.when(s == seqs - 1)
    def _():
        for k in range(5):
            row = VP - groups - 5 + k
            acc[row : row + 1, :] = jnp.sum(taps_acc[k], axis=0, keepdims=True)
        flat[...] = jnp.zeros(flat.shape, F32)
        for k in range(chans // 128):
            flat[VP * k : VP * (k + 1), :] = acc[:, 128 * k : 128 * (k + 1)]
        rows = keep_out.shape[0]
        mine = pl.multiple_of(core_ref[0] * rows, 8)
        theirs = pl.multiple_of((1 - core_ref[0]) * rows, 8)
        keep_out[...] = flat[pl.ds(mine, rows), :]
        send_out[...] = flat[pl.ds(theirs, rows), :]


def adamw(weight, grad, moment, second, rate):
    new_m = 0.9 * moment + 0.1 * grad
    new_v = 0.999 * second + 0.001 * grad * grad
    m_hat = new_m / (1.0 - 0.9**STEP_NUMBER)
    v_hat = new_v / (1.0 - 0.999**STEP_NUMBER)
    new_w = weight - rate * (m_hat / (jnp.sqrt(v_hat) + 1e-08) + 0.01 * weight)
    return new_m, new_v, new_w


def update_kernel(half_ref, place_ref, owner_ref, mine_ref, other_ref, *refs):
    ins, outs, flat = refs[:9], refs[9:18], refs[18]
    core, near, seq = place_ref[0], place_ref[1], place_ref[2]
    rows = mine_ref.shape[0] // 2
    for side, ref in ((core, mine_ref), (1 - core, other_ref)):
        for k in range(2):
            piece = near if k == 0 else 1 - near
            flat[pl.ds(pl.multiple_of((2 * side + piece) * rows, 8), rows), :] = ref[k * rows : (k + 1) * rows, :]
    vocab = ins[0].shape[0]
    chans = ins[0].shape[1]
    groups = ins[6].shape[0]
    spans = ((0, vocab), (VP - groups - 5, 5), (VP - groups, groups))
    for t, rate in enumerate((0.5, 0.3, 0.05)):
        first, count = spans[t]
        owned = owner_ref[t] == seq
        for k in range(chans // 128):
            lanes = slice(128 * k, 128 * (k + 1))
            grad = flat[VP * k + first : VP * k + first + count, :]
            new = adamw(ins[3 * t][:, lanes], grad, ins[3 * t + 1][:, lanes], ins[3 * t + 2][:, lanes], rate)
            for q in range(3):
                outs[3 * t + q][0, :, lanes] = jnp.where(owned, new[q], 0.0)


def local(
    seq_size, byte_ids, lengths, lang_ids, owners, table, conv_w, score_w, cotangent,
    table_m, table_v, conv_m, conv_v, score_m, score_v,
):
    seqs, slot = byte_ids.shape
    vocab, full = table.shape
    half_rows, chans = cotangent.shape[1:]
    groups = score_w.shape[0]
    tiles = -(-half_rows // TJ)
    pairs, width = tiles * TJ, tiles * 128
    half = lax.axis_index("blk").astype(jnp.int32).reshape(1)
    seq = lax.axis_index("seq").astype(jnp.int32)
    core, near = seq % 2, (seq // 4) % 2
    vmem = pltpu.VMEM
    params = lambda mib: pltpu.CompilerParams(vmem_limit_bytes=mib * 1024 * 1024, dimension_semantics=("arbitrary",))
    shape = jax.ShapeDtypeStruct
    whole = lambda *dims: pl.BlockSpec(dims, lambda s, *_: (0,) * len(dims))
    by_seq = lambda *dims: pl.BlockSpec((1,) + dims, lambda s, *_: (s,) + (0,) * len(dims))
    by_half = lambda rows: pl.BlockSpec((rows, chans), lambda s, half, *_: (0, half[0]))

    emb, conv, inner, rows = pl.pallas_call(
        forward_kernel,
        grid_spec=pltpu.PrefetchScalarGridSpec(
            num_scalar_prefetch=2,
            grid=(seqs,),
            in_specs=[whole(seqs, slot), by_seq(half_rows, chans), by_half(vocab), by_half(5)],
            out_specs=[
                by_seq(2, pairs, chans), by_seq(tiles, 2 * TJ, chans), by_seq(8, width), whole(seqs, 8, width)
            ],
            scratch_shapes=[
                vmem((8, 2 * pairs), F32), vmem((2 * pairs, 8), F32), vmem((seqs, 2, pairs, 128), F32),
                vmem((128, chans), F32), vmem((384, chans), BF16), vmem((2, 8 + pairs, chans), F32),
                vmem((6, TJ, TJ), F32),
            ],
        ),
        out_shape=[
            shape((seqs, 2, pairs, chans), BF16), shape((seqs, tiles, 2 * TJ, chans), BF16),
            shape((seqs, 8, width), F32), shape((seqs, 8, width), F32),
        ],
        compiler_params=params(32),
        name="forward",
    )(half, lengths, byte_ids, cotangent, table, conv_w)

    other = lax.ppermute(inner, "blk", [(0, 1), (1, 0)])

    pooled, prob, weights = pl.pallas_call(
        pooled_kernel,
        grid_spec=pltpu.PrefetchScalarGridSpec(
            num_scalar_prefetch=2,
            grid=(seqs,),
            in_specs=[
                whole(seqs, 8, width), whole(vocab, full), whole(5, full), whole(groups, full),
                by_seq(tiles, 2 * TJ, chans),
            ],
            out_specs=[by_seq(half_rows, chans), whole(2, 4, 8, width), whole(seqs, 8, width)],
            scratch_shapes=[
                vmem((128, full), F32), vmem((384, full), BF16),
                vmem((2, 4, 8, width), F32), vmem((8, width), F32), vmem((6, TJ, 128), F32),
            ],
        ),
        out_shape=[
            shape((seqs, half_rows, chans), BF16), shape((2, 4, 8, width), F32), shape((seqs, 8, width), F32)
        ],
        compiler_params=params(32),
        name="pooled",
    )(lengths, lang_ids, rows, table, conv_w, score_w, conv)

    total = -(-VP * (chans // 128) // 32) * 32
    keep, send = pl.pallas_call(
        backward_kernel,
        grid_spec=pltpu.PrefetchScalarGridSpec(
            num_scalar_prefetch=4,
            grid=(seqs,),
            in_specs=[
                whole(seqs, 8, width), by_seq(half_rows, chans), by_half(vocab), by_half(5), by_half(groups),
                by_seq(2, pairs, chans), whole(2, 4, 8, width), whole(seqs, 8, width),
                whole(seqs, 8, width), whole(seqs, 8, width),
            ],
            out_specs=[whole(total // 2, 128), whole(total // 2, 128)],
            scratch_shapes=[
                vmem((128, chans), F32), vmem((384, chans), BF16), vmem((6, TJ, 128), F32),
                vmem((5, 8, width), F32), vmem((seqs, 2, 8, width), F32), vmem((8, width), F32),
                vmem((2, 8 + pairs, chans), F32), vmem((2, pairs + 8, chans), F32),
                vmem((2 * width, chans + 128), BF16), vmem((VP, 2 * width), BF16), vmem((384, 128), F32),
                vmem((VP, chans), F32), vmem((5, 8, chans), F32), vmem((total, 128), F32),
            ],
        ),
        out_shape=[shape((total // 2, 128), F32)] * 2,
        compiler_params=params(40),
        name="backward",
    )(half, lengths, lang_ids, core.reshape(1), rows, cotangent, table, conv_w, score_w, emb, prob, weights, inner, other)

    def swap(x, step):
        return lax.ppermute(x, "seq", [(i, i ^ step) for i in range(seq_size)])

    mine = keep + swap(send, 1)
    quarter = total // 4
    held = lax.dynamic_slice_in_dim(mine, near * quarter, quarter, 0)
    sent = lax.dynamic_slice_in_dim(mine, (1 - near) * quarter, quarter, 0)
    held = held + swap(sent, 4)
    step = 2
    while step < seq_size:
        if step != 4:
            held = held + swap(held, step)
        step *= 2
    mine = jnp.concatenate([held, swap(held, 4)], axis=0)
    other = swap(mine, 1)

    place = jnp.stack([core, near, seq])
    triples = ((table, table_m, table_v), (conv_w, conv_m, conv_v), (score_w, score_m, score_v))
    counts = (vocab, 5, groups)
    in_specs = [whole(total // 2, 128), whole(total // 2, 128)]
    out_specs, out_shape = [], []
    for count in counts:
        in_specs += [by_half(count), whole(count, chans), whole(count, chans)]
        out_specs += [by_seq(count, chans)] * 3
        out_shape += [shape((1, count, chans), F32)] * 3
    updated = pl.pallas_call(
        update_kernel,
        grid_spec=pltpu.PrefetchScalarGridSpec(
            num_scalar_prefetch=3,
            grid=(1,),
            in_specs=in_specs,
            out_specs=out_specs,
            scratch_shapes=[vmem((total, 128), F32)],
        ),
        out_shape=out_shape,
        compiler_params=params(24),
        name="update",
    )(half, place, owners, mine, other, *[x for triple in triples for x in triple])
    return (pooled, *updated)


def solution(mesh):
    row, split, copied = P("seq"), P(None, "blk"), P()
    return jax.shard_map(
        functools.partial(local, mesh.shape["seq"]),
        mesh=mesh,
        in_specs=(P("seq", None), row, row, copied, copied, copied, copied, P("seq", None, "blk"))
        + (split,) * 6,
        out_specs=(P("seq", None, "blk"),) * 10,
        check_vma=False,
    )
```

time: 815 us -> 75.9 us (0.09); the launches traced: 800 us -> 75.6 us
  local copies, waits for them, and re-layouts: 365 us -> 15.5 us
  other arithmetic: 205 us -> 0.16 us
  blocking collectives: 180 us -> 0 us
  Pallas kernels: 0 us -> 32.9 us
  between operations: 16.6 us -> 0.98 us
  waiting for transfers between devices: 26.1 us -> 16.4 us
  starting transfers between devices: 0.16 us -> 9.63 us
    unnamed x61 -> x46, local copies, waits for them, and re-layouts: 307 us -> 15.5 us
    psum x3 -> x0, blocking collectives: 131 us -> none  [the longest x1 61.4 us: local(): whole_grad, score_whole = lax.psum((flat_grad, score_part), 'blk')]
    reduce_sum x5 -> x0, other arithmetic: 78.5 us -> none  [the longest x1 37.9 us: conv_backward(): tap_grads.append(jnp.sum(grad_conv * behind, axis=(0, 1)))]
    add x4, other arithmetic: 52.8 us -> 0.07 us  [the longest x1 0.03 us: local(): mine = keep + swap(send, 1)]
    mul x10 -> x0, other arithmetic: 52.3 us -> none  [the longest x2 20 us: pool_size(): totals = block_total(field * live_mask[..., None], size_val)]
    all_gather x1 -> x0, blocking collectives: 49 us -> none  [local(): all_scores = lax.all_gather(my_scores, 'blk', axis=0, tiled=True)]
    pallas_call x0 -> x4, Pallas kernels: none -> 32.9 us  [the longest x1 14.8 us: local(): pl.pallas_call(backward_kernel, grid_spec=pltpu.PrefetchScalarGridSpec(nu...]
    reshape x2 -> x0, local copies, waits for them, and re-layouts: 31.2 us -> none  [the longest x1 15.8 us: local(): grad_mixed = 0.5 * jnp.repeat(cot_full, 2, axis=1) * live_mask[..., None]]
  transfers between devices with their start and end apart: 4 -> 7, of which waited for: 1 -> 5; matrix products, arithmetic and copies ran while one was open for 59% -> 2% of each run, Pallas kernels for 0% -> 6%
where the time goes in v1:
time: 75.9 us; the launch traced here: 75.6 us
  Pallas kernels  32.9 us (43%)
  waiting for transfers between devices  16.4 us (22%)
  local copies, waits for them, and re-layouts  15.5 us (20%)
  starting transfers between devices  9.63 us (13%)
  between operations  0.98 us (1%)
    ppermute x6, waiting for transfers between devices, swap(): return lax.ppermute(x, 'seq', [(i, i ^ step) for i in range(seq_size)])  16.4 us
    unnamed x46, local copies, waits for them, and re-layouts  15.5 us
    pallas_call x1, Pallas kernels, local(): pl.pallas_call(backward_kernel, grid_spec=pltpu.PrefetchScalarGridSpec(nu...  14.8 us
    pallas_call x1, Pallas kernels, local(): pl.pallas_call(forward_kernel, grid_spec=pltpu.PrefetchScalarGridSpec(num...  12.1 us
    ppermute x6, starting transfers between devices, swap(): return lax.ppermute(x, 'seq', [(i, i ^ step) for i in range(seq_size)])  6.66 us
    pallas_call x1, Pallas kernels, local(): pl.pallas_call(pooled_kernel, grid_spec=pltpu.PrefetchScalarGridSpec(num_...  4.26 us
    ppermute x1, starting transfers between devices, local(): other = lax.ppermute(inner, 'blk', [(0, 1), (1, 0)])  2.97 us
    pallas_call x1, Pallas kernels, local(): pl.pallas_call(update_kernel, grid_spec=pltpu.PrefetchScalarGridSpec(num_...  1.83 us
  transfers between devices with their start and end apart: 7, of which 5 were waited for; matrix products, arithmetic and copies ran while one was open for 2% of the time, Pallas kernels for 6%

profile of v1, /device:TPU:0, one launch (start us, length us, event | category | flops | bytes accessed | tf_op | source)
XLA Modules:
  0.0 75.6 jit_solution(9698181359975676005)
XLA Ops:
  0.7 1.7 %copy.24.cot_ref = bf16[4,516,384]{2,1,0:T(8,128)(2,1)S(1)} copy(bf16[4,516,384]{2,0,1:T(4,128)(2,1)} %param.21) | data formatting | bytes 3170304 | tf_op args[7]
  2.4 0.0 copy-start.10
  2.4 0.0 copy-start.17
  2.4 12.1 %forward.1 = (bf16[4,2,576,384]{3,2,1,0:T(8,128)(2,1)S(1)}, bf16[4,6,192,384]{3,2,1,0:T(8,128)(2,1)S(1)}, f32[4,8,768]{2,1,0:T(8,128)S(1)}, f32[4,8,768]{2,1,0:T(8,128)S(1)}) custom-call(s32[1]{0:T(128)} %bitcast.half_ref, s32[4]{0:T(128)S(1)} %copy-done.16, s32[4,1032]{1,0:T(4,128)S(1)} %copy-done.11, bf16[4,516,384]{2,1,0:T(8,128)(2,1)S(1)} %copy.24.cot_ref, ...), custom_call_target="tpu_custom_call" | custom-call | tf_op jit(solution)/shard_map/forward/pallas_call | solution.py:475
  14.5 1.7 %copy-done.1 = bf16[4,2,576,384]{3,2,1,0:T(8,128)(2,1)} copy-done((bf16[4,2,576,384]{3,2,1,0:T(8,128)(2,1)}, bf16[4,2,576,384]{3,2,1,0:T(8,128)(2,1)S(1)}, u32[]{:S(2)}) %copy-start.1) | copy-done | bytes 3538968
  16.3 1.8 %copy-done.3 = bf16[4,6,192,384]{3,2,1,0:T(8,128)(2,1)} copy-done((bf16[4,6,192,384]{3,2,1,0:T(8,128)(2,1)}, bf16[4,6,192,384]{3,2,1,0:T(8,128)(2,1)S(1)}, u32[]{:S(2)}) %copy-start.3) | copy-done | bytes 3538968
  18.0 3.0 %collective-permute-start = (f32[4,8,768]{2,1,0:T(8,128)S(1)}, f32[4,8,768]{2,1,0:T(8,128)S(1)}, u32[]{:S(2)}, u32[]{:S(2)}) collective-permute-start(f32[4,8,768]{2,1,0:T(8,128)S(1)} %get-tuple-element.34.inner_ref), channel_id=1, source_target_pairs={{0,16},{16,0},{1,17},{17,1},{2,18},{18,2},{3,19},{19,3},{4,20},{20... | collective-permute-start | bytes 294920 | tf_op jit(solution)/shard_map/ppermute | solution.py:498
  21.0 2.0 %copy-done.4 = bf16[4,6,192,384]{3,2,1,0:T(8,128)(2,1)S(1)} copy-done((bf16[4,6,192,384]{3,2,1,0:T(8,128)(2,1)S(1)}, bf16[4,6,192,384]{3,2,1,0:T(8,128)(2,1)}, u32[]{:S(2)}) %copy-start.4) | copy-done | bytes 3538968
  23.0 4.3 %pooled.1 = (bf16[4,516,384]{2,1,0:T(8,128)(2,1)S(1)}, f32[2,4,8,768]{3,2,1,0:T(8,128)S(1)}, f32[4,8,768]{2,1,0:T(8,128)S(1)}) custom-call(s32[4]{0:T(128)S(1)} %copy-done.16, s32[4]{0:T(128)S(1)} %copy-done.17, f32[4,8,768]{2,1,0:T(8,128)S(1)} %get-tuple-element.28.rows_ref, f32[259,768]{1,0:T(8,128)S(1)} %copy-done, f32[5,768]{1,0:T(8,128)S(1)} %copy-done.9, ...), custom_call_target="tpu_custom_call" | custom-call | tf_op jit(solution)/shard_map/pooled/pallas_call | solution.py:500
  27.3 1.2 %copy-done.5 = bf16[4,516,384]{2,1,0:T(8,128)(2,1)} copy-done((bf16[4,516,384]{2,1,0:T(8,128)(2,1)}, bf16[4,516,384]{2,1,0:T(8,128)(2,1)S(1)}, u32[]{:S(2)}) %copy-start.5) | copy-done | bytes 1585176
  28.5 14.8 %backward.1 = (f32[416,128]{1,0:T(8,128)S(1)}, f32[416,128]{1,0:T(8,128)S(1)}) custom-call(s32[1]{0:T(128)} %bitcast.half_ref, s32[4]{0:T(128)S(1)} %copy-done.16, s32[4]{0:T(128)S(1)} %copy-done.17, s32[1]{0:T(128)} %bitcast.1.core_ref, f32[4,8,768]{2,1,0:T(8,128)S(1)} %get-tuple-element.28.rows_ref, bf16[4,516,384]{2,1,0:T(8,128)(2,1)S(1)} %copy.24.cot_ref, ...), custom_call_target="tpu_custom_call" | custom-call | tf_op jit(solution)/shard_map/backward/pallas_call | solution.py:523
  43.3 0.1 collective-permute-start.1
  43.4 1.4 %collective-permute-done.1 = f32[416,128]{1,0:T(8,128)S(1)} collective-permute-done((f32[416,128]{1,0:T(8,128)S(1)}, f32[416,128]{1,0:T(8,128)S(1)}, u32[]{:S(2)}, u32[]{:S(2)}) %collective-permute-start.1) | collective-permute-done | bytes 213024 | tf_op jit(solution)/shard_map/ppermute | solution.py:548
  44.9 1.6 %collective-permute-start.2 = (f32[208,128]{1,0:T(8,128)S(1)}, f32[208,128]{1,0:T(8,128)S(1)}, u32[]{:S(2)}, u32[]{:S(2)}) collective-permute-start(f32[208,128]{1,0:T(8,128)S(1)} %constant_dynamic-slice_fusion), channel_id=1, source_target_pairs={{0,4},{1,5},{2,6},{3,7},{4,0},{5,1},{6,2},{7,3},{8,12},{9,13},{10,... | collective-permute-start | bytes 319496 | tf_op jit(solution)/shard_map/ppermute | solution.py:548
  46.5 3.4 %collective-permute-done.2 = f32[208,128]{1,0:T(8,128)S(1)} collective-permute-done((f32[208,128]{1,0:T(8,128)S(1)}, f32[208,128]{1,0:T(8,128)S(1)}, u32[]{:S(2)}, u32[]{:S(2)}) %collective-permute-start.2) | collective-permute-done | bytes 106528 | tf_op jit(solution)/shard_map/ppermute | solution.py:548
  50.0 1.6 %collective-permute-start.3 = (f32[208,128]{1,0:T(8,128)S(1)}, f32[208,128]{1,0:T(8,128)S(1)}, u32[]{:S(2)}, u32[]{:S(2)}) collective-permute-start(f32[208,128]{1,0:T(8,128)S(1)} %dynamic-slice_add_fusion), channel_id=1, source_target_pairs={{0,2},{1,3},{2,0},{3,1},{4,6},{5,7},{6,4},{7,5},{8,10},{9,11},{10,... | collective-permute-start | bytes 319496 | tf_op jit(solution)/shard_map/ppermute | solution.py:548
  51.5 3.2 %collective-permute-done.3 = f32[208,128]{1,0:T(8,128)S(1)} collective-permute-done((f32[208,128]{1,0:T(8,128)S(1)}, f32[208,128]{1,0:T(8,128)S(1)}, u32[]{:S(2)}, u32[]{:S(2)}) %collective-permute-start.3) | collective-permute-done | bytes 106528 | tf_op jit(solution)/shard_map/ppermute | solution.py:548
  54.7 2.7 %collective-permute-start.4 = (f32[208,128]{1,0:T(8,128)S(1)}, f32[208,128]{1,0:T(8,128)S(1)}, u32[]{:S(2)}, u32[]{:S(2)}) collective-permute-start(f32[208,128]{1,0:T(8,128)S(1)} %add.32), channel_id=1, source_target_pairs={{0,8},{1,9},{2,10},{3,11},{4,12},{5,13},{6,14},{7,15},{8,0},{9,1},... | collective-permute-start | bytes 319496 | tf_op jit(solution)/shard_map/ppermute | solution.py:548
  57.4 4.3 %collective-permute-done.4 = f32[208,128]{1,0:T(8,128)S(1)} collective-permute-done((f32[208,128]{1,0:T(8,128)S(1)}, f32[208,128]{1,0:T(8,128)S(1)}, u32[]{:S(2)}, u32[]{:S(2)}) %collective-permute-start.4) | collective-permute-done | bytes 106528 | tf_op jit(solution)/shard_map/ppermute | solution.py:548
  61.7 0.6 collective-permute-start.5
  62.3 4.1 %collective-permute-done.5 = f32[208,128]{1,0:T(8,128)S(1)} collective-permute-done((f32[208,128]{1,0:T(8,128)S(1)}, f32[208,128]{1,0:T(8,128)S(1)}, u32[]{:S(2)}, u32[]{:S(2)}) %collective-permute-start.5) | collective-permute-done | bytes 106528 | tf_op jit(solution)/shard_map/ppermute | solution.py:548
  66.5 0.0 copy-start.8
  66.5 0.1 collective-permute-start.6
  66.6 1.8 %copy.26 = bf16[4,516,384]{2,0,1:T(4,128)(2,1)} copy(bf16[4,516,384]{2,1,0:T(8,128)(2,1)S(1)} %copy-done.6) | data formatting | bytes 3170304
  68.4 0.1 pad_add_fusion.place_ref
  68.5 1.8 %update.1 = (f32[1,259,384]{2,1,0:T(8,128)S(1)}, f32[1,259,384]{2,1,0:T(8,128)S(1)}, f32[1,259,384]{2,1,0:T(8,128)S(1)}, f32[1,5,384]{2,1,0:T(8,128)S(1)}, f32[1...) custom-call(s32[1]{0:T(128)} %bitcast.half_ref, ...), custom_call_target="tpu_custom_call" | custom-call | tf_op jit(solution)/shard_map/update/pallas_call | solution.py:572
  70.4 1.2 %copy.27 = f32[1,259,384]{2,0,1:T(1,128)} copy(f32[1,259,384]{2,1,0:T(8,128)S(1)} %get-tuple-element.47) | data formatting | bytes 795648
  71.5 1.2 %copy.28 = f32[1,259,384]{2,0,1:T(1,128)} copy(f32[1,259,384]{2,1,0:T(8,128)S(1)} %get-tuple-element.48) | data formatting | bytes 795648
  72.7 1.2 %copy.29 = f32[1,259,384]{2,0,1:T(1,128)} copy(f32[1,259,384]{2,1,0:T(8,128)S(1)} %get-tuple-element.49) | data formatting | bytes 795648
  73.8 0.6 copy.30
  74.4 0.6 copy.31
  75.0 0.6 copy.32
  (39 shorter events, 0.2 us)
Async XLA Ops:
  0.6 1.8 %copy-start.16 = (s32[4]{0:T(128)S(1)}, s32[4]{0:T(128)}, u32[]{:S(2)}) copy-start(s32[4]{0:T(128)} %len_ref.5) | copy-start | bytes 52
  0.7 1.8 %copy-start.11 = (s32[4,1032]{1,0:T(4,128)S(1)}, s32[4,1032]{1,0:T(4,128)}, u32[]{:S(2)}) copy-start(s32[4,1032]{1,0:T(4,128)} %ids_ref.1) | copy-start | bytes 49540
  0.7 1.8 %copy-start = (f32[259,768]{1,0:T(8,128)S(1)}, f32[259,768]{1,0:T(8,128)}, u32[]{:S(2)}) copy-start(f32[259,768]{1,0:T(8,128)} %refs_0_.1) | copy-start | bytes 2386948
  0.7 1.8 %copy-start.9 = (f32[5,768]{1,0:T(8,128)S(1)}, f32[5,768]{1,0:T(8,128)}, u32[]{:S(2)}) copy-start(f32[5,768]{1,0:T(8,128)} %refs_3_.1) | copy-start | bytes 46084
  2.4 18.6 %copy-start.10 = (f32[8,768]{1,0:T(8,128)S(1)}, f32[8,768]{1,0:T(8,128)}, u32[]{:S(2)}) copy-start(f32[8,768]{1,0:T(8,128)} %refs_6_.1) | copy-start | bytes 73732
  2.4 18.6 %copy-start.17 = (s32[4]{0:T(128)S(1)}, s32[4]{0:T(128)}, u32[]{:S(2)}) copy-start(s32[4]{0:T(128)} %lang_ref.3) | copy-start | bytes 52
  14.5 1.7 %copy-start.1 = (bf16[4,2,576,384]{3,2,1,0:T(8,128)(2,1)}, bf16[4,2,576,384]{3,2,1,0:T(8,128)(2,1)S(1)}, u32[]{:S(2)}) copy-start(bf16[4,2,576,384]{3,2,1,0:T(8,128)(2,1)S(1)} %get-tuple-element.31.emb_ref) | copy-start | bytes 10616836
  16.2 1.8 %copy-start.3 = (bf16[4,6,192,384]{3,2,1,0:T(8,128)(2,1)}, bf16[4,6,192,384]{3,2,1,0:T(8,128)(2,1)S(1)}, u32[]{:S(2)}) copy-start(bf16[4,6,192,384]{3,2,1,0:T(8,128)(2,1)S(1)} %get-tuple-element.29.conv_ref) | copy-start | bytes 10616836
  18.0 10.4 %collective-permute-start = (f32[4,8,768]{2,1,0:T(8,128)S(1)}, f32[4,8,768]{2,1,0:T(8,128)S(1)}, u32[]{:S(2)}, u32[]{:S(2)}) collective-permute-start(f32[4,8,768]{2,1,0:T(8,128)S(1)} %get-tuple-element.34.inner_ref), channel_id=1, source_target_pairs={{0,16},{16,0},{1,17},{17,1},{2,18},{18,2},{3,19},{19,3},{4,20},{20... | collective-permute-start | bytes 294920 | tf_op jit(solution)/shard_map/ppermute | solution.py:498
  21.0 2.0 %copy-start.4 = (bf16[4,6,192,384]{3,2,1,0:T(8,128)(2,1)S(1)}, bf16[4,6,192,384]{3,2,1,0:T(8,128)(2,1)}, u32[]{:S(2)}) copy-start(bf16[4,6,192,384]{3,2,1,0:T(8,128)(2,1)} %copy-done.3) | copy-start | bytes 10616836
  23.0 5.4 %copy-start.2 = (bf16[4,2,576,384]{3,2,1,0:T(8,128)(2,1)S(1)}, bf16[4,2,576,384]{3,2,1,0:T(8,128)(2,1)}, u32[]{:S(2)}) copy-start(bf16[4,2,576,384]{3,2,1,0:T(8,128)(2,1)} %copy-done.1) | copy-start | bytes 10616836
  27.3 1.2 %copy-start.5 = (bf16[4,516,384]{2,1,0:T(8,128)(2,1)}, bf16[4,516,384]{2,1,0:T(8,128)(2,1)S(1)}, u32[]{:S(2)}) copy-start(bf16[4,516,384]{2,1,0:T(8,128)(2,1)S(1)} %get-tuple-element.46) | copy-start | bytes 4755460
  43.3 23.4 %copy-start.6 = (bf16[4,516,384]{2,1,0:T(8,128)(2,1)S(1)}, bf16[4,516,384]{2,1,0:T(8,128)(2,1)}, u32[]{:S(2)}) copy-start(bf16[4,516,384]{2,1,0:T(8,128)(2,1)} %copy-done.5) | copy-start | bytes 4755460
  43.3 1.5 %collective-permute-start.1 = (f32[416,128]{1,0:T(8,128)S(1)}, f32[416,128]{1,0:T(8,128)S(1)}, u32[]{:S(2)}, u32[]{:S(2)}) collective-permute-start(f32[416,128]{1,0:T(8,128)S(1)} %get-tuple-element.36), channel_id=1, source_target_pairs={{0,1},{1,0},{2,3},{3,2},{4,5},{5,4},{6,7},{7,6},{8,9},{9,8},{10,11... | collective-permute-start | bytes 638984 | tf_op jit(solution)/shard_map/ppermute | solution.py:548
  44.9 5.1 %collective-permute-start.2 = (f32[208,128]{1,0:T(8,128)S(1)}, f32[208,128]{1,0:T(8,128)S(1)}, u32[]{:S(2)}, u32[]{:S(2)}) collective-permute-start(f32[208,128]{1,0:T(8,128)S(1)} %constant_dynamic-slice_fusion), channel_id=1, source_target_pairs={{0,4},{1,5},{2,6},{3,7},{4,0},{5,1},{6,2},{7,3},{8,12},{9,13},{10,... | collective-permute-start | bytes 319496 | tf_op jit(solution)/shard_map/ppermute | solution.py:548
  50.0 4.8 %collective-permute-start.3 = (f32[208,128]{1,0:T(8,128)S(1)}, f32[208,128]{1,0:T(8,128)S(1)}, u32[]{:S(2)}, u32[]{:S(2)}) collective-permute-start(f32[208,128]{1,0:T(8,128)S(1)} %dynamic-slice_add_fusion), channel_id=1, source_target_pairs={{0,2},{1,3},{2,0},{3,1},{4,6},{5,7},{6,4},{7,5},{8,10},{9,11},{10,... | collective-permute-start | bytes 319496 | tf_op jit(solution)/shard_map/ppermute | solution.py:548
  54.7 6.9 %collective-permute-start.4 = (f32[208,128]{1,0:T(8,128)S(1)}, f32[208,128]{1,0:T(8,128)S(1)}, u32[]{:S(2)}, u32[]{:S(2)}) collective-permute-start(f32[208,128]{1,0:T(8,128)S(1)} %add.32), channel_id=1, source_target_pairs={{0,8},{1,9},{2,10},{3,11},{4,12},{5,13},{6,14},{7,15},{8,0},{9,1},... | collective-permute-start | bytes 319496 | tf_op jit(solution)/shard_map/ppermute | solution.py:548
  61.7 4.8 %collective-permute-start.5 = (f32[208,128]{1,0:T(8,128)S(1)}, f32[208,128]{1,0:T(8,128)S(1)}, u32[]{:S(2)}, u32[]{:S(2)}) collective-permute-start(f32[208,128]{1,0:T(8,128)S(1)} %add.33), channel_id=1, source_target_pairs={{0,4},{1,5},{2,6},{3,7},{4,0},{5,1},{6,2},{7,3},{8,12},{9,13},{10,... | collective-permute-start | bytes 319496 | tf_op jit(solution)/shard_map/ppermute | solution.py:548
  66.5 2.0 %copy-start.7 = (f32[259,384]{1,0:T(8,128)S(1)}, f32[259,384]{1,0:T(8,128)}, u32[]{:S(2)}) copy-start(f32[259,384]{1,0:T(8,128)} %refs_1_.1) | copy-start | bytes 1193476
  66.5 2.0 %copy-start.8 = (f32[259,384]{1,0:T(8,128)S(1)}, f32[259,384]{1,0:T(8,128)}, u32[]{:S(2)}) copy-start(f32[259,384]{1,0:T(8,128)} %refs_2_.1) | copy-start | bytes 1193476
  66.5 2.0 %copy-start.12 = (f32[5,384]{1,0:T(8,128)S(1)}, f32[5,384]{1,0:T(8,128)}, u32[]{:S(2)}) copy-start(f32[5,384]{1,0:T(8,128)} %refs_4_.1) | copy-start | bytes 23044
  66.5 2.0 %copy-start.13 = (f32[5,384]{1,0:T(8,128)S(1)}, f32[5,384]{1,0:T(8,128)}, u32[]{:S(2)}) copy-start(f32[5,384]{1,0:T(8,128)} %refs_5_.1) | copy-start | bytes 23044
  66.5 2.0 %copy-start.14 = (f32[8,384]{1,0:T(8,128)S(1)}, f32[8,384]{1,0:T(8,128)}, u32[]{:S(2)}) copy-start(f32[8,384]{1,0:T(8,128)} %refs_7_.1) | copy-start | bytes 36868
  66.5 2.0 %copy-start.15 = (f32[8,384]{1,0:T(8,128)S(1)}, f32[8,384]{1,0:T(8,128)}, u32[]{:S(2)}) copy-start(f32[8,384]{1,0:T(8,128)} %refs_8_.1) | copy-start | bytes 36868
  66.5 2.0 %copy-start.18 = (s32[3]{0:T(128)S(1)}, s32[3]{0:T(128)}, u32[]{:S(2)}) copy-start(s32[3]{0:T(128)} %owner_ref.1) | copy-start | bytes 40
  66.5 1.9 %collective-permute-start.6 = (f32[416,128]{1,0:T(8,128)S(1)}, f32[416,128]{1,0:T(8,128)S(1)}, u32[]{:S(2)}, u32[]{:S(2)}) collective-permute-start(f32[416,128]{1,0:T(8,128)S(1)} %pad_maximum_fusion.mine_ref), channel_id=1, source_target_pairs={{0,1},{1,0},{2,3},{3,2},{4,5},{5,4},{6,7},{7,6},{8,9},{9,8},{10,11... | collective-permute-start | bytes 638984 | tf_op jit(solution)/shard_map/ppermute | solution.py:548

commit v2 on v0

v2 whole, which is shorter than its diff:
```python
import functools

import jax
import jax.numpy as jnp
from jax import lax
from jax.experimental import pallas as pl
from jax.experimental.pallas import tpu as pltpu
from jax.sharding import PartitionSpec as P

STEP_NUMBER = 5
F32, BF16 = jnp.float32, jnp.bfloat16
PLANES = 12
RP = 96
NO_ID = 511.0
VP = 272
FORWARD_MIB, BACKWARD_MIB, UPDATE_MIB = 32, 32, 16
NN = (((1,), (0,)), ((), ()))
NT = (((1,), (1,)), ((), ()))


def dot(a, b, dims=NN):
    return lax.dot_general(a, b, dims, preferred_element_type=F32)


def iota(shape, dim):
    return lax.broadcasted_iota(jnp.int32, shape, dim)


def split3(x):
    high = x.astype(BF16)
    rest = x - high.astype(F32)
    mid = rest.astype(BF16)
    return high, mid, (rest - mid.astype(F32)).astype(BF16)


def pick_row(x, index):
    return jnp.sum(jnp.where(iota(x.shape, 0) == index, x, 0.0), axis=0, keepdims=True)


def half_lanes(half_ref, chans):
    return pl.ds(pl.multiple_of(half_ref[0] * chans, 128), chans)


def load_table(table_ref, lanes, tail_ref, tab_ref, count):
    vocab = table_ref.shape[0]
    whole = vocab // 128 * 128
    tab_ref[:whole, :count] = table_ref[:whole, lanes].astype(BF16)
    tail_ref[...] = jnp.zeros(tail_ref.shape, F32)
    tail_ref[: vocab - whole, :] = table_ref[whole:, lanes]
    tab_ref[whole:, :count] = tail_ref[...].astype(BF16)


def blocks(x):
    two = [x[2 * p] + x[2 * p + 1] for p in range(6)]
    three = [two[0] + x[2], x[3] + two[2], two[3] + x[8], x[9] + two[5]]
    four = [two[0] + two[1], two[2] + two[3], two[4] + two[5]]
    return [x, two, three, four]


def live_planes(length):
    place = PLANES * iota((1, 128), 1)
    return [jnp.where(place + m < length, 1.0, 0.0).astype(F32) for m in range(PLANES)]


def inverse_counts(live):
    return [[1.0 / jnp.maximum(c, 1.0) for c in side] for side in blocks(live)]


def after_lane(x):
    return jnp.where(iota(x.shape, 1) == 127, 0.0, pltpu.roll(x, 127, 1))


def before_lane(x):
    return jnp.where(iota(x.shape, 1) == 0, 0.0, pltpu.roll(x, 1, 1))


def coefficients(weights):
    one, two, three, four = weights
    rows = [one[m] + two[m // 2 * 2] + two[m // 2 * 2 + 1] for m in range(PLANES)]
    rows += [four[2 * p] + four[2 * p + 1] for p in range(6)]
    for h in (0, 6):
        rows += [three[h] + three[h + 1], three[h + 2], three[h + 3], three[h + 4] + three[h + 5]]
    return rows


def pair_terms(pairs, sums):
    terms = [(m, m // 2, sums[0][m]) for m in range(PLANES)]
    terms += [(12 + p, p, sums[3][p // 2]) for p in range(6)]
    for h in range(2):
        for k, (p, j) in enumerate(((0, 0), (1, 0), (1, 1), (2, 1))):
            terms.append((18 + 4 * h + k, 3 * h + p, sums[2][2 * h + j]))
    return terms


THIRD = [18, 18, 19, 20, 21, 21, 22, 22, 23, 24, 25, 25]


def forward_kernel(
    half_ref, len_ref, lang_ref, ids_ref, cot_ref, table_ref, convw_ref, score_ref,
    emb_out, pooled_out, prob_out, coef_out, inner_out, rows_out,
    xs, cs, idcol, idc, tail, tab_all, looks, tail_half, tab, emb, conv_half, bias,
):
    s = pl.program_id(0)
    seqs, slot = ids_ref.shape
    rows, chans = cot_ref.shape[2:]
    mine = half_lanes(half_ref, chans)

    @pl.when(s == 0)
    def _():
        xs[...] = jnp.full(xs.shape, NO_ID, F32)
        xs[:seqs, :slot] = ids_ref[...].astype(F32)
        for i in range(xs.shape[1] // 128):
            cs[128 * i : 128 * (i + 1), :] = xs[:, 128 * i : 128 * (i + 1)].T
        idcol[...] = jnp.full(idcol.shape, NO_ID, F32)
        for m in range(PLANES):
            idcol[RP * m : RP * m + rows, :] = cs[pl.ds(m, rows, stride=PLANES), :]
        cols = idcol[...]
        high = jnp.floor(cols * (1.0 / 128.0))
        idc[:, 0:8] = (cols - 128.0 * high).astype(BF16)
        idc[:, 8:16] = high.astype(BF16)
        rows_out[...] = jnp.zeros(rows_out.shape, F32)
        for i in range(PLANES * RP // 128):
            flipped = idcol[128 * i : 128 * (i + 1), :].T
            for k in range(seqs):
                rows_out[k, 0:1, 128 * i : 128 * (i + 1)] = flipped[k : k + 1, :]
        load_table(table_ref, mine, tail_half, tab, chans)
        load_table(table_ref, slice(None), tail, tab_all, table_ref.shape[1])
        scores = score_ref[...]
        mixed = jnp.concatenate([convw_ref[k : k + 1, :] * scores for k in range(4)], axis=0)
        whole = tab_all[...]
        got = dot(jnp.concatenate([whole] * 3, axis=1), jnp.concatenate(split3(mixed), axis=1), NT)
        for k, part in enumerate(split3(got)):
            looks[k] = part
        constant = jnp.sum(convw_ref[4:5, :] * scores, axis=1, keepdims=True)
        bias[...] = jnp.broadcast_to(constant, bias.shape)
        conv_half[...] = convw_ref[:, mine]
        emb[PLANES * RP :, :] = jnp.zeros((emb.shape[0] - PLANES * RP, emb.shape[1]), F32)

    length, lang = len_ref[s], lang_ref[s]
    sub, lane = iota((32, 128), 0), iota((32, 128), 1)
    here = (sub % 8 == lang) & (lane % 8 == sub // 8)
    extra = 0.0
    for k in range(3):
        extra = extra + dot(looks[k], jnp.where(here & (lane // 8 == k), 1.0, 0.0).astype(BF16))
    tab[:, chans:] = extra.astype(BF16)
    sub = iota((16, 128), 0)
    spread = jnp.where(sub == s, 1.0, jnp.where(sub == s + 8, 128.0, 0.0)).astype(BF16)
    ids = dot(idc[...], spread)
    lane = iota((PLANES * RP, 128), 1).astype(F32)
    hot = jnp.concatenate([jnp.where(ids == lane + 128.0 * k, 1.0, 0.0).astype(BF16) for k in range(3)], axis=1)
    found = dot(hot, tab[...])
    emb[: PLANES * RP, :] = found
    emb_out[0] = found[:, :chans].astype(BF16)

    look = []
    for m in range(PLANES):
        x = emb[RP * m : RP * m + 128, chans : chans + 24].T
        look.append(x[0:8] + x[8:16] + x[16:24])
    ahead = {m: before_lane(look[m]) for m in (9, 10, 11)}
    live = live_planes(length)
    inverse = inverse_counts(live)
    base = pick_row(bias[...], lang)
    score = []
    for m in range(PLANES):
        value = base
        for k in range(4):
            x = look[m - k] if m >= k else ahead[m - k + PLANES]
            value = value + x[k : k + 1, :]
        score.append(jnp.where(live[m] > 0, value, 0.0))
    means = [[t * c for t, c in zip(side, inv)] for side, inv in zip(blocks(score), inverse)]
    weights = [[], [], [], []]
    for m in range(PLANES):
        own = [means[b][m // (b + 1)] for b in range(4)]
        top = functools.reduce(jnp.maximum, own)
        grown = [jnp.exp(x - top) for x in own]
        scale = 1.0 / functools.reduce(jnp.add, grown)
        for b in range(4):
            prob = grown[b] * scale
            prob_out[0, PLANES * b + m : PLANES * b + m + 1, :] = prob
            weights[b].append(0.5 * live[m] * prob * inverse[b][m // (b + 1)])
    coef_out[0, 24:32, :] = jnp.zeros((8, 128), F32)
    for k, row in enumerate(coefficients(weights)):
        coef_out[0, k : k + 1, :] = row
    coef = coef_out[0].T

    place = PLANES * iota((rows, 128), 0)
    inner = [0.0] * 26
    for c in range(chans // 128):
        lanes = slice(128 * c, 128 * (c + 1))
        w = [conv_half[k : k + 1, lanes] for k in range(5)]
        e = [emb[RP * m : RP * m + rows, lanes] for m in range(PLANES)]
        behind = {m: emb[RP * m - 1 : RP * m - 1 + rows, lanes] for m in (9, 10, 11)}
        conv = []
        for m in range(PLANES):
            value = w[4] + w[0] * e[m]
            for k in range(1, 4):
                value = value + w[k] * (e[m - k] if m >= k else behind[m - k + PLANES])
            conv.append(jnp.where(place < length - m, value, 0.0))
        cot = [cot_ref[0, p, :, lanes].astype(F32) for p in range(6)]
        pooled = [0.0] * 6
        for k, p, x in pair_terms(cot, blocks(conv)):
            inner[k] = inner[k] + cot[p] * x
            pooled[p] = pooled[p] + coef[:rows, k : k + 1] * x
        for p in range(6):
            pooled_out[0, p, :, lanes] = pooled[p].astype(BF16)
    lane = iota((rows, 128), 1)
    cols = jnp.zeros((rows, 128), F32)
    for k in range(26):
        cols = jnp.where(lane == k, jnp.sum(inner[k], axis=1, keepdims=True), cols)
    inner_out[0] = jnp.zeros((32, 128), F32)
    inner_out[0, :, :rows] = cols.T[:32]


def backward_kernel(
    half_ref, len_ref, lang_ref, core_ref, rows_ref, cot_ref, table_ref, convw_ref, score_ref,
    emb_ref, prob_ref, coef_ref, inner_ref, other_ref,
    keep_out, send_out,
    tail, tab, pulls, mixed, grad, gemb, hist, acc, taps_acc, flat, conv_half, score_half,
):
    s = pl.program_id(0)
    seqs = len_ref.shape[0]
    rows, chans = cot_ref.shape[2:]
    groups = score_ref.shape[0]
    mine = half_lanes(half_ref, chans)
    padded = (rows + 7) // 8 * 8

    @pl.when(s == 0)
    def _():
        load_table(table_ref, mine, tail, tab, chans)
        pulls[...] = jnp.zeros(pulls.shape, F32)
        mixed[...] = jnp.zeros(mixed.shape, F32)
        grad[...] = jnp.zeros(grad.shape, F32)
        acc[...] = jnp.zeros(acc.shape, F32)
        taps_acc[...] = jnp.zeros(taps_acc.shape, F32)
        hist[...] = jnp.zeros(hist.shape, F32)
        conv_half[...] = convw_ref[:, mine]
        score_half[...] = score_ref[:, mine]

    length, lang = len_ref[s], lang_ref[s]
    both = inner_ref[0] + other_ref[0]
    live = live_planes(length)
    inverse = inverse_counts(live)
    row = lambda k: both[k : k + 1, :]
    pull = [[], [], [], []]
    for m in range(PLANES):
        p = m // 2
        dots = [row(m), row(2 * p) + row(2 * p + 1), row(THIRD[m]), row(12 + p)]
        prob = [prob_ref[0, PLANES * b + m : PLANES * b + m + 1, :] for b in range(4)]
        inv = [inverse[b][m // (b + 1)] for b in range(4)]
        inner = [0.5 * jnp.where(live[m] > 0, d, 0.0) * c for d, c in zip(dots, inv)]
        mean = functools.reduce(jnp.add, [x * y for x, y in zip(prob, inner)])
        for b in range(4):
            pull[b].append(prob[b] * (inner[b] - mean) * inv[b])
    totals = [blocks(pull[b])[b] for b in range(4)]
    pull = [live[m] * (totals[0][m] + totals[1][m // 2] + totals[2][m // 3] + totals[3][m // 4]) for m in range(PLANES)]
    whole = jnp.sum(functools.reduce(jnp.add, pull), axis=1, keepdims=True)
    mixed[0:32, :] = coef_ref[0]
    for m in range(PLANES):
        mixed[32 + m : 33 + m, :] = pull[m]
    for m, x in enumerate(pull + [after_lane(x) for x in pull[:3]]):
        high = x.astype(BF16).astype(F32)
        pulls[m : m + 1, :] = high
        pulls[64 + m : 65 + m, :] = x - high
    coef = mixed[...].T
    turned = pulls[...].T
    for m in range(PLANES):
        x = turned if m == 0 else pltpu.roll(turned, 128 - m, 1)
        gemb[RP * m : RP * (m + 1), chans:] = x[:RP].astype(BF16)

    score = pick_row(score_half[...], lang)
    place = PLANES * iota((rows, 128), 0)
    for c in range(chans // 128):
        lanes = slice(128 * c, 128 * (c + 1))
        w = [conv_half[k : k + 1, lanes] for k in range(4)]
        cot = [cot_ref[0, p, :, lanes].astype(F32) for p in range(6)]
        times = lambda k, p: coef[:rows, k : k + 1] * cot[p]
        four = [times(12 + 2 * n, 2 * n) + times(13 + 2 * n, 2 * n + 1) for n in range(3)]
        three = []
        for h in range(2):
            three.append(times(18 + 4 * h, 3 * h) + times(19 + 4 * h, 3 * h + 1))
            three.append(times(20 + 4 * h, 3 * h + 1) + times(21 + 4 * h, 3 * h + 2))
        for m in range(PLANES):
            value = times(m, m // 2) + four[m // 4] + three[m // 3] + coef[:rows, 32 + m : 33 + m] * score[:, lanes]
            grad[c, RP * m : RP * m + rows, :] = jnp.where(place < length - m, value, 0.0)
        g = [grad[c, RP * m : RP * m + padded, :] for m in range(PLANES)]
        g += [grad[c, RP * m + 1 : RP * m + 1 + padded, :] for m in range(3)]
        tap = [0.0] * 5
        fold = lambda x: jnp.sum(x.reshape(padded // 8, 8, 128), axis=0)
        for m in range(PLANES):
            back = w[0] * g[m] + w[1] * g[m + 1] + w[2] * g[m + 2] + w[3] * g[m + 3]
            back = jnp.concatenate([back, jnp.zeros((RP - padded, 128), F32)], axis=0)
            gemb[RP * m : RP * (m + 1), lanes] = back.astype(BF16)
            e = emb_ref[0, RP * m : RP * (m + 1), lanes].astype(F32)[:padded]
            for k in range(4):
                tap[k] = tap[k] + fold(e * g[m + k])
            tap[4] = tap[4] + fold(g[m])
        for k in range(5):
            taps_acc[k, :, lanes] += tap[k]
    sub = iota((VP, PLANES * RP), 0).astype(F32)
    hot = jnp.where(rows_ref[0, 0:1, :] == sub, 1.0, 0.0).astype(BF16)
    got = dot(hot, gemb[...])
    acc[...] += got[:, :chans]
    hist[:VP, :] = got[:, chans:]
    counts = hist[...].T
    counts = counts[0:8] + counts[64:72]
    counts = jnp.concatenate(split3(jnp.concatenate([counts, jnp.zeros((8, 384), F32)], axis=0)), axis=0)
    from_table = dot(counts, tab[...])
    from_table = from_table[:16] + from_table[16:32] + from_table[32:]
    part = conv_half[4:5, :] * whole
    for k in range(4):
        part = part + conv_half[k : k + 1, :] * from_table[k : k + 1, :]
    acc[VP - groups : VP, :] += jnp.where(iota((groups, chans), 0) == lang, part, 0.0)

    @pl.when(s == seqs - 1)
    def _():
        for k in range(5):
            at = VP - groups - 5 + k
            acc[at : at + 1, :] = jnp.sum(taps_acc[k], axis=0, keepdims=True)
        flat[...] = jnp.zeros(flat.shape, F32)
        for k in range(chans // 128):
            flat[VP * k : VP * (k + 1), :] = acc[:, 128 * k : 128 * (k + 1)]
        part = keep_out.shape[0]
        own = pl.multiple_of(core_ref[0] * part, 8)
        theirs = pl.multiple_of((1 - core_ref[0]) * part, 8)
        keep_out[...] = flat[pl.ds(own, part), :]
        send_out[...] = flat[pl.ds(theirs, part), :]


def adamw(weight, grad, moment, second, rate):
    new_m = 0.9 * moment + 0.1 * grad
    new_v = 0.999 * second + 0.001 * grad * grad
    m_hat = new_m / (1.0 - 0.9**STEP_NUMBER)
    v_hat = new_v / (1.0 - 0.999**STEP_NUMBER)
    new_w = weight - rate * (m_hat / (jnp.sqrt(v_hat) + 1e-08) + 0.01 * weight)
    return new_m, new_v, new_w


def update_kernel(half_ref, place_ref, owner_ref, mine_ref, other_ref, *refs):
    ins, outs, flat = refs[:9], refs[9:18], refs[18]
    core, near, seq = place_ref[0], place_ref[1], place_ref[2]
    rows = mine_ref.shape[0] // 2
    for side, ref in ((core, mine_ref), (1 - core, other_ref)):
        for k in range(2):
            piece = near if k == 0 else 1 - near
            flat[pl.ds(pl.multiple_of((2 * side + piece) * rows, 8), rows), :] = ref[k * rows : (k + 1) * rows, :]
    vocab, chans = ins[1].shape
    groups = ins[6].shape[0]
    spans = ((0, vocab), (VP - groups - 5, 5), (VP - groups, groups))
    for t, rate in enumerate((0.5, 0.3, 0.05)):
        first, count = spans[t]
        owned = owner_ref[t] == seq
        for k in range(chans // 128):
            lanes = slice(128 * k, 128 * (k + 1))
            weight = ins[3 * t][:, pl.ds(pl.multiple_of(half_ref[0] * chans + 128 * k, 128), 128)]
            grad = flat[VP * k + first : VP * k + first + count, :]
            new = adamw(weight, grad, ins[3 * t + 1][:, lanes], ins[3 * t + 2][:, lanes], rate)
            for q in range(3):
                out = outs[3 * t + q]
                value = jnp.where(owned, new[q], 0.0)
                if count == groups:
                    out[0, :, lanes] = value
                else:
                    out[:, 0, lanes] = value


def local(
    seq_size, byte_ids, lengths, lang_ids, owners, table, conv_w, score_w, cotangent,
    table_m, table_v, conv_m, conv_v, score_m, score_v,
):
    seqs, slot = byte_ids.shape
    vocab, full = table.shape
    half_rows, chans = cotangent.shape[1:]
    groups = score_w.shape[0]
    rows = slot // PLANES
    assert rows * PLANES == slot and rows <= RP - 2
    half = lax.axis_index("blk").astype(jnp.int32).reshape(1)
    seq = lax.axis_index("seq").astype(jnp.int32)
    core, near = seq % 2, (seq // 4) % 2
    vmem = pltpu.VMEM
    shape = jax.ShapeDtypeStruct
    whole = lambda *dims: pl.BlockSpec(dims, lambda s, *_: (0,) * len(dims))
    by_seq = lambda *dims: pl.BlockSpec((1,) + dims, lambda s, *_: (s,) + (0,) * len(dims))

    def call(kernel, name, scalars, arrays, in_specs, outs, out_specs, scratch, mib, steps):
        return pl.pallas_call(
            kernel,
            grid_spec=pltpu.PrefetchScalarGridSpec(
                num_scalar_prefetch=len(scalars), grid=(steps,),
                in_specs=in_specs, out_specs=out_specs, scratch_shapes=scratch,
            ),
            out_shape=outs,
            compiler_params=pltpu.CompilerParams(
                vmem_limit_bytes=mib * 1024 * 1024, dimension_semantics=("arbitrary",)
            ),
            name=name,
        )(*scalars, *arrays)

    planes = cotangent.reshape(seqs, rows, 6, chans).transpose(0, 2, 1, 3)
    long = PLANES * RP
    emb, pooled, prob, coef, inner, id_rows = call(
        forward_kernel, "forward",
        [half, lengths, lang_ids], [byte_ids, planes, table, conv_w, score_w],
        [whole(seqs, slot), by_seq(6, rows, chans), whole(vocab, full), whole(5, full), whole(groups, full)],
        [
            pltpu.HBM((seqs, long, chans), BF16), pltpu.HBM((seqs, 6, rows, chans), BF16),
            shape((seqs, 48, 128), F32), shape((seqs, 32, 128), F32), shape((seqs, 32, 128), F32),
            shape((seqs, 8, long), F32),
        ],
        [
            by_seq(long, chans), by_seq(6, rows, chans), by_seq(48, 128), by_seq(32, 128), by_seq(32, 128),
            whole(seqs, 8, long),
        ],
        [
            vmem((8, long), F32), vmem((long, 8), F32), vmem((long, 8), F32), vmem((long, 16), BF16),
            vmem((128, full), F32), vmem((384, full), BF16), vmem((3, 384, 32), BF16),
            vmem((128, chans), F32), vmem((384, chans + 128), BF16), vmem((long + 32, chans + 128), F32),
            vmem((5, chans), F32), vmem((8, 128), F32),
        ],
        FORWARD_MIB, seqs,
    )
    other = lax.ppermute(inner, "blk", [(0, 1), (1, 0)])
    emb = pltpu.with_memory_space_constraint(emb, pltpu.HBM)
    total = -(-VP * (chans // 128) // 32) * 32
    keep, send = call(
        backward_kernel, "backward",
        [half, lengths, lang_ids, core.reshape(1)],
        [id_rows, planes, table, conv_w, score_w, emb, prob, coef, inner, other],
        [
            by_seq(8, long), by_seq(6, rows, chans), whole(vocab, full), whole(5, full), whole(groups, full),
            by_seq(long, chans), by_seq(48, 128), by_seq(32, 128), by_seq(32, 128), by_seq(32, 128),
        ],
        [shape((total // 2, 128), F32)] * 2,
        [whole(total // 2, 128)] * 2,
        [
            vmem((128, chans), F32), vmem((384, chans), BF16), vmem((128, 128), F32), vmem((48, 128), F32),
            vmem((chans // 128, long + 8, 128), F32), vmem((long, chans + 128), BF16), vmem((384, 128), F32),
            vmem((VP, chans), F32), vmem((5, 8, chans), F32), vmem((total, 128), F32),
            vmem((5, chans), F32), vmem((groups, chans), F32),
        ],
        BACKWARD_MIB, seqs,
    )

    def swap(x, step):
        return lax.ppermute(x, "seq", [(i, i ^ step) for i in range(seq_size)])

    keep, pooled = lax.optimization_barrier((keep, pooled))
    pooled = pooled.transpose(0, 2, 1, 3).reshape(seqs, half_rows, chans)
    mine = keep + swap(send, 1)
    quarter = total // 4
    held = lax.dynamic_slice_in_dim(mine, near * quarter, quarter, 0)
    sent = lax.dynamic_slice_in_dim(mine, (1 - near) * quarter, quarter, 0)
    held = held + swap(sent, 4)
    step = 2
    while step < seq_size:
        if step != 4:
            sent = swap(held, step)
            if step * 2 == seq_size:
                sent, pooled = lax.optimization_barrier((sent, pooled))
            held = held + sent
        step *= 2
    mine = jnp.concatenate([held, swap(held, 4)], axis=0)
    other = swap(mine, 1)

    place = jnp.stack([core, near, seq])
    arrays = [mine, other, table, table_m, table_v, conv_w, conv_m, conv_v, score_w, score_m, score_v]
    outs = []
    for count in (vocab, 5):
        outs += [shape((count, 1, chans), F32)] * 3
    outs += [shape((1, groups, chans), F32)] * 3
    updated = call(
        update_kernel, "update",
        [half, place, owners], arrays, [whole(*x.shape) for x in arrays],
        outs, [whole(*x.shape) for x in outs], [vmem((total, 128), F32)], UPDATE_MIB, 1,
    )
    updated = [jnp.transpose(x, (1, 0, 2)) if k < 6 else x for k, x in enumerate(updated)]
    return (pooled, *updated)


def solution(mesh):
    row, split, copied = P("seq"), P(None, "blk"), P()
    return jax.shard_map(
        functools.partial(local, mesh.shape["seq"]),
        mesh=mesh,
        in_specs=(P("seq", None), row, row, copied, copied, copied, copied, P("seq", None, "blk"))
        + (split,) * 6,
        out_specs=(P("seq", None, "blk"),) * 10,
        check_vma=False,
    )
```

time: 815 us -> 61.1 us (0.07); the launches traced: 800 us -> 60.9 us
  local copies, waits for them, and re-layouts: 365 us -> 5.02 us
  other arithmetic: 205 us -> 0.16 us
  blocking collectives: 180 us -> 0 us
  Pallas kernels: 0 us -> 28.9 us
  between operations: 16.6 us -> 0.9 us
  waiting for transfers between devices: 26.1 us -> 14.5 us
  starting transfers between devices: 0.16 us -> 11.5 us
    unnamed x61 -> x26, local copies, waits for them, and re-layouts: 307 us -> 0.06 us
    psum x3 -> x0, blocking collectives: 131 us -> none  [the longest x1 61.4 us: local(): whole_grad, score_whole = lax.psum((flat_grad, score_part), 'blk')]
    reduce_sum x5 -> x0, other arithmetic: 78.5 us -> none  [the longest x1 37.9 us: conv_backward(): tap_grads.append(jnp.sum(grad_conv * behind, axis=(0, 1)))]
    add x4, other arithmetic: 52.8 us -> 0.07 us  [the longest x2 0.03 us: local(): held = held + sent]
    mul x10 -> x0, other arithmetic: 52.3 us -> none  [the longest x2 20 us: pool_size(): totals = block_total(field * live_mask[..., None], size_val)]
    all_gather x1 -> x0, blocking collectives: 49 us -> none  [local(): all_scores = lax.all_gather(my_scores, 'blk', axis=0, tiled=True)]
    reshape x2 -> x1, local copies, waits for them, and re-layouts: 31.2 us -> 1.69 us  [local(): planes = cotangent.reshape(seqs, rows, 6, chans).transpose(0, 2, 1, 3)]
    pallas_call x0 -> x3, Pallas kernels: none -> 28.9 us  [call(): pl.pallas_call(kernel, grid_spec=pltpu.PrefetchScalarGridSpec(num_scalar_...]
  transfers between devices with their start and end apart: 4 -> 7, of which waited for: 1 -> 6; matrix products, arithmetic and copies ran while one was open for 59% -> 5% of each run, Pallas kernels for 0% -> 0%
where the time goes in v2:
time: 61.1 us; the launch traced here: 60.9 us
  Pallas kernels  28.9 us (47%)
  waiting for transfers between devices  14.5 us (24%)
  starting transfers between devices  11.5 us (19%)
  local copies, waits for them, and re-layouts  5.02 us (8%)
  between operations  0.9 us (1%)
    pallas_call x3, Pallas kernels, call(): pl.pallas_call(kernel, grid_spec=pltpu.PrefetchScalarGridSpec(num_scalar_...  28.9 us
    ppermute x6, waiting for transfers between devices, swap(): return lax.ppermute(x, 'seq', [(i, i ^ step) for i in range(seq_size)])  12.2 us
    ppermute x6, starting transfers between devices, swap(): return lax.ppermute(x, 'seq', [(i, i ^ step) for i in range(seq_size)])  8.52 us
    transpose x1, local copies, waits for them, and re-layouts, local(): pooled = pooled.transpose(0, 2, 1, 3).reshape(seqs, half_rows, chans)  3.25 us
    ppermute x1, starting transfers between devices, local(): other = lax.ppermute(inner, 'blk', [(0, 1), (1, 0)])  2.94 us
    ppermute x1, waiting for transfers between devices, local(): other = lax.ppermute(inner, 'blk', [(0, 1), (1, 0)])  2.24 us
    reshape x1, local copies, waits for them, and re-layouts, local(): planes = cotangent.reshape(seqs, rows, 6, chans).transpose(0, 2, 1, 3)  1.69 us
  transfers between devices with their start and end apart: 7, of which 6 were waited for; matrix products, arithmetic and copies ran while one was open for 5% of the time, Pallas kernels for 0%

profile of v2, /device:TPU:0, one launch (start us, length us, event | category | flops | bytes accessed | tf_op | source)
XLA Modules:
  0.0 60.9 jit_solution(4723543684460077194)
XLA Ops:
  0.6 0.0 copy-start.4
  0.7 0.0 copy-start.3
  0.7 1.7 %copy.27 = bf16[4,86,6,384]{3,1,2,0:T(8,128)(2,1)S(1)} copy(bf16[4,86,6,384]{3,0,2,1:T(4,128)(2,1)} %bitcast.19) | data formatting | bytes 3170304 | tf_op jit(solution)/shard_map/reshape | solution.py:398
  2.4 0.0 copy-done.4
  2.4 0.0 copy-done.3
  2.4 0.0 copy-done
  2.4 0.0 copy-done.11
  2.4 0.0 copy-done.10
  2.5 0.0 copy-done.5
  2.5 12.9 %forward.1 = (bf16[4,1152,384]{2,1,0:T(8,128)(2,1)}, bf16[4,6,86,384]{3,2,1,0:T(8,128)(2,1)}, f32[4,48,128]{2,1,0:T(8,128)S(1)}, f32[4,32,128]{2,1,0:T(8,128)S(1...) custom-call(s32[1]{0:T(128)} %bitcast.half_ref, s32[4]{0:T(128)S(1)} %copy-done.10, s32[4]{0:T(128)S(1)} %copy-done.11, ...), custom_call_target="tpu_custom_call" | custom-call | tf_op jit(solution)/shard_map/forward/pallas_call | solution.py:385
  15.4 2.9 %collective-permute-start = (f32[4,32,128]{2,1,0:T(8,128)S(1)}, f32[4,32,128]{2,1,0:T(8,128)S(1)}, u32[]{:S(2)}, u32[]{:S(2)}) collective-permute-start(f32[4,32,128]{2,1,0:T(8,128)S(1)} %get-tuple-element.35.inner_ref), channel_id=1, source_target_pairs={{0,16},{16,0},{1,17},{17,1},{2,18},{18,2},{3,19},{19,3},{4,20},{20... | collective-permute-start | bytes 196616 | tf_op jit(solution)/shard_map/ppermute | solution.py:421
  18.3 2.2 %collective-permute-done.other_ref = f32[4,32,128]{2,1,0:T(8,128)S(1)} collective-permute-done((f32[4,32,128]{2,1,0:T(8,128)S(1)}, f32[4,32,128]{2,1,0:T(8,128)S(1)}, u32[]{:S(2)}, u32[]{:S(2)}) %collective-permute-start) | collective-permute-done | bytes 65568 | tf_op jit(solution)/shard_map/ppermute | solution.py:421
  20.6 13.3 %backward.1 = (f32[416,128]{1,0:T(8,128)S(1)}, f32[416,128]{1,0:T(8,128)S(1)}) custom-call(s32[1]{0:T(128)} %bitcast.half_ref, s32[4]{0:T(128)S(1)} %copy-done.10, s32[4]{0:T(128)S(1)} %copy-done.11, s32[1]{0:T(128)} %bitcast.1.core_ref, f32[4,8,1152]{2,1,0:T(8,128)S(1)} %get-tuple-element.31.rows_ref, bf16[4,6,86,384]{3,2,1,0:T(8,128)(2,1)S(1)} %bitcast.17, ...), custom_call_target="tpu_custom_call" | custom-call | tf_op jit(solution)/shard_map/backward/pallas_call | solution.py:385
  33.9 0.1 collective-permute-start.1
  34.0 1.4 %collective-permute-done.1 = f32[416,128]{1,0:T(8,128)S(1)} collective-permute-done((f32[416,128]{1,0:T(8,128)S(1)}, f32[416,128]{1,0:T(8,128)S(1)}, u32[]{:S(2)}, u32[]{:S(2)}) %collective-permute-start.1) | collective-permute-done | bytes 213024 | tf_op jit(solution)/shard_map/ppermute | solution.py:444
  35.5 2.2 %collective-permute-start.2 = (f32[208,128]{1,0:T(8,128)S(1)}, f32[208,128]{1,0:T(8,128)S(1)}, u32[]{:S(2)}, u32[]{:S(2)}) collective-permute-start(f32[208,128]{1,0:T(8,128)S(1)} %constant_dynamic-slice_fusion), channel_id=1, source_target_pairs={{0,4},{1,5},{2,6},{3,7},{4,0},{5,1},{6,2},{7,3},{8,12},{9,13},{10,... | collective-permute-start | bytes 319496 | tf_op jit(solution)/shard_map/ppermute | solution.py:444
  37.7 3.3 %collective-permute-done.2 = f32[208,128]{1,0:T(8,128)S(1)} collective-permute-done((f32[208,128]{1,0:T(8,128)S(1)}, f32[208,128]{1,0:T(8,128)S(1)}, u32[]{:S(2)}, u32[]{:S(2)}) %collective-permute-start.2) | collective-permute-done | bytes 106528 | tf_op jit(solution)/shard_map/ppermute | solution.py:444
  41.0 1.7 %collective-permute-start.3 = (f32[208,128]{1,0:T(8,128)S(1)}, f32[208,128]{1,0:T(8,128)S(1)}, u32[]{:S(2)}, u32[]{:S(2)}) collective-permute-start(f32[208,128]{1,0:T(8,128)S(1)} %dynamic-slice_add_fusion), channel_id=1, source_target_pairs={{0,2},{1,3},{2,0},{3,1},{4,6},{5,7},{6,4},{7,5},{8,10},{9,11},{10,... | collective-permute-start | bytes 319496 | tf_op jit(solution)/shard_map/ppermute | solution.py:444
  42.7 3.0 %collective-permute-done.3 = f32[208,128]{1,0:T(8,128)S(1)} collective-permute-done((f32[208,128]{1,0:T(8,128)S(1)}, f32[208,128]{1,0:T(8,128)S(1)}, u32[]{:S(2)}, u32[]{:S(2)}) %collective-permute-start.3) | collective-permute-done | bytes 106528 | tf_op jit(solution)/shard_map/ppermute | solution.py:444
  45.7 2.8 %collective-permute-start.4 = (f32[208,128]{1,0:T(8,128)S(1)}, f32[208,128]{1,0:T(8,128)S(1)}, u32[]{:S(2)}, u32[]{:S(2)}) collective-permute-start(f32[208,128]{1,0:T(8,128)S(1)} %add.32), channel_id=1, source_target_pairs={{0,8},{1,9},{2,10},{3,11},{4,12},{5,13},{6,14},{7,15},{8,0},{9,1},... | collective-permute-start | bytes 319496 | tf_op jit(solution)/shard_map/ppermute | solution.py:444
  48.6 0.0 copy-start.8
  48.6 0.0 copy-start.9
  48.6 0.0 copy-start.12
  48.6 3.2 %copy.25 = bf16[4,86,6,384]{3,0,2,1:T(4,128)(2,1)} copy(bf16[4,86,6,384]{3,1,2,0:T(8,128)(2,1)} %bitcast.18) | data formatting | bytes 3170304 | tf_op jit(solution)/shard_map/transpose | solution.py:447
  51.9 0.0 collective-permute-done.4
  51.9 1.6 %collective-permute-start.5 = (f32[208,128]{1,0:T(8,128)S(1)}, f32[208,128]{1,0:T(8,128)S(1)}, u32[]{:S(2)}, u32[]{:S(2)}) collective-permute-start(f32[208,128]{1,0:T(8,128)S(1)} %add.33), channel_id=1, source_target_pairs={{0,4},{1,5},{2,6},{3,7},{4,0},{5,1},{6,2},{7,3},{8,12},{9,13},{10,... | collective-permute-start | bytes 319496 | tf_op jit(solution)/shard_map/ppermute | solution.py:444
  53.5 3.1 %collective-permute-done.5 = f32[208,128]{1,0:T(8,128)S(1)} collective-permute-done((f32[208,128]{1,0:T(8,128)S(1)}, f32[208,128]{1,0:T(8,128)S(1)}, u32[]{:S(2)}, u32[]{:S(2)}) %collective-permute-start.5) | collective-permute-done | bytes 106528 | tf_op jit(solution)/shard_map/ppermute | solution.py:444
  56.7 0.1 collective-permute-start.6
  56.7 0.1 pad_add_fusion.place_ref
  56.8 1.4 %collective-permute-done.6.other_ref = f32[416,128]{1,0:T(8,128)S(1)} collective-permute-done((f32[416,128]{1,0:T(8,128)S(1)}, f32[416,128]{1,0:T(8,128)S(1)}, u32[]{:S(2)}, u32[]{:S(2)}) %collective-permute-start.6) | collective-permute-done | bytes 213024 | tf_op jit(solution)/shard_map/ppermute | solution.py:444
  58.2 0.0 copy-done.2
  58.2 2.6 %update.1 = (f32[259,1,384]{2,1,0:T(1,128)}, f32[259,1,384]{2,1,0:T(1,128)}, f32[259,1,384]{2,1,0:T(1,128)}, f32[5,1,384]{2,1,0:T(1,128)}, f32[5,1,384]{2,1,0:T(...) custom-call(s32[1]{0:T(128)} %bitcast.half_ref, ...), custom_call_target="tpu_custom_call" | custom-call | tf_op jit(solution)/shard_map/update/pallas_call | solution.py:385
  (20 shorter events, 0.1 us)
Async XLA Ops:
  0.6 1.8 %copy-start.4 = (f32[8,768]{1,0:T(8,128)S(1)}, f32[8,768]{1,0:T(8,128)}, u32[]{:S(2)}) copy-start(f32[8,768]{1,0:T(8,128)} %refs_6_.1) | copy-start | bytes 73732
  0.7 1.8 %copy-start.3 = (f32[5,768]{1,0:T(8,128)S(1)}, f32[5,768]{1,0:T(8,128)}, u32[]{:S(2)}) copy-start(f32[5,768]{1,0:T(8,128)} %refs_3_.1) | copy-start | bytes 46084
  0.7 1.8 %copy-start = (f32[259,768]{1,0:T(8,128)S(1)}, f32[259,768]{1,0:T(8,128)}, u32[]{:S(2)}) copy-start(f32[259,768]{1,0:T(8,128)} %refs_0_.1) | copy-start | bytes 2386948
  0.7 1.8 %copy-start.11 = (s32[4]{0:T(128)S(1)}, s32[4]{0:T(128)}, u32[]{:S(2)}) copy-start(s32[4]{0:T(128)} %lang_ref.3) | copy-start | bytes 52
  0.7 1.8 %copy-start.10 = (s32[4]{0:T(128)S(1)}, s32[4]{0:T(128)}, u32[]{:S(2)}) copy-start(s32[4]{0:T(128)} %len_ref.3) | copy-start | bytes 52
  0.7 1.8 %copy-start.5 = (s32[4,1032]{1,0:T(4,128)S(1)}, s32[4,1032]{1,0:T(4,128)}, u32[]{:S(2)}) copy-start(s32[4,1032]{1,0:T(4,128)} %ids_ref.1) | copy-start | bytes 49540
  15.4 5.2 %collective-permute-start = (f32[4,32,128]{2,1,0:T(8,128)S(1)}, f32[4,32,128]{2,1,0:T(8,128)S(1)}, u32[]{:S(2)}, u32[]{:S(2)}) collective-permute-start(f32[4,32,128]{2,1,0:T(8,128)S(1)} %get-tuple-element.35.inner_ref), channel_id=1, source_target_pairs={{0,16},{16,0},{1,17},{17,1},{2,18},{18,2},{3,19},{19,3},{4,20},{20... | collective-permute-start | bytes 196616 | tf_op jit(solution)/shard_map/ppermute | solution.py:421
  33.9 1.5 %collective-permute-start.1 = (f32[416,128]{1,0:T(8,128)S(1)}, f32[416,128]{1,0:T(8,128)S(1)}, u32[]{:S(2)}, u32[]{:S(2)}) collective-permute-start(f32[416,128]{1,0:T(8,128)S(1)} %get-tuple-element.39), channel_id=1, source_target_pairs={{0,1},{1,0},{2,3},{3,2},{4,5},{5,4},{6,7},{7,6},{8,9},{9,8},{10,11... | collective-permute-start | bytes 638984 | tf_op jit(solution)/shard_map/ppermute | solution.py:444
  35.5 5.4 %collective-permute-start.2 = (f32[208,128]{1,0:T(8,128)S(1)}, f32[208,128]{1,0:T(8,128)S(1)}, u32[]{:S(2)}, u32[]{:S(2)}) collective-permute-start(f32[208,128]{1,0:T(8,128)S(1)} %constant_dynamic-slice_fusion), channel_id=1, source_target_pairs={{0,4},{1,5},{2,6},{3,7},{4,0},{5,1},{6,2},{7,3},{8,12},{9,13},{10,... | collective-permute-start | bytes 319496 | tf_op jit(solution)/shard_map/ppermute | solution.py:444
  41.0 4.8 %collective-permute-start.3 = (f32[208,128]{1,0:T(8,128)S(1)}, f32[208,128]{1,0:T(8,128)S(1)}, u32[]{:S(2)}, u32[]{:S(2)}) collective-permute-start(f32[208,128]{1,0:T(8,128)S(1)} %dynamic-slice_add_fusion), channel_id=1, source_target_pairs={{0,2},{1,3},{2,0},{3,1},{4,6},{5,7},{6,4},{7,5},{8,10},{9,11},{10,... | collective-permute-start | bytes 319496 | tf_op jit(solution)/shard_map/ppermute | solution.py:444
  45.7 6.1 %collective-permute-start.4 = (f32[208,128]{1,0:T(8,128)S(1)}, f32[208,128]{1,0:T(8,128)S(1)}, u32[]{:S(2)}, u32[]{:S(2)}) collective-permute-start(f32[208,128]{1,0:T(8,128)S(1)} %add.32), channel_id=1, source_target_pairs={{0,8},{1,9},{2,10},{3,11},{4,12},{5,13},{6,14},{7,15},{8,0},{9,1},... | collective-permute-start | bytes 319496 | tf_op jit(solution)/shard_map/ppermute | solution.py:444
  48.6 9.6 %copy-start.1 = (f32[259,384]{1,0:T(8,128)S(1)}, f32[259,384]{1,0:T(8,128)}, u32[]{:S(2)}) copy-start(f32[259,384]{1,0:T(8,128)} %refs_1_.1) | copy-start | bytes 1193476
  48.6 9.6 %copy-start.2 = (f32[259,384]{1,0:T(8,128)S(1)}, f32[259,384]{1,0:T(8,128)}, u32[]{:S(2)}) copy-start(f32[259,384]{1,0:T(8,128)} %refs_2_.1) | copy-start | bytes 1193476
  48.6 9.6 %copy-start.6 = (f32[5,384]{1,0:T(8,128)S(1)}, f32[5,384]{1,0:T(8,128)}, u32[]{:S(2)}) copy-start(f32[5,384]{1,0:T(8,128)} %refs_4_.1) | copy-start | bytes 23044
  48.6 9.6 %copy-start.7 = (f32[5,384]{1,0:T(8,128)S(1)}, f32[5,384]{1,0:T(8,128)}, u32[]{:S(2)}) copy-start(f32[5,384]{1,0:T(8,128)} %refs_5_.1) | copy-start | bytes 23044
  48.6 9.6 %copy-start.8 = (f32[8,384]{1,0:T(8,128)S(1)}, f32[8,384]{1,0:T(8,128)}, u32[]{:S(2)}) copy-start(f32[8,384]{1,0:T(8,128)} %refs_7_.1) | copy-start | bytes 36868
  48.6 9.6 %copy-start.9 = (f32[8,384]{1,0:T(8,128)S(1)}, f32[8,384]{1,0:T(8,128)}, u32[]{:S(2)}) copy-start(f32[8,384]{1,0:T(8,128)} %refs_8_.1) | copy-start | bytes 36868
  48.6 9.6 %copy-start.12 = (s32[3]{0:T(128)S(1)}, s32[3]{0:T(128)}, u32[]{:S(2)}) copy-start(s32[3]{0:T(128)} %owner_ref.1) | copy-start | bytes 40
  51.9 4.8 %collective-permute-start.5 = (f32[208,128]{1,0:T(8,128)S(1)}, f32[208,128]{1,0:T(8,128)S(1)}, u32[]{:S(2)}, u32[]{:S(2)}) collective-permute-start(f32[208,128]{1,0:T(8,128)S(1)} %add.33), channel_id=1, source_target_pairs={{0,4},{1,5},{2,6},{3,7},{4,0},{5,1},{6,2},{7,3},{8,12},{9,13},{10,... | collective-permute-start | bytes 319496 | tf_op jit(solution)/shard_map/ppermute | solution.py:444
  56.7 1.5 %collective-permute-start.6 = (f32[416,128]{1,0:T(8,128)S(1)}, f32[416,128]{1,0:T(8,128)S(1)}, u32[]{:S(2)}, u32[]{:S(2)}) collective-permute-start(f32[416,128]{1,0:T(8,128)S(1)} %pad_maximum_fusion.mine_ref), channel_id=1, source_target_pairs={{0,1},{1,0},{2,3},{3,2},{4,5},{5,4},{6,7},{7,6},{8,9},{9,8},{10,11... | collective-permute-start | bytes 638984 | tf_op jit(solution)/shard_map/ppermute | solution.py:444

commit v3 on v2

v3 whole, which is shorter than its diff:
```python
import functools

import jax
import jax.numpy as jnp
from jax import lax
from jax.experimental import pallas as pl
from jax.experimental.pallas import tpu as pltpu
from jax.sharding import PartitionSpec as P

STEP_NUMBER = 5
F32, BF16 = jnp.float32, jnp.bfloat16
PLANES = 12
RP = 96
NO_ID = 511.0
VP = 272
FORWARD_MIB, POOLED_MIB, BACKWARD_MIB, UPDATE_MIB = 32, 16, 32, 16
NN = (((1,), (0,)), ((), ()))
NT = (((1,), (1,)), ((), ()))


def dot(a, b, dims=NN):
    return lax.dot_general(a, b, dims, preferred_element_type=F32)


def iota(shape, dim):
    return lax.broadcasted_iota(jnp.int32, shape, dim)


def split3(x):
    high = x.astype(BF16)
    rest = x - high.astype(F32)
    mid = rest.astype(BF16)
    return high, mid, (rest - mid.astype(F32)).astype(BF16)


def pick_row(x, index):
    return jnp.sum(jnp.where(iota(x.shape, 0) == index, x, 0.0), axis=0, keepdims=True)


def half_lanes(half_ref, chans):
    return pl.ds(pl.multiple_of(half_ref[0] * chans, 128), chans)


def load_table(table_ref, lanes, tail_ref, tab_ref, count):
    vocab = table_ref.shape[0]
    whole = vocab // 128 * 128
    tab_ref[:whole, :count] = table_ref[:whole, lanes].astype(BF16)
    tail_ref[...] = jnp.zeros(tail_ref.shape, F32)
    tail_ref[: vocab - whole, :] = table_ref[whole:, lanes]
    tab_ref[whole:, :count] = tail_ref[...].astype(BF16)


def blocks(x):
    two = [x[2 * p] + x[2 * p + 1] for p in range(6)]
    three = [two[0] + x[2], x[3] + two[2], two[3] + x[8], x[9] + two[5]]
    four = [two[0] + two[1], two[2] + two[3], two[4] + two[5]]
    return [x, two, three, four]


def live_planes(length):
    place = PLANES * iota((1, 128), 1)
    return [jnp.where(place + m < length, 1.0, 0.0).astype(F32) for m in range(PLANES)]


def inverse_counts(live):
    return [[1.0 / jnp.maximum(c, 1.0) for c in side] for side in blocks(live)]


def after_lane(x):
    return jnp.where(iota(x.shape, 1) == 127, 0.0, pltpu.roll(x, 127, 1))


def before_lane(x):
    return jnp.where(iota(x.shape, 1) == 0, 0.0, pltpu.roll(x, 1, 1))


def coefficients(weights):
    one, two, three, four = weights
    rows = [one[m] + two[m // 2 * 2] + two[m // 2 * 2 + 1] for m in range(PLANES)]
    rows += [four[2 * p] + four[2 * p + 1] for p in range(6)]
    for h in (0, 6):
        rows += [three[h] + three[h + 1], three[h + 2], three[h + 3], three[h + 4] + three[h + 5]]
    return rows


def convolved(w, e, behind, live):
    out = []
    for m in range(PLANES):
        value = w[4] + w[0] * e[m]
        for k in range(1, 4):
            value = value + w[k] * (e[m - k] if m >= k else behind[m - k + PLANES])
        out.append(jnp.where(live[m], value, 0.0))
    return out


def pair_terms(sums):
    terms = [(m, m // 2, sums[0][m]) for m in range(PLANES)]
    terms += [(12 + p, p, sums[3][p // 2]) for p in range(6)]
    for h in range(2):
        for k, (p, j) in enumerate(((0, 0), (1, 0), (1, 1), (2, 1))):
            terms.append((18 + 4 * h + k, 3 * h + p, sums[2][2 * h + j]))
    return terms


THIRD = [18, 18, 19, 20, 21, 21, 22, 22, 23, 24, 25, 25]


def forward_kernel(
    half_ref, len_ref, lang_ref, ids_ref, cot_ref, table_ref, convw_ref, score_ref,
    emb_out, conv_out, look_out, inner_out, rows_out,
    xs, cs, idcol, idc, tail, tab_all, looks, tail_half, tab, emb_a, emb_b, low_a, low_b,
    conv_half, cotf, turned, hots, conv_a, conv_b, sems,
):
    n = pl.program_id(0)
    seqs, slot = ids_ref.shape
    rows, chans = cot_ref.shape[2:]
    long = PLANES * RP
    mine = half_lanes(half_ref, chans)
    slots = ((emb_a, low_a), (emb_b, low_b))
    convs = (conv_a, conv_b)

    def send(q, k):
        return pltpu.make_async_copy(slots[k][1], emb_out.at[q], sems.at[k])

    def send_conv(q, k):
        return pltpu.make_async_copy(convs[k], conv_out.at[q], sems.at[2 + k])

    def look_up(q, slot_refs):
        emb, low = slot_refs
        lang = lang_ref[q]
        sub, lane = iota((32, 128), 0), iota((32, 128), 1)
        here = (sub % 8 == lang) & (lane % 8 == sub // 8)
        extra = 0.0
        for k in range(3):
            extra = extra + dot(looks[k], jnp.where(here & (lane // 8 == k), 1.0, 0.0).astype(BF16))
        tab[:, chans:] = extra.astype(BF16)
        sub = iota((16, 128), 0)
        spread = jnp.where(sub == q, 1.0, jnp.where(sub == q + 8, 128.0, 0.0)).astype(BF16)
        ids = dot(idc[...], spread)
        lane = iota((long, 128), 1).astype(F32)
        for k in range(3):
            hots[:, 128 * k : 128 * (k + 1)] = jnp.where(ids == lane + 128.0 * k, 1.0, 0.0).astype(BF16)
        found = dot(hots[...], tab[...])
        emb[:long, :] = found
        low[...] = found[:, :chans].astype(BF16)
        for m in range(PLANES):
            x = emb[RP * m : RP * m + 128, chans : chans + 24].T
            look_out[q, 8 * m : 8 * m + 8, :] = x[0:8] + x[8:16] + x[16:24]

    def convolve(q, u):
        emb, _ = slots[u]
        length = len_ref[q]
        for p in range(6):
            cotf[p, :rows, :] = cot_ref[u, p].astype(F32)
        place = PLANES * iota((8, 128), 0)
        lane = iota((8, 128), 1)
        for r in range(0, rows, 8):
            live = [place < length - (m + PLANES * r) for m in range(PLANES)]
            inner = [0.0] * 26
            for c in range(chans // 128):
                lanes = slice(128 * c, 128 * (c + 1))
                w = [conv_half[k : k + 1, lanes] for k in range(5)]
                e = [emb[RP * m + r : RP * m + r + 8, lanes] for m in range(PLANES)]
                behind = {m: emb[RP * m - 1 + r : RP * m + 7 + r, lanes] for m in (9, 10, 11)}
                conv = convolved(w, e, behind, live)
                for m in range(PLANES):
                    convs[u][m, r : r + 8, lanes] = conv[m]
                for k, p, x in pair_terms(blocks(conv)):
                    inner[k] = inner[k] + cotf[p, r : r + 8, lanes] * x
            out = jnp.zeros((8, 128), F32)
            for k in range(26):
                out = jnp.where(lane == k, jnp.sum(inner[k], axis=1, keepdims=True), out)
            turned[r : r + 8, :] = out
        inner_out[q] = turned[...].T[:32]

    @pl.when(n == 0)
    def _():
        xs[...] = jnp.full(xs.shape, NO_ID, F32)
        xs[:seqs, :slot] = ids_ref[...].astype(F32)
        for i in range(xs.shape[1] // 128):
            cs[128 * i : 128 * (i + 1), :] = xs[:, 128 * i : 128 * (i + 1)].T
        idcol[...] = jnp.full(idcol.shape, NO_ID, F32)
        for m in range(PLANES):
            idcol[RP * m : RP * m + rows, :] = cs[pl.ds(m, rows, stride=PLANES), :]
        cols = idcol[...]
        high = jnp.floor(cols * (1.0 / 128.0))
        idc[:, 0:8] = (cols - 128.0 * high).astype(BF16)
        idc[:, 8:16] = high.astype(BF16)
        rows_out[...] = jnp.zeros(rows_out.shape, F32)
        for i in range(long // 128):
            flipped = idcol[128 * i : 128 * (i + 1), :].T
            for k in range(seqs):
                rows_out[k, 0:1, 128 * i : 128 * (i + 1)] = flipped[k : k + 1, :]
        load_table(table_ref, mine, tail_half, tab, chans)
        load_table(table_ref, slice(None), tail, tab_all, table_ref.shape[1])
        scores = score_ref[...]
        mixed = jnp.concatenate([convw_ref[k : k + 1, :] * scores for k in range(4)], axis=0)
        mixed = jnp.concatenate(list(split3(mixed)) + [jnp.zeros(mixed.shape, BF16)], axis=0)
        got = dot(tab_all[...], mixed, NT)
        got = got + pltpu.roll(got, 96, 1) + pltpu.roll(got, 64, 1)
        for k, part in enumerate(split3(got[:, :32])):
            looks[k] = part
        conv_half[...] = convw_ref[:, mine]
        turned[...] = jnp.zeros(turned.shape, F32)
        cotf[...] = jnp.zeros(cotf.shape, F32)
        for emb, _ in slots:
            emb[long:, :] = jnp.zeros((emb.shape[0] - long, emb.shape[1]), F32)
        look_up(0, slots[0])
        send(0, 0).start()

    for u in range(2):
        q = 2 * n + u
        later = q + 1
        within = jnp.minimum(later, seqs - 1)

        @pl.when(later >= 2)
        def _():
            send(0, 1 - u).wait()

        @pl.when(q >= 2)
        def _():
            send_conv(0, u).wait()

        look_up(within, slots[1 - u])
        convolve(q, u)
        send_conv(q, u).start()

        @pl.when(later < seqs)
        def _():
            send(within, 1 - u).start()

    @pl.when(n == pl.num_programs(0) - 1)
    def _():
        send(0, 1).wait()
        for k in range(2):
            send_conv(0, k).wait()


def score_kernel(len_ref, lang_ref, look_ref, convw_ref, score_ref, prob_out, coef_out):
    bias = jnp.sum(convw_ref[4:5, :] * score_ref[...], axis=1, keepdims=True)
    bias = jnp.broadcast_to(bias, (score_ref.shape[0], 128))
    for q in range(look_ref.shape[0]):
        look = [look_ref[q, 8 * m : 8 * m + 8, :] for m in range(PLANES)]
        ahead = {m: before_lane(look[m]) for m in (9, 10, 11)}
        live = live_planes(len_ref[q])
        inverse = inverse_counts(live)
        base = pick_row(bias, lang_ref[q])
        score = []
        for m in range(PLANES):
            value = base
            for k in range(4):
                x = look[m - k] if m >= k else ahead[m - k + PLANES]
                value = value + x[k : k + 1, :]
            score.append(jnp.where(live[m] > 0, value, 0.0))
        means = [[t * c for t, c in zip(side, inv)] for side, inv in zip(blocks(score), inverse)]
        weights = [[], [], [], []]
        for m in range(PLANES):
            own = [means[b][m // (b + 1)] for b in range(4)]
            top = functools.reduce(jnp.maximum, own)
            grown = [jnp.exp(x - top) for x in own]
            scale = 1.0 / functools.reduce(jnp.add, grown)
            for b in range(4):
                prob = grown[b] * scale
                prob_out[q, PLANES * b + m : PLANES * b + m + 1, :] = prob
                weights[b].append(0.5 * live[m] * prob * inverse[b][m // (b + 1)])
        coef_out[q, 24:32, :] = jnp.zeros((8, 128), F32)
        for k, row in enumerate(coefficients(weights)):
            coef_out[q, k : k + 1, :] = row


def spread_masks(keep_ref):
    lane = iota((16, 128), 1)
    for j in range(keep_ref.shape[0]):
        keep_ref[j] = jnp.where(lane % 64 == j, 1.0, 0.0).astype(BF16)


def spread_columns(both, keep_ref, cols_ref, columns):
    count = both.shape[0] // 16
    both = both.reshape(count, 16, 128)
    wide = [(both * keep_ref[j][None]).reshape(16 * count, 128) for j in columns]
    got = dot(jnp.concatenate(wide, axis=0), jnp.ones((128, 128), BF16))
    for k, j in enumerate(columns):
        cols_ref[j] = got[16 * count * k : 16 * count * (k + 1)]


def pooled_kernel(first, *refs):
    if first:
        refs = refs[1:]
    coef_ref, conv_ref, pooled_out, cols, conv, poolf, low, keep, both, sems = refs
    padded, chans = conv_ref.shape[2:]
    rows = pooled_out.shape[2]
    chunks = chans // 128
    fetches = []
    for u in range(2):
        for c in range(chunks):
            source = conv_ref.at[first + u, :, :, pl.ds(128 * c, 128)]
            fetches.append(pltpu.make_async_copy(source, conv.at[u, c], sems.at[chunks * u + c]))
            fetches[-1].start()
    sends = []
    spread_masks(keep)
    both[...] = jnp.zeros(both.shape, F32)
    for u in range(2):
        high = coef_ref[first + u].astype(BF16).astype(F32)
        both[0:32, :] = high
        both[64:96, :] = coef_ref[first + u] - high
        across = both[...].T[:RP].astype(BF16)
        for k in range(0, 26, 13):
            spread_columns(across, keep, cols, range(k, k + 13))
        for c in range(chunks):
            fetches[chunks * u + c].wait()
            for r in range(0, padded, 8):
                pooled = [0.0] * 6
                for k, p, x in pair_terms(blocks([conv[u, c, m, r : r + 8, :] for m in range(PLANES)])):
                    pooled[p] = pooled[p] + cols[k, r : r + 8, :] * x
                for p in range(6):
                    poolf[p, r : r + 8, :] = pooled[p]
            for p in range(6):
                low[u, p, :, 128 * c : 128 * (c + 1)] = poolf[p, :rows, :].astype(BF16)
        sends.append(pltpu.make_async_copy(low.at[u], pooled_out.at[first + u], sems.at[2 * chunks + u]))
        sends[-1].start()
    for copy in sends:
        copy.wait()


def backward_kernel(
    half_ref, len_ref, lang_ref, core_ref, rows_ref, cot_ref, table_ref, convw_ref, score_ref,
    emb_ref, prob_ref, coef_ref, inner_ref, other_ref,
    keep_out, send_out,
    tail, tab, pulls, mixed, grad, hist, acc, taps_acc, flat, conv_half, score_half, cotf,
    gemb_a, gemb_b, low_a, low_b, cols_a, cols_b, turned_a, turned_b, total_a, total_b, wholes_a, wholes_b, hots,
    keep, sems,
):
    n = pl.program_id(0)
    seqs = len_ref.shape[0]
    rows, chans = cot_ref.shape[2:]
    groups = score_ref.shape[0]
    mine = half_lanes(half_ref, chans)
    padded = (rows + 7) // 8 * 8
    gembs, lows, wholes = (gemb_a, gemb_b), (low_a, low_b), (wholes_a, wholes_b)
    ready = ((cols_a, turned_a, total_a), (cols_b, turned_b, total_b))

    def fetch(q, k):
        return pltpu.make_async_copy(emb_ref.at[q], lows[k], sems.at[k])

    def to_table(q, k):
        sub = iota((VP, PLANES * RP), 0).astype(F32)
        hots[...] = jnp.where(rows_ref[q, 0:1, :] == sub, 1.0, 0.0).astype(BF16)
        acc[:, :256] += dot(hots[...], gembs[k][:, :256])
        yield
        got = dot(hots[...], gembs[k][:, 256:])
        acc[:, 256:] += got[:, : chans - 256]
        hist[:VP, :] = got[:, chans - 256 :]
        yield
        counts = hist[...].T
        counts = counts[0:8] + counts[64:72]
        counts = jnp.concatenate([counts, jnp.zeros((8, 384), F32)], axis=0)
        from_table = dot(jnp.concatenate(split3(counts), axis=0), tab[...])
        from_table = from_table[:16] + from_table[16:32] + from_table[32:]
        part = conv_half[4:5, :] * wholes[k][0:1, :]
        for j in range(4):
            part = part + conv_half[j : j + 1, :] * from_table[j : j + 1, :]
        acc[VP - groups : VP, :] += jnp.where(iota((groups, chans), 0) == lang_ref[q], part, 0.0)
        yield

    def prepare(q, k):
        cols, turned, total = ready[k]
        both = inner_ref[q] + other_ref[q]
        live = live_planes(len_ref[q])
        inverse = inverse_counts(live)
        row = lambda j: both[j : j + 1, :]
        pull = [[], [], [], []]
        for m in range(PLANES):
            p = m // 2
            dots = [row(m), row(2 * p) + row(2 * p + 1), row(THIRD[m]), row(12 + p)]
            prob = [prob_ref[q, PLANES * b + m : PLANES * b + m + 1, :] for b in range(4)]
            inv = [inverse[b][m // (b + 1)] for b in range(4)]
            inner = [0.5 * jnp.where(live[m] > 0, d, 0.0) * c for d, c in zip(dots, inv)]
            mean = functools.reduce(jnp.add, [x * y for x, y in zip(prob, inner)])
            for b in range(4):
                pull[b].append(prob[b] * (inner[b] - mean) * inv[b])
            if m in (2, 5, 8):
                yield
        sums = [blocks(pull[b])[b] for b in range(4)]
        pull = [live[m] * (sums[0][m] + sums[1][m // 2] + sums[2][m // 3] + sums[3][m // 4]) for m in range(PLANES)]
        whole = jnp.sum(functools.reduce(jnp.add, pull), axis=1, keepdims=True)
        total[...] = jnp.broadcast_to(whole, total.shape)
        high = coef_ref[q].astype(BF16).astype(F32)
        mixed[0:32, :] = high
        mixed[64:96, :] = coef_ref[q] - high
        for m, x in enumerate(pull + [after_lane(x) for x in pull[:3]]):
            high = x.astype(BF16).astype(F32)
            pulls[m : m + 1, :] = high
            pulls[64 + m : 65 + m, :] = x - high
            if m < PLANES:
                mixed[32 + m : 33 + m, :] = high
                mixed[96 + m : 97 + m, :] = x - high
        yield
        turned[...] = pulls[...].T
        coef = mixed[...].T[:RP].astype(BF16)
        yield
        columns = [*range(26), *range(32, 44)]
        for k in range(0, len(columns), 5):
            spread_columns(coef, keep, cols, columns[k : k + 5])
            yield
        while True:
            yield

    def gradients(q, u, table, coming):
        cols, turned, total = ready[u]
        gemb, low = gembs[u], lows[u]
        wholes[u][...] = total[...]
        length = len_ref[q]
        for m in range(PLANES):
            x = turned[...] if m == 0 else pltpu.roll(turned[...], 128 - m, 1)
            gemb[RP * m : RP * (m + 1), chans:] = x[:RP].astype(BF16)
        score = pick_row(score_half[...], lang_ref[q])
        for p in range(6):
            cotf[p, :rows, :] = cot_ref[u, p].astype(F32)
        place = PLANES * iota((8, 128), 0)
        for r in range(0, rows, 8):
            if r == 8:
                next(table)
            alive = [place < length - (m + PLANES * r) for m in range(PLANES)]
            for c in range(chans // 128):
                lanes = slice(128 * c, 128 * (c + 1))
                cot = [cotf[p, r : r + 8, lanes] for p in range(6)]
                times = lambda j, p: cols[j, r : r + 8, :] * cot[p]
                four = [times(12 + 2 * j, 2 * j) + times(13 + 2 * j, 2 * j + 1) for j in range(3)]
                three = []
                for h in range(2):
                    three.append(times(18 + 4 * h, 3 * h) + times(19 + 4 * h, 3 * h + 1))
                    three.append(times(20 + 4 * h, 3 * h + 1) + times(21 + 4 * h, 3 * h + 2))
                for m in range(PLANES):
                    value = times(m, m // 2) + four[m // 4] + three[m // 3]
                    value = value + cols[32 + m, r : r + 8, :] * score[:, lanes]
                    grad[c, RP * m + r : RP * m + r + 8, :] = jnp.where(alive[m], value, 0.0)
        @pl.when(length > 0)
        def _():
            for c in range(chans // 128):
                lanes = slice(128 * c, 128 * (c + 1))
                w = [conv_half[k : k + 1, lanes] for k in range(4)]
                tap = [0.0] * 5
                for r in range(0, padded, 16):
                    count = min(16, padded - r)
                    if r == 16 and c < 2:
                        next(table)
                    next(coming)
                    g = [grad[c, RP * m + r : RP * m + r + count, :] for m in range(PLANES)]
                    g += [grad[c, RP * m + r + 1 : RP * m + r + 1 + count, :] for m in range(3)]
                    fold = lambda x: x[:8] + x[8:] if count == 16 else x
                    for m in range(PLANES):
                        back = w[0] * g[m] + w[1] * g[m + 1] + w[2] * g[m + 2] + w[3] * g[m + 3]
                        if count < 16:
                            back = jnp.concatenate([back, jnp.zeros((16 - count, 128), F32)], axis=0)
                        gemb[RP * m + r : RP * m + r + 16, lanes] = back.astype(BF16)
                        e = low[RP * m + r : RP * m + r + 16, lanes].astype(F32)[:count]
                        for k in range(4):
                            tap[k] = tap[k] + fold(e * g[m + k])
                        tap[4] = tap[4] + fold(g[m])
                for k in range(5):
                    taps_acc[k, :, lanes] += tap[k]

    @pl.when(n == 0)
    def _():
        fetch(0, 0).start()
        load_table(table_ref, mine, tail, tab, chans)
        for k in range(2):
            gembs[k][...] = jnp.zeros(gembs[k].shape, BF16)
            wholes[k][...] = jnp.zeros(wholes[k].shape, F32)
        cotf[...] = jnp.zeros(cotf.shape, F32)
        pulls[...] = jnp.zeros(pulls.shape, F32)
        mixed[...] = jnp.zeros(mixed.shape, F32)
        for m in range(PLANES):
            grad[:, RP * m + rows : RP * (m + 1), :] = jnp.zeros((chans // 128, RP - rows, 128), F32)
        grad[:, PLANES * RP :, :] = jnp.zeros((chans // 128, 8, 128), F32)
        acc[...] = jnp.zeros(acc.shape, F32)
        taps_acc[...] = jnp.zeros(taps_acc.shape, F32)
        hist[...] = jnp.zeros(hist.shape, F32)
        conv_half[...] = convw_ref[:, mine]
        score_half[...] = score_ref[:, mine]
        spread_masks(keep)
        first = prepare(0, 0)
        for _ in range(30):
            next(first)

    for u in range(2):
        q = 2 * n + u
        later = jnp.minimum(q + 1, seqs - 1)
        fetch(q, u).wait()

        @pl.when(q + 1 < seqs)
        def _():
            fetch(later, 1 - u).start()

        gradients(q, u, to_table(jnp.maximum(q - 1, 0), 1 - u), prepare(later, 1 - u))

    @pl.when(n == pl.num_programs(0) - 1)
    def _():
        for _ in to_table(seqs - 1, 1):
            pass
        for k in range(5):
            at = VP - groups - 5 + k
            acc[at : at + 1, :] = jnp.sum(taps_acc[k], axis=0, keepdims=True)
        flat[VP * (chans // 128) :, :] = jnp.zeros((flat.shape[0] - VP * (chans // 128), 128), F32)
        for k in range(chans // 128):
            flat[VP * k : VP * (k + 1), :] = acc[:, 128 * k : 128 * (k + 1)]
        part = keep_out.shape[0]
        own = pl.multiple_of(core_ref[0] * part, 8)
        theirs = pl.multiple_of((1 - core_ref[0]) * part, 8)
        keep_out[...] = flat[pl.ds(own, part), :]
        send_out[...] = flat[pl.ds(theirs, part), :]


def adamw(weight, grad, moment, second, rate):
    new_m = 0.9 * moment + 0.1 * grad
    new_v = 0.999 * second + 0.001 * grad * grad
    m_hat = new_m / (1.0 - 0.9**STEP_NUMBER)
    v_hat = new_v / (1.0 - 0.999**STEP_NUMBER)
    new_w = weight - rate * (m_hat / (jnp.sqrt(v_hat) + 1e-08) + 0.01 * weight)
    return new_m, new_v, new_w


def update_kernel(half_ref, place_ref, owner_ref, mine_ref, other_ref, *refs):
    ins, outs, flat = refs[:9], refs[9:18], refs[18]
    core, seq = place_ref[0], place_ref[3]
    rows = mine_ref.shape[0] // 2
    for side, near, ref in ((core, place_ref[1], mine_ref), (1 - core, place_ref[2], other_ref)):
        for k in range(2):
            piece = near if k == 0 else 1 - near
            flat[pl.ds(pl.multiple_of((2 * side + piece) * rows, 8), rows), :] = ref[k * rows : (k + 1) * rows, :]
    vocab, chans = ins[1].shape
    groups = ins[6].shape[0]
    spans = ((0, vocab), (VP - groups - 5, 5), (VP - groups, groups))
    for t, rate in enumerate((0.5, 0.3, 0.05)):
        first, count = spans[t]
        owned = owner_ref[t] == seq
        for k in range(chans // 128):
            lanes = slice(128 * k, 128 * (k + 1))
            weight = ins[3 * t][:, pl.ds(pl.multiple_of(half_ref[0] * chans + 128 * k, 128), 128)]
            grad = flat[VP * k + first : VP * k + first + count, :]
            new = adamw(weight, grad, ins[3 * t + 1][:, lanes], ins[3 * t + 2][:, lanes], rate)
            for q in range(3):
                out = outs[3 * t + q]
                value = jnp.where(owned, new[q], 0.0)
                if count == groups:
                    out[0, :, lanes] = value
                else:
                    out[:, 0, lanes] = value


def local(
    seq_size, byte_ids, lengths, lang_ids, owners, table, conv_w, score_w, cotangent,
    table_m, table_v, conv_m, conv_v, score_m, score_v,
):
    seqs, slot = byte_ids.shape
    vocab, full = table.shape
    half_rows, chans = cotangent.shape[1:]
    groups = score_w.shape[0]
    rows = slot // PLANES
    assert rows * PLANES == slot and rows <= RP - 2 and seqs % 2 == 0
    half = lax.axis_index("blk").astype(jnp.int32).reshape(1)
    seq = lax.axis_index("seq").astype(jnp.int32)
    core, far_bit, near_bit = seq % 2, (seq // 4) % 2, (seq // 2) % 2
    near = jnp.where(core == 0, far_bit, near_bit)
    near_other = jnp.where(core == 0, near_bit, far_bit)
    vmem = pltpu.VMEM
    shape = jax.ShapeDtypeStruct
    whole = lambda *dims: pl.BlockSpec(dims, lambda s, *_: (0,) * len(dims))
    by_two = lambda *dims: pl.BlockSpec((2,) + dims, lambda s, *_: (s,) + (0,) * len(dims))
    by_seq = lambda *dims: pl.BlockSpec((1,) + dims, lambda s, *_: (s,) + (0,) * len(dims))

    def call(kernel, name, scalars, arrays, in_specs, outs, out_specs, scratch, mib, steps):
        return pl.pallas_call(
            kernel,
            grid_spec=pltpu.PrefetchScalarGridSpec(
                num_scalar_prefetch=len(scalars), grid=(steps,),
                in_specs=in_specs, out_specs=out_specs, scratch_shapes=scratch,
            ),
            out_shape=outs,
            compiler_params=pltpu.CompilerParams(
                vmem_limit_bytes=mib * 1024 * 1024, dimension_semantics=("arbitrary",)
            ),
            name=name,
        )(*scalars, *arrays)

    planes = cotangent.reshape(seqs, rows, 6, chans).transpose(0, 2, 1, 3)
    long = PLANES * RP
    padded = (rows + 7) // 8 * 8
    emb, conv, look, inner, id_rows = call(
        forward_kernel, "forward",
        [half, lengths, lang_ids], [byte_ids, planes, table, conv_w, score_w],
        [whole(seqs, slot), by_two(6, rows, chans), whole(vocab, full), whole(5, full), whole(groups, full)],
        [
            pltpu.HBM((seqs, long, chans), BF16), pltpu.HBM((seqs, PLANES, padded, chans), F32),
            shape((seqs, 8 * PLANES, 128), F32),
            shape((seqs, 32, 128), F32), shape((seqs, 8, long), F32),
        ],
        [
            pl.BlockSpec(memory_space=pltpu.HBM), pl.BlockSpec(memory_space=pltpu.HBM),
            whole(seqs, 8 * PLANES, 128), whole(seqs, 32, 128), whole(seqs, 8, long),
        ],
        [
            vmem((8, long), F32), vmem((long, 8), F32), vmem((long, 8), F32), vmem((long, 16), BF16),
            vmem((128, full), F32), vmem((384, full), BF16), vmem((3, 384, 32), BF16),
            vmem((128, chans), F32), vmem((384, chans + 128), BF16),
            vmem((long + 32, chans + 128), F32), vmem((long + 32, chans + 128), F32),
            vmem((long, chans), BF16), vmem((long, chans), BF16),
            vmem((5, chans), F32), vmem((6, RP, chans), F32), vmem((128, 128), F32), vmem((long, 384), BF16),
            vmem((PLANES, padded, chans), F32), vmem((PLANES, padded, chans), F32), pltpu.SemaphoreType.DMA((4,)),
        ],
        FORWARD_MIB, seqs // 2,
    )
    emb = pltpu.with_memory_space_constraint(emb, pltpu.HBM)
    other = lax.ppermute(inner, "blk", [(0, 1), (1, 0)])
    prob, coef = call(
        score_kernel, "scores",
        [lengths, lang_ids], [look, conv_w, score_w],
        [whole(seqs, 8 * PLANES, 128), whole(5, full), whole(groups, full)],
        [shape((seqs, 48, 128), F32), shape((seqs, 32, 128), F32)],
        [whole(seqs, 48, 128), whole(seqs, 32, 128)], [], 16, 1,
    )
    other, prob, coef = lax.optimization_barrier((other, prob, coef))
    total = -(-VP * (chans // 128) // 32) * 32
    keep, send = call(
        backward_kernel, "backward",
        [half, lengths, lang_ids, core.reshape(1)],
        [id_rows, planes, table, conv_w, score_w, emb, prob, coef, inner, other],
        [
            whole(seqs, 8, long), by_two(6, rows, chans), whole(vocab, full), whole(5, full), whole(groups, full),
            pl.BlockSpec(memory_space=pltpu.HBM), whole(seqs, 48, 128), whole(seqs, 32, 128),
            whole(seqs, 32, 128), whole(seqs, 32, 128),
        ],
        [shape((total // 2, 128), F32)] * 2,
        [whole(total // 2, 128)] * 2,
        [
            vmem((128, chans), F32), vmem((384, chans), BF16), vmem((128, 128), F32), vmem((128, 128), F32),
            vmem((chans // 128, long + 8, 128), F32), vmem((384, 128), F32), vmem((VP, chans), F32),
            vmem((5, 8, chans), F32), vmem((total, 128), F32), vmem((5, chans), F32), vmem((groups, chans), F32),
            vmem((6, RP, chans), F32),
            vmem((long, chans + 128), BF16), vmem((long, chans + 128), BF16),
            vmem((long, chans), BF16), vmem((long, chans), BF16),
            vmem((44, RP, 128), F32), vmem((44, RP, 128), F32),
            vmem((128, 128), F32), vmem((128, 128), F32), vmem((8, chans), F32), vmem((8, chans), F32),
            vmem((8, chans), F32), vmem((8, chans), F32), vmem((VP, long), BF16),
            vmem((44, 16, 128), BF16), pltpu.SemaphoreType.DMA((2,)),
        ],
        BACKWARD_MIB, seqs // 2,
    )

    def swap(x, step, odd_step):
        return lax.ppermute(x, "seq", [(i, i ^ (odd_step if i % 2 else step)) for i in range(seq_size)])

    def pooled_two(first, before):
        held = [] if first == 0 else [before]
        return pl.pallas_call(
            functools.partial(pooled_kernel, first),
            in_specs=[pl.BlockSpec(memory_space=pltpu.HBM)] * len(held)
            + [pl.BlockSpec(memory_space=pltpu.VMEM), pl.BlockSpec(memory_space=pltpu.HBM)],
            out_specs=pl.BlockSpec(memory_space=pltpu.HBM),
            scratch_shapes=[
                vmem((26, RP, 128), F32), vmem((2, chans // 128, PLANES, padded, 128), F32),
                vmem((6, padded, 128), F32), vmem((2, 6, rows, chans), BF16),
                vmem((32, 16, 128), BF16), vmem((128, 128), F32),
                pltpu.SemaphoreType.DMA((2 * (chans // 128) + 2,)),
            ],
            out_shape=pltpu.HBM((seqs, 6, rows, chans), BF16),
            input_output_aliases={0: 0} if held else {},
            compiler_params=pltpu.CompilerParams(vmem_limit_bytes=POOLED_MIB * 1024 * 1024),
            name="pooled",
        )(*held, coef, pltpu.with_memory_space_constraint(conv, pltpu.HBM))

    keep, conv = lax.optimization_barrier((keep, conv))
    mine = keep + swap(send, 1, 1)
    quarter = total // 4
    held = lax.dynamic_slice_in_dim(mine, near * quarter, quarter, 0)
    sent = lax.dynamic_slice_in_dim(mine, (1 - near) * quarter, quarter, 0)
    pooled = pooled_two(0, None)
    got, pooled = lax.optimization_barrier((swap(sent, 4, 2), pooled))
    held = held + got
    even, odd = [2, 8], [8, 4]
    step = 16
    while step < seq_size:
        even, odd, step = even + [step], odd + [step], step * 2
    for k, (step, odd_step) in enumerate(zip(even, odd)):
        got = swap(held, step, odd_step)
        if k == 0:
            for first in range(2, seqs, 2):
                pooled = pooled_two(first, pooled)
        elif k == 1:
            pooled = pooled.transpose(0, 2, 1, 3).reshape(seqs, half_rows, chans)
        if k < 2:
            got, pooled = lax.optimization_barrier((got, pooled))
        held = held + got
    mine = jnp.concatenate([held, swap(held, 4, 2)], axis=0)
    other = swap(mine, 1, 1)

    place = jnp.stack([core, near, near_other, seq])
    arrays = [mine, other, table, table_m, table_v, conv_w, conv_m, conv_v, score_w, score_m, score_v]
    outs = []
    for count in (vocab, 5):
        outs += [shape((count, 1, chans), F32)] * 3
    outs += [shape((1, groups, chans), F32)] * 3
    updated = call(
        update_kernel, "update",
        [half, place, owners], arrays, [whole(*x.shape) for x in arrays],
        outs, [whole(*x.shape) for x in outs], [vmem((total, 128), F32)], UPDATE_MIB, 1,
    )
    updated = [jnp.transpose(x, (1, 0, 2)) if k < 6 else x for k, x in enumerate(updated)]
    return (pooled, *updated)


def solution(mesh):
    row, split, copied = P("seq"), P(None, "blk"), P()
    return jax.shard_map(
        functools.partial(local, mesh.shape["seq"]),
        mesh=mesh,
        in_specs=(P("seq", None), row, row, copied, copied, copied, copied, P("seq", None, "blk"))
        + (split,) * 6,
        out_specs=(P("seq", None, "blk"),) * 10,
        check_vma=False,
    )
```

time: 61.1 us -> 57.9 us (0.948)
  waiting for transfers between devices: 14.5 us -> 6.88 us
  Pallas kernels: 28.9 us -> 32.9 us
    ppermute x6, waiting for transfers between devices: 12.2 us -> 5.63 us  [swap(): lax.ppermute(x, 'seq', [(i, i ^ (odd_step if i % 2 else step)) for i in r...]
    pallas_call x0 -> x2, Pallas kernels: none -> 5.98 us  [pooled_two(): pl.pallas_call(functools.partial(pooled_kernel, first), in_specs=[pl.Bloc...]
    pallas_call x3 -> x4, Pallas kernels: 28.9 us -> 26.9 us  [call(): pl.pallas_call(kernel, grid_spec=pltpu.PrefetchScalarGridSpec(num_scalar_...]
    ppermute x1, waiting for transfers between devices: 2.24 us -> 1.25 us  [local(): other = lax.ppermute(inner, 'blk', [(0, 1), (1, 0)])]
  transfers between devices with their start and end apart: 7 -> 7, of which waited for: 6 -> 4; matrix products, arithmetic and copies ran while one was open for 5% -> 6% of each run, Pallas kernels for 0% -> 12%
where the time goes in v3:
time: 57.9 us; the launch traced here: 57.6 us
  Pallas kernels  32.9 us (57%)
  starting transfers between devices  11.7 us (20%)
  waiting for transfers between devices  6.88 us (12%)
  local copies, waits for them, and re-layouts  5.02 us (9%)
  between operations  0.99 us (2%)
    pallas_call x4, Pallas kernels, call(): pl.pallas_call(kernel, grid_spec=pltpu.PrefetchScalarGridSpec(num_scalar_...  26.9 us
    ppermute x6, starting transfers between devices, swap(): lax.ppermute(x, 'seq', [(i, i ^ (odd_step if i % 2 else step)) for i in r...  8.73 us
    pallas_call x2, Pallas kernels, pooled_two(): pl.pallas_call(functools.partial(pooled_kernel, first), in_specs=[pl.Bloc...  5.98 us
    ppermute x6, waiting for transfers between devices, swap(): lax.ppermute(x, 'seq', [(i, i ^ (odd_step if i % 2 else step)) for i in r...  5.63 us
    transpose x1, local copies, waits for them, and re-layouts, local(): pooled = pooled.transpose(0, 2, 1, 3).reshape(seqs, half_rows, chans)  3.25 us
    ppermute x1, starting transfers between devices, local(): other = lax.ppermute(inner, 'blk', [(0, 1), (1, 0)])  3.01 us
    reshape x1, local copies, waits for them, and re-layouts, local(): planes = cotangent.reshape(seqs, rows, 6, chans).transpose(0, 2, 1, 3)  1.69 us
    ppermute x1, waiting for transfers between devices, local(): other = lax.ppermute(inner, 'blk', [(0, 1), (1, 0)])  1.25 us
  transfers between devices with their start and end apart: 7, of which 4 were waited for; matrix products, arithmetic and copies ran while one was open for 6% of the time, Pallas kernels for 12%

profile of v3, /device:TPU:0, one launch (start us, length us, event | category | flops | bytes accessed | tf_op | source)
XLA Modules:
  0.0 57.6 jit_solution(7883725807060941681)
XLA Ops:
  0.6 0.0 copy-start.4
  0.7 0.0 copy-start.3
  0.7 0.0 copy-start
  0.7 0.0 copy-start.11
  0.7 0.0 copy-start.10
  0.7 1.7 %copy.28 = bf16[4,86,6,384]{3,1,2,0:T(8,128)(2,1)S(1)} copy(bf16[4,86,6,384]{3,0,2,1:T(4,128)(2,1)} %bitcast.20) | data formatting | bytes 3170304 | tf_op jit(solution)/shard_map/reshape | solution.py:586
  2.5 10.9 %forward.1 = (bf16[4,1152,384]{2,1,0:T(8,128)(2,1)}, f32[4,12,88,384]{3,2,1,0:T(8,128)}, f32[4,96,128]{2,1,0:T(8,128)S(1)}, f32[4,32,128]{2,1,0:T(8,128)S(1)}, f32[4,8,1152]{2,1,0:T(8,128)S(1)}) custom-call(s32[1]{0:T(128)} %bitcast.half_ref, s32[4]{0:T(128)S(1)} %copy-done.10, s32[4]{0:T(128)S(1)} %copy-done.11, s32[4,1032]{1,0:T(4,128)S(1)} %copy-done.5, ...), custom_call_target="tpu_custom_call" | custom-call | tf_op jit(solution)/shard_map/forward/pallas_call | solution.py:573
  13.4 3.0 %collective-permute-start = (f32[4,32,128]{2,1,0:T(8,128)S(1)}, f32[4,32,128]{2,1,0:T(8,128)S(1)}, u32[]{:S(2)}, u32[]{:S(2)}) collective-permute-start(f32[4,32,128]{2,1,0:T(8,128)S(1)} %get-tuple-element.41.inner_ref), channel_id=1, source_target_pairs={{0,16},{16,0},{1,17},{17,1},{2,18},{18,2},{3,19},{19,3},{4,20},{20... | collective-permute-start | bytes 196616 | tf_op jit(solution)/shard_map/ppermute | solution.py:614
  16.4 1.0 %scores.1 = (f32[4,48,128]{2,1,0:T(8,128)S(1)}, f32[4,32,128]{2,1,0:T(8,128)S(1)}) custom-call(s32[4]{0:T(128)S(1)} %copy-done.10, s32[4]{0:T(128)S(1)} %copy-done.11, f32[4,96,128]{2,1,0:T(8,128)S(1)} %get-tuple-element.42.look_ref, f32[5,768]{1,0:T(8,128)S(1)} %copy-done.3, f32[8,768]{1,0:T(8,128)S(1)} %copy-done.4), custom_call_target="tpu_custom_call" | custom-call | tf_op jit(solution)/shard_map/scores/pallas_call | solution.py:573
  17.4 1.3 %collective-permute-done.other_ref = f32[4,32,128]{2,1,0:T(8,128)S(1)} collective-permute-done((f32[4,32,128]{2,1,0:T(8,128)S(1)}, f32[4,32,128]{2,1,0:T(8,128)S(1)}, u32[]{:S(2)}, u32[]{:S(2)}) %collective-permute-start) | collective-permute-done | bytes 65568 | tf_op jit(solution)/shard_map/ppermute | solution.py:614
  18.7 12.3 %backward.1 = (f32[416,128]{1,0:T(8,128)S(1)}, f32[416,128]{1,0:T(8,128)S(1)}) custom-call(s32[1]{0:T(128)} %bitcast.half_ref, s32[4]{0:T(128)S(1)} %copy-done.10, s32[4]{0:T(128)S(1)} %copy-done.11, s32[1]{0:T(128)} %bitcast.1.core_ref, f32[4,8,1152]{2,1,0:T(8,128)S(1)} %get-tuple-element.39.rows_ref, bf16[4,6,86,384]{3,2,1,0:T(8,128)(2,1)S(1)} %bitcast.18, ...), custom_call_target="tpu_custom_call" | custom-call | tf_op jit(solution)/shard_map/backward/pallas_call | solution.py:573
  31.0 0.1 collective-permute-start.1
  31.2 1.4 %collective-permute-done.1 = f32[416,128]{1,0:T(8,128)S(1)} collective-permute-done((f32[416,128]{1,0:T(8,128)S(1)}, f32[416,128]{1,0:T(8,128)S(1)}, u32[]{:S(2)}, u32[]{:S(2)}) %collective-permute-start.1) | collective-permute-done | bytes 213024 | tf_op jit(solution)/shard_map/ppermute | solution.py:651
  32.6 2.2 %collective-permute-start.2 = (f32[208,128]{1,0:T(8,128)S(1)}, f32[208,128]{1,0:T(8,128)S(1)}, u32[]{:S(2)}, u32[]{:S(2)}) collective-permute-start(f32[208,128]{1,0:T(8,128)S(1)} %constant_dynamic-slice_fusion), channel_id=1, source_target_pairs={{0,4},{1,3},{2,6},{3,1},{4,0},{5,7},{6,2},{7,5},{8,12},{9,11},{10,... | collective-permute-start | bytes 319496 | tf_op jit(solution)/shard_map/ppermute | solution.py:651
  34.8 3.0 %pooled.2.refs_0_ = bf16[4,6,86,384]{3,2,1,0:T(8,128)(2,1)} custom-call(f32[4,32,128]{2,1,0:T(8,128)S(1)} %get-tuple-element.46.coef_ref.refs_0_.refs_1_, f32[4,12,88,384]{3,2,1,0:T(8,128)} %get-tuple-element.52.refs_1_.refs_2_), custom_call_target="tpu_custom_call" | custom-call | tf_op jit(solution)/shard_map/pooled/pallas_call | solution.py:655
  37.7 0.0 collective-permute-done.2
  37.8 1.7 %collective-permute-start.3 = (f32[208,128]{1,0:T(8,128)S(1)}, f32[208,128]{1,0:T(8,128)S(1)}, u32[]{:S(2)}, u32[]{:S(2)}) collective-permute-start(f32[208,128]{1,0:T(8,128)S(1)} %dynamic-slice_add_fusion), channel_id=1, source_target_pairs={{0,2},{1,9},{2,0},{3,11},{4,6},{5,13},{6,4},{7,15},{8,10},{9,1},{1... | collective-permute-start | bytes 319496 | tf_op jit(solution)/shard_map/ppermute | solution.py:651
  39.5 3.0 %pooled.3 = bf16[4,6,86,384]{3,2,1,0:T(8,128)(2,1)} custom-call(bf16[4,6,86,384]{3,2,1,0:T(8,128)(2,1)} %pooled.2.refs_0_, f32[4,32,128]{2,1,0:T(8,128)S(1)} %get-tuple-element.46.coef_ref.refs_0_.refs_1_, f32[4,12,88,384]{3,2,1,0:T(8,128)} %get-tuple-element.52.refs_1_.refs_2_), custom_call_target="tpu_custom_call", output_to_operand_aliasing={{}: (0, {})} | custom-call | tf_op jit(solution)/shard_map/pooled/pallas_call | solution.py:655
  42.5 0.0 collective-permute-done.3
  42.6 2.8 %collective-permute-start.4 = (f32[208,128]{1,0:T(8,128)S(1)}, f32[208,128]{1,0:T(8,128)S(1)}, u32[]{:S(2)}, u32[]{:S(2)}) collective-permute-start(f32[208,128]{1,0:T(8,128)S(1)} %add.37), channel_id=1, source_target_pairs={{0,8},{1,5},{2,10},{3,7},{4,12},{5,1},{6,14},{7,3},{8,0},{9,13},{1... | collective-permute-start | bytes 319496 | tf_op jit(solution)/shard_map/ppermute | solution.py:651
  45.4 0.0 copy-start.8
  45.4 0.0 copy-start.9
  45.4 0.0 copy-start.12
  45.4 3.2 %copy.26 = bf16[4,86,6,384]{3,0,2,1:T(4,128)(2,1)} copy(bf16[4,86,6,384]{3,1,2,0:T(8,128)(2,1)} %bitcast.19) | data formatting | bytes 3170304 | tf_op jit(solution)/shard_map/transpose | solution.py:690
  48.6 0.0 collective-permute-done.4
  48.7 1.9 %collective-permute-start.5 = (f32[208,128]{1,0:T(8,128)S(1)}, f32[208,128]{1,0:T(8,128)S(1)}, u32[]{:S(2)}, u32[]{:S(2)}) collective-permute-start(f32[208,128]{1,0:T(8,128)S(1)} %add.38), channel_id=1, source_target_pairs={{0,4},{1,3},{2,6},{3,1},{4,0},{5,7},{6,2},{7,5},{8,12},{9,11},{10,... | collective-permute-start | bytes 319496 | tf_op jit(solution)/shard_map/ppermute | solution.py:651
  50.6 2.8 %collective-permute-done.5 = f32[208,128]{1,0:T(8,128)S(1)} collective-permute-done((f32[208,128]{1,0:T(8,128)S(1)}, f32[208,128]{1,0:T(8,128)S(1)}, u32[]{:S(2)}, u32[]{:S(2)}) %collective-permute-start.5) | collective-permute-done | bytes 106528 | tf_op jit(solution)/shard_map/ppermute | solution.py:651
  53.4 0.1 collective-permute-start.6
  53.5 0.1 pad_add_fusion.place_ref
  53.6 1.4 %collective-permute-done.6.other_ref = f32[416,128]{1,0:T(8,128)S(1)} collective-permute-done((f32[416,128]{1,0:T(8,128)S(1)}, f32[416,128]{1,0:T(8,128)S(1)}, u32[]{:S(2)}, u32[]{:S(2)}) %collective-permute-start.6) | collective-permute-done | bytes 213024 | tf_op jit(solution)/shard_map/ppermute | solution.py:651
  55.0 0.0 copy-done.2
  55.0 2.6 %update.1 = (f32[259,1,384]{2,1,0:T(1,128)}, f32[259,1,384]{2,1,0:T(1,128)}, f32[259,1,384]{2,1,0:T(1,128)}, f32[5,1,384]{2,1,0:T(1,128)}, f32[5,1,384]{2,1,0:T(...) custom-call(s32[1]{0:T(128)} %bitcast.half_ref, ...), custom_call_target="tpu_custom_call" | custom-call | tf_op jit(solution)/shard_map/update/pallas_call | solution.py:573
  (23 shorter events, 0.1 us)
Async XLA Ops:
  0.6 1.8 %copy-start.4 = (f32[8,768]{1,0:T(8,128)S(1)}, f32[8,768]{1,0:T(8,128)}, u32[]{:S(2)}) copy-start(f32[8,768]{1,0:T(8,128)} %refs_6_.1) | copy-start | bytes 73732
  0.7 1.8 %copy-start.3 = (f32[5,768]{1,0:T(8,128)S(1)}, f32[5,768]{1,0:T(8,128)}, u32[]{:S(2)}) copy-start(f32[5,768]{1,0:T(8,128)} %refs_3_.1) | copy-start | bytes 46084
  0.7 1.8 %copy-start = (f32[259,768]{1,0:T(8,128)S(1)}, f32[259,768]{1,0:T(8,128)}, u32[]{:S(2)}) copy-start(f32[259,768]{1,0:T(8,128)} %refs_0_.1) | copy-start | bytes 2386948
  0.7 1.8 %copy-start.11 = (s32[4]{0:T(128)S(1)}, s32[4]{0:T(128)}, u32[]{:S(2)}) copy-start(s32[4]{0:T(128)} %lang_ref.5) | copy-start | bytes 52
  0.7 1.8 %copy-start.10 = (s32[4]{0:T(128)S(1)}, s32[4]{0:T(128)}, u32[]{:S(2)}) copy-start(s32[4]{0:T(128)} %len_ref.5) | copy-start | bytes 52
  0.7 1.8 %copy-start.5 = (s32[4,1032]{1,0:T(4,128)S(1)}, s32[4,1032]{1,0:T(4,128)}, u32[]{:S(2)}) copy-start(s32[4,1032]{1,0:T(4,128)} %ids_ref.1) | copy-start | bytes 49540
  13.4 5.3 %collective-permute-start = (f32[4,32,128]{2,1,0:T(8,128)S(1)}, f32[4,32,128]{2,1,0:T(8,128)S(1)}, u32[]{:S(2)}, u32[]{:S(2)}) collective-permute-start(f32[4,32,128]{2,1,0:T(8,128)S(1)} %get-tuple-element.41.inner_ref), channel_id=1, source_target_pairs={{0,16},{16,0},{1,17},{17,1},{2,18},{18,2},{3,19},{19,3},{4,20},{20... | collective-permute-start | bytes 196616 | tf_op jit(solution)/shard_map/ppermute | solution.py:614
  31.0 1.5 %collective-permute-start.1 = (f32[416,128]{1,0:T(8,128)S(1)}, f32[416,128]{1,0:T(8,128)S(1)}, u32[]{:S(2)}, u32[]{:S(2)}) collective-permute-start(f32[416,128]{1,0:T(8,128)S(1)} %get-tuple-element.51), channel_id=1, source_target_pairs={{0,1},{1,0},{2,3},{3,2},{4,5},{5,4},{6,7},{7,6},{8,9},{9,8},{10,11... | collective-permute-start | bytes 638984 | tf_op jit(solution)/shard_map/ppermute | solution.py:651
  32.6 5.1 %collective-permute-start.2 = (f32[208,128]{1,0:T(8,128)S(1)}, f32[208,128]{1,0:T(8,128)S(1)}, u32[]{:S(2)}, u32[]{:S(2)}) collective-permute-start(f32[208,128]{1,0:T(8,128)S(1)} %constant_dynamic-slice_fusion), channel_id=1, source_target_pairs={{0,4},{1,3},{2,6},{3,1},{4,0},{5,7},{6,2},{7,5},{8,12},{9,11},{10,... | collective-permute-start | bytes 319496 | tf_op jit(solution)/shard_map/ppermute | solution.py:651
  37.8 4.8 %collective-permute-start.3 = (f32[208,128]{1,0:T(8,128)S(1)}, f32[208,128]{1,0:T(8,128)S(1)}, u32[]{:S(2)}, u32[]{:S(2)}) collective-permute-start(f32[208,128]{1,0:T(8,128)S(1)} %dynamic-slice_add_fusion), channel_id=1, source_target_pairs={{0,2},{1,9},{2,0},{3,11},{4,6},{5,13},{6,4},{7,15},{8,10},{9,1},{1... | collective-permute-start | bytes 319496 | tf_op jit(solution)/shard_map/ppermute | solution.py:651
  42.6 6.1 %collective-permute-start.4 = (f32[208,128]{1,0:T(8,128)S(1)}, f32[208,128]{1,0:T(8,128)S(1)}, u32[]{:S(2)}, u32[]{:S(2)}) collective-permute-start(f32[208,128]{1,0:T(8,128)S(1)} %add.37), channel_id=1, source_target_pairs={{0,8},{1,5},{2,10},{3,7},{4,12},{5,1},{6,14},{7,3},{8,0},{9,13},{1... | collective-permute-start | bytes 319496 | tf_op jit(solution)/shard_map/ppermute | solution.py:651
  45.3 9.6 %copy-start.1 = (f32[259,384]{1,0:T(8,128)S(1)}, f32[259,384]{1,0:T(8,128)}, u32[]{:S(2)}) copy-start(f32[259,384]{1,0:T(8,128)} %refs_1_.1) | copy-start | bytes 1193476
  45.3 9.6 %copy-start.2 = (f32[259,384]{1,0:T(8,128)S(1)}, f32[259,384]{1,0:T(8,128)}, u32[]{:S(2)}) copy-start(f32[259,384]{1,0:T(8,128)} %refs_2_.1) | copy-start | bytes 1193476
  45.3 9.6 %copy-start.6 = (f32[5,384]{1,0:T(8,128)S(1)}, f32[5,384]{1,0:T(8,128)}, u32[]{:S(2)}) copy-start(f32[5,384]{1,0:T(8,128)} %refs_4_.1) | copy-start | bytes 23044
  45.3 9.6 %copy-start.7 = (f32[5,384]{1,0:T(8,128)S(1)}, f32[5,384]{1,0:T(8,128)}, u32[]{:S(2)}) copy-start(f32[5,384]{1,0:T(8,128)} %refs_5_.1) | copy-start | bytes 23044
  45.4 9.6 %copy-start.8 = (f32[8,384]{1,0:T(8,128)S(1)}, f32[8,384]{1,0:T(8,128)}, u32[]{:S(2)}) copy-start(f32[8,384]{1,0:T(8,128)} %refs_7_.1) | copy-start | bytes 36868
  45.4 9.6 %copy-start.9 = (f32[8,384]{1,0:T(8,128)S(1)}, f32[8,384]{1,0:T(8,128)}, u32[]{:S(2)}) copy-start(f32[8,384]{1,0:T(8,128)} %refs_8_.1) | copy-start | bytes 36868
  45.4 9.6 %copy-start.12 = (s32[3]{0:T(128)S(1)}, s32[3]{0:T(128)}, u32[]{:S(2)}) copy-start(s32[3]{0:T(128)} %owner_ref.1) | copy-start | bytes 40
  48.7 4.8 %collective-permute-start.5 = (f32[208,128]{1,0:T(8,128)S(1)}, f32[208,128]{1,0:T(8,128)S(1)}, u32[]{:S(2)}, u32[]{:S(2)}) collective-permute-start(f32[208,128]{1,0:T(8,128)S(1)} %add.38), channel_id=1, source_target_pairs={{0,4},{1,3},{2,6},{3,1},{4,0},{5,7},{6,2},{7,5},{8,12},{9,11},{10,... | collective-permute-start | bytes 319496 | tf_op jit(solution)/shard_map/ppermute | solution.py:651
  53.4 1.5 %collective-permute-start.6 = (f32[416,128]{1,0:T(8,128)S(1)}, f32[416,128]{1,0:T(8,128)S(1)}, u32[]{:S(2)}, u32[]{:S(2)}) collective-permute-start(f32[416,128]{1,0:T(8,128)S(1)} %pad_maximum_fusion.mine_ref), channel_id=1, source_target_pairs={{0,1},{1,0},{2,3},{3,2},{4,5},{5,4},{6,7},{7,6},{8,9},{9,8},{10,11... | collective-permute-start | bytes 638984 | tf_op jit(solution)/shard_map/ppermute | solution.py:651

commit v4 on v3

--- a/solution.py
+++ b/solution.py
@@ -108,7 +108,7 @@
 def forward_kernel(
     half_ref, len_ref, lang_ref, ids_ref, cot_ref, table_ref, convw_ref, score_ref,
     emb_out, conv_out, look_out, inner_out, rows_out,
-    xs, cs, idcol, idc, tail, tab_all, looks, tail_half, tab, emb_a, emb_b, low_a, low_b,
+    xs, cs, idcol, tail, tab_all, looks, tail_half, tab, emb_a, emb_b, low_a, low_b, extras,
     conv_half, cotf, turned, hots, conv_a, conv_b, sems,
 ):
     n = pl.program_id(0)
@@ -116,61 +116,57 @@
     rows, chans = cot_ref.shape[2:]
     long = PLANES * RP
     mine = half_lanes(half_ref, chans)
-    slots = ((emb_a, low_a), (emb_b, low_b))
+    embs, lows = (emb_a, emb_b), (low_a, low_b)
     convs = (conv_a, conv_b)
 
     def send(q, k):
-        return pltpu.make_async_copy(slots[k][1], emb_out.at[q], sems.at[k])
+        return pltpu.make_async_copy(lows[k], emb_out.at[q], sems.at[k])
 
     def send_conv(q, k):
         return pltpu.make_async_copy(convs[k], conv_out.at[q], sems.at[2 + k])
 
-    def look_up(q, slot_refs):
-        emb, low = slot_refs
-        lang = lang_ref[q]
-        sub, lane = iota((32, 128), 0), iota((32, 128), 1)
-        here = (sub % 8 == lang) & (lane % 8 == sub // 8)
-        extra = 0.0
-        for k in range(3):
-            extra = extra + dot(looks[k], jnp.where(here & (lane // 8 == k), 1.0, 0.0).astype(BF16))
-        tab[:, chans:] = extra.astype(BF16)
-        sub = iota((16, 128), 0)
-        spread = jnp.where(sub == q, 1.0, jnp.where(sub == q + 8, 128.0, 0.0)).astype(BF16)
-        ids = dot(idc[...], spread)
-        lane = iota((long, 128), 1).astype(F32)
-        for k in range(3):
-            hots[:, 128 * k : 128 * (k + 1)] = jnp.where(ids == lane + 128.0 * k, 1.0, 0.0).astype(BF16)
+    def look_up(q, u):
+        emb = embs[u]
+        tab[:, chans:] = extras[q]
+        lane = iota((128, 128), 1).astype(F32)
+        for at in range(0, long, 128):
+            ids = jnp.broadcast_to(rows_out[q, 0:1, at : at + 128], (128, 128)).T
+            for k in range(3):
+                hots[at : at + 128, 128 * k : 128 * (k + 1)] = jnp.where(ids == lane + 128.0 * k, 1.0, 0.0).astype(BF16)
         found = dot(hots[...], tab[...])
-        emb[:long, :] = found
-        low[...] = found[:, :chans].astype(BF16)
-        for m in range(PLANES):
-            x = emb[RP * m : RP * m + 128, chans : chans + 24].T
+        for c in range(chans // 128 + 1):
+            emb[c, :long, :] = found[:, 128 * c : 128 * (c + 1)]
+        lows[u][...] = found[:, :chans].astype(BF16)
+        for m in range(PLANES):
+            x = emb[chans // 128, RP * m : RP * m + 128, :24].T
             look_out[q, 8 * m : 8 * m + 8, :] = x[0:8] + x[8:16] + x[16:24]
 
     def convolve(q, u):
-        emb, _ = slots[u]
+        emb = embs[u]
         length = len_ref[q]
         for p in range(6):
             cotf[p, :rows, :] = cot_ref[u, p].astype(F32)
         place = PLANES * iota((8, 128), 0)
         lane = iota((8, 128), 1)
+        bits = [(lane >> k) % 2 == 1 for k in range(5)]
         for r in range(0, rows, 8):
             live = [place < length - (m + PLANES * r) for m in range(PLANES)]
             inner = [0.0] * 26
             for c in range(chans // 128):
                 lanes = slice(128 * c, 128 * (c + 1))
                 w = [conv_half[k : k + 1, lanes] for k in range(5)]
-                e = [emb[RP * m + r : RP * m + r + 8, lanes] for m in range(PLANES)]
-                behind = {m: emb[RP * m - 1 + r : RP * m + 7 + r, lanes] for m in (9, 10, 11)}
+                e = [emb[c, RP * m + r : RP * m + r + 8, :] for m in range(PLANES)]
+                behind = {m: emb[c, RP * m - 1 + r : RP * m + 7 + r, :] for m in (9, 10, 11)}
                 conv = convolved(w, e, behind, live)
                 for m in range(PLANES):
                     convs[u][m, r : r + 8, lanes] = conv[m]
                 for k, p, x in pair_terms(blocks(conv)):
                     inner[k] = inner[k] + cotf[p, r : r + 8, lanes] * x
-            out = jnp.zeros((8, 128), F32)
-            for k in range(26):
-                out = jnp.where(lane == k, jnp.sum(inner[k], axis=1, keepdims=True), out)
-            turned[r : r + 8, :] = out
+            level = [jnp.broadcast_to(jnp.sum(x, axis=1, keepdims=True), (8, 128)) for x in inner]
+            for bit in bits:
+                level.append(level[-1])
+                level = [jnp.where(bit, b, a) for a, b in zip(level[0:-1:2], level[1::2])]
+            turned[r : r + 8, :] = level[0]
         inner_out[q] = turned[...].T[:32]
 
     @pl.when(n == 0)
@@ -182,10 +178,6 @@
         idcol[...] = jnp.full(idcol.shape, NO_ID, F32)
         for m in range(PLANES):
             idcol[RP * m : RP * m + rows, :] = cs[pl.ds(m, rows, stride=PLANES), :]
-        cols = idcol[...]
-        high = jnp.floor(cols * (1.0 / 128.0))
-        idc[:, 0:8] = (cols - 128.0 * high).astype(BF16)
-        idc[:, 8:16] = high.astype(BF16)
         rows_out[...] = jnp.zeros(rows_out.shape, F32)
         for i in range(long // 128):
             flipped = idcol[128 * i : 128 * (i + 1), :].T
@@ -198,41 +190,36 @@
         mixed = jnp.concatenate(list(split3(mixed)) + [jnp.zeros(mixed.shape, BF16)], axis=0)
         got = dot(tab_all[...], mixed, NT)
         got = got + pltpu.roll(got, 96, 1) + pltpu.roll(got, 64, 1)
+        looks[...] = jnp.zeros(looks.shape, BF16)
         for k, part in enumerate(split3(got[:, :32])):
-            looks[k] = part
+            looks[:, 32 * k : 32 * (k + 1)] = part
+        sub, lane = iota((128, 128), 0), iota((128, 128), 1)
+        for q in range(seqs):
+            here = (sub % 8 == lang_ref[q]) & (lane == sub // 32 * 8 + sub % 32 // 8) & (sub < 96)
+            extras[q] = dot(looks[...], jnp.where(here, 1.0, 0.0).astype(BF16)).astype(BF16)
         conv_half[...] = convw_ref[:, mine]
         turned[...] = jnp.zeros(turned.shape, F32)
         cotf[...] = jnp.zeros(cotf.shape, F32)
-        for emb, _ in slots:
-            emb[long:, :] = jnp.zeros((emb.shape[0] - long, emb.shape[1]), F32)
-        look_up(0, slots[0])
-        send(0, 0).start()
+        for emb in embs:
+            emb[:, long:, :] = jnp.zeros((emb.shape[0], emb.shape[1] - long, 128), F32)
 
     for u in range(2):
         q = 2 * n + u
-        later = q + 1
-        within = jnp.minimum(later, seqs - 1)
-
-        @pl.when(later >= 2)
+
+        @pl.when(n > 0)
         def _():
-            send(0, 1 - u).wait()
-
-        @pl.when(q >= 2)
-        def _():
+            send(0, u).wait()
             send_conv(0, u).wait()
 
-        look_up(within, slots[1 - u])
+        look_up(q, u)
+        send(q, u).start()
         convolve(q, u)
         send_conv(q, u).start()
 
-        @pl.when(later < seqs)
-        def _():
-            send(within, 1 - u).start()
-
     @pl.when(n == pl.num_programs(0) - 1)
     def _():
-        send(0, 1).wait()
         for k in range(2):
+            send(0, k).wait()
             send_conv(0, k).wait()
 
 
@@ -327,8 +314,7 @@
     emb_ref, prob_ref, coef_ref, inner_ref, other_ref,
     keep_out, send_out,
     tail, tab, pulls, mixed, grad, hist, acc, taps_acc, flat, conv_half, score_half, cotf,
-    gemb_a, gemb_b, low_a, low_b, cols_a, cols_b, turned_a, turned_b, total_a, total_b, wholes_a, wholes_b, hots,
-    keep, sems,
+    gemb, low_a, low_b, cols, across, totals, keep, sems,
 ):
     n = pl.program_id(0)
     seqs = len_ref.shape[0]
@@ -336,34 +322,32 @@
     groups = score_ref.shape[0]
     mine = half_lanes(half_ref, chans)
     padded = (rows + 7) // 8 * 8
-    gembs, lows, wholes = (gemb_a, gemb_b), (low_a, low_b), (wholes_a, wholes_b)
-    ready = ((cols_a, turned_a, total_a), (cols_b, turned_b, total_b))
+    lows = (low_a, low_b)
+    long = PLANES * RP
 
     def fetch(q, k):
         return pltpu.make_async_copy(emb_ref.at[q], lows[k], sems.at[k])
 
-    def to_table(q, k):
-        sub = iota((VP, PLANES * RP), 0).astype(F32)
-        hots[...] = jnp.where(rows_ref[q, 0:1, :] == sub, 1.0, 0.0).astype(BF16)
-        acc[:, :256] += dot(hots[...], gembs[k][:, :256])
-        yield
-        got = dot(hots[...], gembs[k][:, 256:])
-        acc[:, 256:] += got[:, : chans - 256]
-        hist[:VP, :] = got[:, chans - 256 :]
-        yield
+    def to_table():
+        sub = iota((VP, long), 0).astype(F32)
+        hot = [jnp.where(rows_ref[q, 0:1, :] == sub, 1.0, 0.0).astype(BF16) for q in range(seqs)]
+        got = dot(jnp.concatenate(hot, axis=1), gemb[...])
+        acc[...] = got[:, :chans]
+        hist[:VP, :] = got[:, chans:]
         counts = hist[...].T
-        counts = counts[0:8] + counts[64:72]
-        counts = jnp.concatenate([counts, jnp.zeros((8, 384), F32)], axis=0)
+        counts = counts[: 4 * seqs] + counts[64 : 64 + 4 * seqs]
         from_table = dot(jnp.concatenate(split3(counts), axis=0), tab[...])
-        from_table = from_table[:16] + from_table[16:32] + from_table[32:]
-        part = conv_half[4:5, :] * wholes[k][0:1, :]
-        for j in range(4):
-            part = part + conv_half[j : j + 1, :] * from_table[j : j + 1, :]
-        acc[VP - groups : VP, :] += jnp.where(iota((groups, chans), 0) == lang_ref[q], part, 0.0)
-        yield
-
-    def prepare(q, k):
-        cols, turned, total = ready[k]
+        from_table = from_table[: 4 * seqs] + from_table[4 * seqs : 8 * seqs] + from_table[8 * seqs :]
+        group = iota((groups, chans), 0)
+        total = 0.0
+        for q in range(seqs):
+            part = conv_half[4:5, :] * totals[q, 0:1, :]
+            for j in range(4):
+                part = part + conv_half[j : j + 1, :] * from_table[4 * q + j : 4 * q + j + 1, :]
+            total = total + jnp.where(group == lang_ref[q], part, 0.0)
+        acc[VP - groups : VP, :] += total
+
+    def prepare(q):
         both = inner_ref[q] + other_ref[q]
         live = live_planes(len_ref[q])
         inverse = inverse_counts(live)
@@ -378,49 +362,37 @@
             mean = functools.reduce(jnp.add, [x * y for x, y in zip(prob, inner)])
             for b in range(4):
                 pull[b].append(prob[b] * (inner[b] - mean) * inv[b])
-            if m in (2, 5, 8):
-                yield
         sums = [blocks(pull[b])[b] for b in range(4)]
         pull = [live[m] * (sums[0][m] + sums[1][m // 2] + sums[2][m // 3] + sums[3][m // 4]) for m in range(PLANES)]
         whole = jnp.sum(functools.reduce(jnp.add, pull), axis=1, keepdims=True)
-        total[...] = jnp.broadcast_to(whole, total.shape)
+        totals[q] = jnp.broadcast_to(whole, totals.shape[1:])
         high = coef_ref[q].astype(BF16).astype(F32)
-        mixed[0:32, :] = high
-        mixed[64:96, :] = coef_ref[q] - high
+        mixed[q, 0:32, :] = high
+        mixed[q, 64:96, :] = coef_ref[q] - high
         for m, x in enumerate(pull + [after_lane(x) for x in pull[:3]]):
             high = x.astype(BF16).astype(F32)
-            pulls[m : m + 1, :] = high
-            pulls[64 + m : 65 + m, :] = x - high
+            pulls[q, m : m + 1, :] = high
+            pulls[q, 64 + m : 65 + m, :] = x - high
             if m < PLANES:
-                mixed[32 + m : 33 + m, :] = high
-                mixed[96 + m : 97 + m, :] = x - high
-        yield
-        turned[...] = pulls[...].T
-        coef = mixed[...].T[:RP].astype(BF16)
-        yield
-        columns = [*range(26), *range(32, 44)]
-        for k in range(0, len(columns), 5):
-            spread_columns(coef, keep, cols, columns[k : k + 5])
-            yield
-        while True:
-            yield
-
-    def gradients(q, u, table, coming):
-        cols, turned, total = ready[u]
-        gemb, low = gembs[u], lows[u]
-        wholes[u][...] = total[...]
+                mixed[q, 32 + m : 33 + m, :] = high
+                mixed[q, 96 + m : 97 + m, :] = x - high
+        turned = pulls[q].T
+        lane = iota((RP, 128), 1)
+        for m in range(PLANES):
+            x = turned if (4 * q - m) % 128 == 0 else pltpu.roll(turned, (4 * q - m) % 128, 1)
+            x = jnp.where(lane % 64 // 4 == q, x[:RP], 0.0)
+            gemb[long * q + RP * m : long * q + RP * (m + 1), chans:] = x.astype(BF16)
+        across[q] = mixed[q].T[:RP].astype(BF16)
+
+    def gradients(q, u):
         length = len_ref[q]
-        for m in range(PLANES):
-            x = turned[...] if m == 0 else pltpu.roll(turned[...], 128 - m, 1)
-            gemb[RP * m : RP * (m + 1), chans:] = x[:RP].astype(BF16)
         score = pick_row(score_half[...], lang_ref[q])
         for p in range(6):
             cotf[p, :rows, :] = cot_ref[u, p].astype(F32)
-        place = PLANES * iota((8, 128), 0)
+        columns = [*range(26), *range(32, 44)]
         for r in range(0, rows, 8):
-            if r == 8:
-                next(table)
-            alive = [place < length - (m + PLANES * r) for m in range(PLANES)]
+            if r % 16 == 0:
+                spread_columns(across[q, r : r + 16, :], keep, cols.at[:, r : r + 16, :], columns)
             for c in range(chans // 128):
                 lanes = slice(128 * c, 128 * (c + 1))
                 cot = [cotf[p, r : r + 8, lanes] for p in range(6)]
@@ -433,55 +405,54 @@
                 for m in range(PLANES):
                     value = times(m, m // 2) + four[m // 4] + three[m // 3]
                     value = value + cols[32 + m, r : r + 8, :] * score[:, lanes]
-                    grad[c, RP * m + r : RP * m + r + 8, :] = jnp.where(alive[m], value, 0.0)
-        @pl.when(length > 0)
-        def _():
+                    grad[c, RP * m + r : RP * m + r + 8, :] = value
+        end = length // PLANES
+        for m in range(PLANES):
             for c in range(chans // 128):
-                lanes = slice(128 * c, 128 * (c + 1))
-                w = [conv_half[k : k + 1, lanes] for k in range(4)]
-                tap = [0.0] * 5
-                for r in range(0, padded, 16):
-                    count = min(16, padded - r)
-                    if r == 16 and c < 2:
-                        next(table)
-                    next(coming)
-                    g = [grad[c, RP * m + r : RP * m + r + count, :] for m in range(PLANES)]
-                    g += [grad[c, RP * m + r + 1 : RP * m + r + 1 + count, :] for m in range(3)]
-                    fold = lambda x: x[:8] + x[8:] if count == 16 else x
-                    for m in range(PLANES):
-                        back = w[0] * g[m] + w[1] * g[m + 1] + w[2] * g[m + 2] + w[3] * g[m + 3]
-                        if count < 16:
-                            back = jnp.concatenate([back, jnp.zeros((16 - count, 128), F32)], axis=0)
-                        gemb[RP * m + r : RP * m + r + 16, lanes] = back.astype(BF16)
-                        e = low[RP * m + r : RP * m + r + 16, lanes].astype(F32)[:count]
-                        for k in range(4):
-                            tap[k] = tap[k] + fold(e * g[m + k])
-                        tap[4] = tap[4] + fold(g[m])
-                for k in range(5):
-                    taps_acc[k, :, lanes] += tap[k]
+                at = pl.ds(RP * m + end, 1)
+                grad[c, at, :] = jnp.where(PLANES * end + m < length, grad[c, at, :], 0.0)
+
+    def weight_gradients(q, u):
+        low = lows[u]
+        base = pl.multiple_of(q * long, 128)
+        for c in range(chans // 128):
+            lanes = slice(128 * c, 128 * (c + 1))
+            w = [conv_half[k : k + 1, lanes] for k in range(4)]
+            tap = [0.0] * 5
+            for r in range(0, padded, 16):
+                count = min(16, padded - r)
+                g = [grad[c, RP * m + r : RP * m + r + count, :] for m in range(PLANES)]
+                g += [grad[c, RP * m + r + 1 : RP * m + r + 1 + count, :] for m in range(3)]
+                fold = lambda x: x[:8] + x[8:] if count == 16 else x
+                for m in range(PLANES):
+                    back = w[0] * g[m] + w[1] * g[m + 1] + w[2] * g[m + 2] + w[3] * g[m + 3]
+                    if count < 16:
+                        back = jnp.concatenate([back, jnp.zeros((16 - count, 128), F32)], axis=0)
+                    gemb[pl.ds(base + RP * m + r, 16), lanes] = back.astype(BF16)
+                    e = low[RP * m + r : RP * m + r + 16, lanes].astype(F32)[:count]
+                    for k in range(4):
+                        tap[k] = tap[k] + fold(e * g[m + k])
+                    tap[4] = tap[4] + fold(g[m])
+            for k in range(5):
+                taps_acc[k, :, lanes] += tap[k]
 
     @pl.when(n == 0)
     def _():
         fetch(0, 0).start()
         load_table(table_ref, mine, tail, tab, chans)
-        for k in range(2):
-            gembs[k][...] = jnp.zeros(gembs[k].shape, BF16)
-            wholes[k][...] = jnp.zeros(wholes[k].shape, F32)
         cotf[...] = jnp.zeros(cotf.shape, F32)
         pulls[...] = jnp.zeros(pulls.shape, F32)
         mixed[...] = jnp.zeros(mixed.shape, F32)
         for m in range(PLANES):
             grad[:, RP * m + rows : RP * (m + 1), :] = jnp.zeros((chans // 128, RP - rows, 128), F32)
         grad[:, PLANES * RP :, :] = jnp.zeros((chans // 128, 8, 128), F32)
-        acc[...] = jnp.zeros(acc.shape, F32)
         taps_acc[...] = jnp.zeros(taps_acc.shape, F32)
         hist[...] = jnp.zeros(hist.shape, F32)
         conv_half[...] = convw_ref[:, mine]
         score_half[...] = score_ref[:, mine]
         spread_masks(keep)
-        first = prepare(0, 0)
-        for _ in range(30):
-            next(first)
+        for q in range(seqs):
+            prepare(q)
 
     for u in range(2):
         q = 2 * n + u
@@ -492,12 +463,15 @@
         def _():
             fetch(later, 1 - u).start()
 
-        gradients(q, u, to_table(jnp.maximum(q - 1, 0), 1 - u), prepare(later, 1 - u))
+        gradients(q, u)
+
+        @pl.when(len_ref[q] > 0)
+        def _():
+            weight_gradients(q, u)
 
     @pl.when(n == pl.num_programs(0) - 1)
     def _():
-        for _ in to_table(seqs - 1, 1):
-            pass
+        to_table()
         for k in range(5):
             at = VP - groups - 5 + k
             acc[at : at + 1, :] = jnp.sum(taps_acc[k], axis=0, keepdims=True)
@@ -557,7 +531,7 @@
     half_rows, chans = cotangent.shape[1:]
     groups = score_w.shape[0]
     rows = slot // PLANES
-    assert rows * PLANES == slot and rows <= RP - 2 and seqs % 2 == 0
+    assert rows * PLANES == slot and rows <= RP - 2 and seqs % 2 == 0 and seqs <= 16
     half = lax.axis_index("blk").astype(jnp.int32).reshape(1)
     seq = lax.axis_index("seq").astype(jnp.int32)
     core, far_bit, near_bit = seq % 2, (seq // 4) % 2, (seq // 2) % 2
@@ -600,13 +574,14 @@
             whole(seqs, 8 * PLANES, 128), whole(seqs, 32, 128), whole(seqs, 8, long),
         ],
         [
-            vmem((8, long), F32), vmem((long, 8), F32), vmem((long, 8), F32), vmem((long, 16), BF16),
-            vmem((128, full), F32), vmem((384, full), BF16), vmem((3, 384, 32), BF16),
+            vmem((8, long), F32), vmem((long, 8), F32), vmem((long, 8), F32),
+            vmem((128, full), F32), vmem((384, full), BF16), vmem((384, 128), BF16),
             vmem((128, chans), F32), vmem((384, chans + 128), BF16),
-            vmem((long + 32, chans + 128), F32), vmem((long + 32, chans + 128), F32),
-            vmem((long, chans), BF16), vmem((long, chans), BF16),
+            vmem((chans // 128 + 1, long + 32, 128), F32), vmem((chans // 128 + 1, long + 32, 128), F32),
+            vmem((long, chans), BF16), vmem((long, chans), BF16), vmem((seqs, 384, 128), BF16),
             vmem((5, chans), F32), vmem((6, RP, chans), F32), vmem((128, 128), F32), vmem((long, 384), BF16),
-            vmem((PLANES, padded, chans), F32), vmem((PLANES, padded, chans), F32), pltpu.SemaphoreType.DMA((4,)),
+            vmem((PLANES, padded, chans), F32), vmem((PLANES, padded, chans), F32),
+            pltpu.SemaphoreType.DMA((4,)),
         ],
         FORWARD_MIB, seqs // 2,
     )
@@ -633,15 +608,13 @@
         [shape((total // 2, 128), F32)] * 2,
         [whole(total // 2, 128)] * 2,
         [
-            vmem((128, chans), F32), vmem((384, chans), BF16), vmem((128, 128), F32), vmem((128, 128), F32),
+            vmem((128, chans), F32), vmem((384, chans), BF16),
+            vmem((seqs, 128, 128), F32), vmem((seqs, 128, 128), F32),
             vmem((chans // 128, long + 8, 128), F32), vmem((384, 128), F32), vmem((VP, chans), F32),
             vmem((5, 8, chans), F32), vmem((total, 128), F32), vmem((5, chans), F32), vmem((groups, chans), F32),
             vmem((6, RP, chans), F32),
-            vmem((long, chans + 128), BF16), vmem((long, chans + 128), BF16),
-            vmem((long, chans), BF16), vmem((long, chans), BF16),
-            vmem((44, RP, 128), F32), vmem((44, RP, 128), F32),
-            vmem((128, 128), F32), vmem((128, 128), F32), vmem((8, chans), F32), vmem((8, chans), F32),
-            vmem((8, chans), F32), vmem((8, chans), F32), vmem((VP, long), BF16),
+            vmem((seqs * long, chans + 128), BF16), vmem((long, chans), BF16), vmem((long, chans), BF16),
+            vmem((44, RP, 128), F32), vmem((seqs, RP, 128), BF16), vmem((seqs, 8, chans), F32),
             vmem((44, 16, 128), BF16), pltpu.SemaphoreType.DMA((2,)),
         ],
         BACKWARD_MIB, seqs // 2,

time: 57.9 us -> 57.1 us (0.986)
  Pallas kernels: 32.9 us -> 32.1 us
    pallas_call x4, Pallas kernels: 26.9 us -> 26.1 us  [call(): pl.pallas_call(kernel, grid_spec=pltpu.PrefetchScalarGridSpec(num_scalar_...]
where the time goes in v4:
time: 57.1 us; the launch traced here: 56.9 us
  Pallas kernels  32.1 us (56%)
  starting transfers between devices  11.7 us (20%)
  waiting for transfers between devices  6.9 us (12%)
  local copies, waits for them, and re-layouts  5.02 us (9%)
  between operations  0.99 us (2%)
    pallas_call x4, Pallas kernels, call(): pl.pallas_call(kernel, grid_spec=pltpu.PrefetchScalarGridSpec(num_scalar_...  26.1 us
    ppermute x6, starting transfers between devices, swap(): lax.ppermute(x, 'seq', [(i, i ^ (odd_step if i % 2 else step)) for i in r...  8.73 us
    pallas_call x2, Pallas kernels, pooled_two(): pl.pallas_call(functools.partial(pooled_kernel, first), in_specs=[pl.Bloc...  5.98 us
    ppermute x6, waiting for transfers between devices, swap(): lax.ppermute(x, 'seq', [(i, i ^ (odd_step if i % 2 else step)) for i in r...  5.65 us
    transpose x1, local copies, waits for them, and re-layouts, local(): pooled = pooled.transpose(0, 2, 1, 3).reshape(seqs, half_rows, chans)  3.25 us
    ppermute x1, starting transfers between devices, local(): other = lax.ppermute(inner, 'blk', [(0, 1), (1, 0)])  3 us
    reshape x1, local copies, waits for them, and re-layouts, local(): planes = cotangent.reshape(seqs, rows, 6, chans).transpose(0, 2, 1, 3)  1.69 us
    ppermute x1, waiting for transfers between devices, local(): other = lax.ppermute(inner, 'blk', [(0, 1), (1, 0)])  1.25 us
  transfers between devices with their start and end apart: 7, of which 4 were waited for; matrix products, arithmetic and copies ran while one was open for 6% of the time, Pallas kernels for 12%

profile of v4, /device:TPU:0, one launch (start us, length us, event | category | flops | bytes accessed | tf_op | source)
XLA Modules:
  0.0 56.9 jit_solution(4025134216388027148)
XLA Ops:
  0.6 0.0 copy-start.4
  0.7 0.0 copy-start.3
  0.7 0.0 copy-start
  0.7 0.0 copy-start.11
  0.7 0.0 copy-start.10
  0.7 1.7 %copy.28 = bf16[4,86,6,384]{3,1,2,0:T(8,128)(2,1)S(1)} copy(bf16[4,86,6,384]{3,0,2,1:T(4,128)(2,1)} %bitcast.20) | data formatting | bytes 3170304 | tf_op jit(solution)/shard_map/reshape | solution.py:560
  2.5 10.4 %forward.1 = (bf16[4,1152,384]{2,1,0:T(8,128)(2,1)}, f32[4,12,88,384]{3,2,1,0:T(8,128)}, f32[4,96,128]{2,1,0:T(8,128)S(1)}, f32[4,32,128]{2,1,0:T(8,128)S(1)}, f32[4,8,1152]{2,1,0:T(8,128)S(1)}) custom-call(s32[1]{0:T(128)} %bitcast.half_ref, s32[4]{0:T(128)S(1)} %copy-done.10, s32[4]{0:T(128)S(1)} %copy-done.11, s32[4,1032]{1,0:T(4,128)S(1)} %copy-done.5, ...), custom_call_target="tpu_custom_call" | custom-call | tf_op jit(solution)/shard_map/forward/pallas_call | solution.py:547
  12.9 3.0 %collective-permute-start = (f32[4,32,128]{2,1,0:T(8,128)S(1)}, f32[4,32,128]{2,1,0:T(8,128)S(1)}, u32[]{:S(2)}, u32[]{:S(2)}) collective-permute-start(f32[4,32,128]{2,1,0:T(8,128)S(1)} %get-tuple-element.41.inner_ref), channel_id=1, source_target_pairs={{0,16},{16,0},{1,17},{17,1},{2,18},{18,2},{3,19},{19,3},{4,20},{20... | collective-permute-start | bytes 196616 | tf_op jit(solution)/shard_map/ppermute | solution.py:589
  15.9 1.0 %scores.1 = (f32[4,48,128]{2,1,0:T(8,128)S(1)}, f32[4,32,128]{2,1,0:T(8,128)S(1)}) custom-call(s32[4]{0:T(128)S(1)} %copy-done.10, s32[4]{0:T(128)S(1)} %copy-done.11, f32[4,96,128]{2,1,0:T(8,128)S(1)} %get-tuple-element.42.look_ref, f32[5,768]{1,0:T(8,128)S(1)} %copy-done.3, f32[8,768]{1,0:T(8,128)S(1)} %copy-done.4), custom_call_target="tpu_custom_call" | custom-call | tf_op jit(solution)/shard_map/scores/pallas_call | solution.py:547
  16.9 1.3 %collective-permute-done.other_ref = f32[4,32,128]{2,1,0:T(8,128)S(1)} collective-permute-done((f32[4,32,128]{2,1,0:T(8,128)S(1)}, f32[4,32,128]{2,1,0:T(8,128)S(1)}, u32[]{:S(2)}, u32[]{:S(2)}) %collective-permute-start) | collective-permute-done | bytes 65568 | tf_op jit(solution)/shard_map/ppermute | solution.py:589
  18.1 12.1 %backward.1 = (f32[416,128]{1,0:T(8,128)S(1)}, f32[416,128]{1,0:T(8,128)S(1)}) custom-call(s32[1]{0:T(128)} %bitcast.half_ref, s32[4]{0:T(128)S(1)} %copy-done.10, s32[4]{0:T(128)S(1)} %copy-done.11, s32[1]{0:T(128)} %bitcast.1.core_ref, f32[4,8,1152]{2,1,0:T(8,128)S(1)} %get-tuple-element.39.rows_ref, bf16[4,6,86,384]{3,2,1,0:T(8,128)(2,1)S(1)} %bitcast.18, ...), custom_call_target="tpu_custom_call" | custom-call | tf_op jit(solution)/shard_map/backward/pallas_call | solution.py:547
  30.2 0.1 collective-permute-start.1
  30.4 1.4 %collective-permute-done.1 = f32[416,128]{1,0:T(8,128)S(1)} collective-permute-done((f32[416,128]{1,0:T(8,128)S(1)}, f32[416,128]{1,0:T(8,128)S(1)}, u32[]{:S(2)}, u32[]{:S(2)}) %collective-permute-start.1) | collective-permute-done | bytes 213024 | tf_op jit(solution)/shard_map/ppermute | solution.py:624
  31.8 2.2 %collective-permute-start.2 = (f32[208,128]{1,0:T(8,128)S(1)}, f32[208,128]{1,0:T(8,128)S(1)}, u32[]{:S(2)}, u32[]{:S(2)}) collective-permute-start(f32[208,128]{1,0:T(8,128)S(1)} %constant_dynamic-slice_fusion), channel_id=1, source_target_pairs={{0,4},{1,3},{2,6},{3,1},{4,0},{5,7},{6,2},{7,5},{8,12},{9,11},{10,... | collective-permute-start | bytes 319496 | tf_op jit(solution)/shard_map/ppermute | solution.py:624
  34.0 3.0 %pooled.2.refs_0_ = bf16[4,6,86,384]{3,2,1,0:T(8,128)(2,1)} custom-call(f32[4,32,128]{2,1,0:T(8,128)S(1)} %get-tuple-element.46.coef_ref.refs_0_.refs_1_, f32[4,12,88,384]{3,2,1,0:T(8,128)} %get-tuple-element.52.refs_1_.refs_2_), custom_call_target="tpu_custom_call" | custom-call | tf_op jit(solution)/shard_map/pooled/pallas_call | solution.py:628
  37.0 0.0 collective-permute-done.2
  37.0 1.7 %collective-permute-start.3 = (f32[208,128]{1,0:T(8,128)S(1)}, f32[208,128]{1,0:T(8,128)S(1)}, u32[]{:S(2)}, u32[]{:S(2)}) collective-permute-start(f32[208,128]{1,0:T(8,128)S(1)} %dynamic-slice_add_fusion), channel_id=1, source_target_pairs={{0,2},{1,9},{2,0},{3,11},{4,6},{5,13},{6,4},{7,15},{8,10},{9,1},{1... | collective-permute-start | bytes 319496 | tf_op jit(solution)/shard_map/ppermute | solution.py:624
  38.7 3.0 %pooled.3 = bf16[4,6,86,384]{3,2,1,0:T(8,128)(2,1)} custom-call(bf16[4,6,86,384]{3,2,1,0:T(8,128)(2,1)} %pooled.2.refs_0_, f32[4,32,128]{2,1,0:T(8,128)S(1)} %get-tuple-element.46.coef_ref.refs_0_.refs_1_, f32[4,12,88,384]{3,2,1,0:T(8,128)} %get-tuple-element.52.refs_1_.refs_2_), custom_call_target="tpu_custom_call", output_to_operand_aliasing={{}: (0, {})} | custom-call | tf_op jit(solution)/shard_map/pooled/pallas_call | solution.py:628
  41.7 0.0 collective-permute-done.3
  41.8 2.8 %collective-permute-start.4 = (f32[208,128]{1,0:T(8,128)S(1)}, f32[208,128]{1,0:T(8,128)S(1)}, u32[]{:S(2)}, u32[]{:S(2)}) collective-permute-start(f32[208,128]{1,0:T(8,128)S(1)} %add.37), channel_id=1, source_target_pairs={{0,8},{1,5},{2,10},{3,7},{4,12},{5,1},{6,14},{7,3},{8,0},{9,13},{1... | collective-permute-start | bytes 319496 | tf_op jit(solution)/shard_map/ppermute | solution.py:624
  44.6 0.0 copy-start.8
  44.6 0.0 copy-start.9
  44.6 0.0 copy-start.12
  44.6 3.2 %copy.26 = bf16[4,86,6,384]{3,0,2,1:T(4,128)(2,1)} copy(bf16[4,86,6,384]{3,1,2,0:T(8,128)(2,1)} %bitcast.19) | data formatting | bytes 3170304 | tf_op jit(solution)/shard_map/transpose | solution.py:663
  47.9 0.0 collective-permute-done.4
  47.9 1.9 %collective-permute-start.5 = (f32[208,128]{1,0:T(8,128)S(1)}, f32[208,128]{1,0:T(8,128)S(1)}, u32[]{:S(2)}, u32[]{:S(2)}) collective-permute-start(f32[208,128]{1,0:T(8,128)S(1)} %add.38), channel_id=1, source_target_pairs={{0,4},{1,3},{2,6},{3,1},{4,0},{5,7},{6,2},{7,5},{8,12},{9,11},{10,... | collective-permute-start | bytes 319496 | tf_op jit(solution)/shard_map/ppermute | solution.py:624
  49.8 2.8 %collective-permute-done.5 = f32[208,128]{1,0:T(8,128)S(1)} collective-permute-done((f32[208,128]{1,0:T(8,128)S(1)}, f32[208,128]{1,0:T(8,128)S(1)}, u32[]{:S(2)}, u32[]{:S(2)}) %collective-permute-start.5) | collective-permute-done | bytes 106528 | tf_op jit(solution)/shard_map/ppermute | solution.py:624
  52.7 0.1 collective-permute-start.6
  52.7 0.1 pad_add_fusion.place_ref
  52.8 1.4 %collective-permute-done.6.other_ref = f32[416,128]{1,0:T(8,128)S(1)} collective-permute-done((f32[416,128]{1,0:T(8,128)S(1)}, f32[416,128]{1,0:T(8,128)S(1)}, u32[]{:S(2)}, u32[]{:S(2)}) %collective-permute-start.6) | collective-permute-done | bytes 213024 | tf_op jit(solution)/shard_map/ppermute | solution.py:624
  54.2 0.0 copy-done.2
  54.2 2.6 %update.1 = (f32[259,1,384]{2,1,0:T(1,128)}, f32[259,1,384]{2,1,0:T(1,128)}, f32[259,1,384]{2,1,0:T(1,128)}, f32[5,1,384]{2,1,0:T(1,128)}, f32[5,1,384]{2,1,0:T(...) custom-call(s32[1]{0:T(128)} %bitcast.half_ref, ...), custom_call_target="tpu_custom_call" | custom-call | tf_op jit(solution)/shard_map/update/pallas_call | solution.py:547
  (23 shorter events, 0.1 us)
Async XLA Ops:
  0.6 1.8 %copy-start.4 = (f32[8,768]{1,0:T(8,128)S(1)}, f32[8,768]{1,0:T(8,128)}, u32[]{:S(2)}) copy-start(f32[8,768]{1,0:T(8,128)} %refs_6_.1) | copy-start | bytes 73732
  0.7 1.8 %copy-start.3 = (f32[5,768]{1,0:T(8,128)S(1)}, f32[5,768]{1,0:T(8,128)}, u32[]{:S(2)}) copy-start(f32[5,768]{1,0:T(8,128)} %refs_3_.1) | copy-start | bytes 46084
  0.7 1.8 %copy-start = (f32[259,768]{1,0:T(8,128)S(1)}, f32[259,768]{1,0:T(8,128)}, u32[]{:S(2)}) copy-start(f32[259,768]{1,0:T(8,128)} %refs_0_.1) | copy-start | bytes 2386948
  0.7 1.8 %copy-start.11 = (s32[4]{0:T(128)S(1)}, s32[4]{0:T(128)}, u32[]{:S(2)}) copy-start(s32[4]{0:T(128)} %lang_ref.5) | copy-start | bytes 52
  0.7 1.8 %copy-start.10 = (s32[4]{0:T(128)S(1)}, s32[4]{0:T(128)}, u32[]{:S(2)}) copy-start(s32[4]{0:T(128)} %len_ref.5) | copy-start | bytes 52
  0.7 1.8 %copy-start.5 = (s32[4,1032]{1,0:T(4,128)S(1)}, s32[4,1032]{1,0:T(4,128)}, u32[]{:S(2)}) copy-start(s32[4,1032]{1,0:T(4,128)} %ids_ref.1) | copy-start | bytes 49540
  12.9 5.2 %collective-permute-start = (f32[4,32,128]{2,1,0:T(8,128)S(1)}, f32[4,32,128]{2,1,0:T(8,128)S(1)}, u32[]{:S(2)}, u32[]{:S(2)}) collective-permute-start(f32[4,32,128]{2,1,0:T(8,128)S(1)} %get-tuple-element.41.inner_ref), channel_id=1, source_target_pairs={{0,16},{16,0},{1,17},{17,1},{2,18},{18,2},{3,19},{19,3},{4,20},{20... | collective-permute-start | bytes 196616 | tf_op jit(solution)/shard_map/ppermute | solution.py:589
  30.2 1.5 %collective-permute-start.1 = (f32[416,128]{1,0:T(8,128)S(1)}, f32[416,128]{1,0:T(8,128)S(1)}, u32[]{:S(2)}, u32[]{:S(2)}) collective-permute-start(f32[416,128]{1,0:T(8,128)S(1)} %get-tuple-element.51), channel_id=1, source_target_pairs={{0,1},{1,0},{2,3},{3,2},{4,5},{5,4},{6,7},{7,6},{8,9},{9,8},{10,11... | collective-permute-start | bytes 638984 | tf_op jit(solution)/shard_map/ppermute | solution.py:624
  31.8 5.2 %collective-permute-start.2 = (f32[208,128]{1,0:T(8,128)S(1)}, f32[208,128]{1,0:T(8,128)S(1)}, u32[]{:S(2)}, u32[]{:S(2)}) collective-permute-start(f32[208,128]{1,0:T(8,128)S(1)} %constant_dynamic-slice_fusion), channel_id=1, source_target_pairs={{0,4},{1,3},{2,6},{3,1},{4,0},{5,7},{6,2},{7,5},{8,12},{9,11},{10,... | collective-permute-start | bytes 319496 | tf_op jit(solution)/shard_map/ppermute | solution.py:624
  37.0 4.8 %collective-permute-start.3 = (f32[208,128]{1,0:T(8,128)S(1)}, f32[208,128]{1,0:T(8,128)S(1)}, u32[]{:S(2)}, u32[]{:S(2)}) collective-permute-start(f32[208,128]{1,0:T(8,128)S(1)} %dynamic-slice_add_fusion), channel_id=1, source_target_pairs={{0,2},{1,9},{2,0},{3,11},{4,6},{5,13},{6,4},{7,15},{8,10},{9,1},{1... | collective-permute-start | bytes 319496 | tf_op jit(solution)/shard_map/ppermute | solution.py:624
  41.8 6.1 %collective-permute-start.4 = (f32[208,128]{1,0:T(8,128)S(1)}, f32[208,128]{1,0:T(8,128)S(1)}, u32[]{:S(2)}, u32[]{:S(2)}) collective-permute-start(f32[208,128]{1,0:T(8,128)S(1)} %add.37), channel_id=1, source_target_pairs={{0,8},{1,5},{2,10},{3,7},{4,12},{5,1},{6,14},{7,3},{8,0},{9,13},{1... | collective-permute-start | bytes 319496 | tf_op jit(solution)/shard_map/ppermute | solution.py:624
  44.6 9.6 %copy-start.1 = (f32[259,384]{1,0:T(8,128)S(1)}, f32[259,384]{1,0:T(8,128)}, u32[]{:S(2)}) copy-start(f32[259,384]{1,0:T(8,128)} %refs_1_.1) | copy-start | bytes 1193476
  44.6 9.6 %copy-start.2 = (f32[259,384]{1,0:T(8,128)S(1)}, f32[259,384]{1,0:T(8,128)}, u32[]{:S(2)}) copy-start(f32[259,384]{1,0:T(8,128)} %refs_2_.1) | copy-start | bytes 1193476
  44.6 9.6 %copy-start.6 = (f32[5,384]{1,0:T(8,128)S(1)}, f32[5,384]{1,0:T(8,128)}, u32[]{:S(2)}) copy-start(f32[5,384]{1,0:T(8,128)} %refs_4_.1) | copy-start | bytes 23044
  44.6 9.6 %copy-start.7 = (f32[5,384]{1,0:T(8,128)S(1)}, f32[5,384]{1,0:T(8,128)}, u32[]{:S(2)}) copy-start(f32[5,384]{1,0:T(8,128)} %refs_5_.1) | copy-start | bytes 23044
  44.6 9.6 %copy-start.8 = (f32[8,384]{1,0:T(8,128)S(1)}, f32[8,384]{1,0:T(8,128)}, u32[]{:S(2)}) copy-start(f32[8,384]{1,0:T(8,128)} %refs_7_.1) | copy-start | bytes 36868
  44.6 9.6 %copy-start.9 = (f32[8,384]{1,0:T(8,128)S(1)}, f32[8,384]{1,0:T(8,128)}, u32[]{:S(2)}) copy-start(f32[8,384]{1,0:T(8,128)} %refs_8_.1) | copy-start | bytes 36868
  44.6 9.6 %copy-start.12 = (s32[3]{0:T(128)S(1)}, s32[3]{0:T(128)}, u32[]{:S(2)}) copy-start(s32[3]{0:T(128)} %owner_ref.1) | copy-start | bytes 40
  47.9 4.8 %collective-permute-start.5 = (f32[208,128]{1,0:T(8,128)S(1)}, f32[208,128]{1,0:T(8,128)S(1)}, u32[]{:S(2)}, u32[]{:S(2)}) collective-permute-start(f32[208,128]{1,0:T(8,128)S(1)} %add.38), channel_id=1, source_target_pairs={{0,4},{1,3},{2,6},{3,1},{4,0},{5,7},{6,2},{7,5},{8,12},{9,11},{10,... | collective-permute-start | bytes 319496 | tf_op jit(solution)/shard_map/ppermute | solution.py:624
  52.7 1.5 %collective-permute-start.6 = (f32[416,128]{1,0:T(8,128)S(1)}, f32[416,128]{1,0:T(8,128)S(1)}, u32[]{:S(2)}, u32[]{:S(2)}) collective-permute-start(f32[416,128]{1,0:T(8,128)S(1)} %pad_maximum_fusion.mine_ref), channel_id=1, source_target_pairs={{0,1},{1,0},{2,3},{3,2},{4,5},{5,4},{6,7},{7,6},{8,9},{9,8},{10,11... | collective-permute-start | bytes 638984 | tf_op jit(solution)/shard_map/ppermute | solution.py:624

commit v5 on v4

--- a/solution.py
+++ b/solution.py
@@ -314,7 +314,7 @@
     emb_ref, prob_ref, coef_ref, inner_ref, other_ref,
     keep_out, send_out,
     tail, tab, pulls, mixed, grad, hist, acc, taps_acc, flat, conv_half, score_half, cotf,
-    gemb, low_a, low_b, cols, across, totals, keep, sems,
+    gemb, low, cols, across, totals, keep, sems,
 ):
     n = pl.program_id(0)
     seqs = len_ref.shape[0]
@@ -322,11 +322,10 @@
     groups = score_ref.shape[0]
     mine = half_lanes(half_ref, chans)
     padded = (rows + 7) // 8 * 8
-    lows = (low_a, low_b)
     long = PLANES * RP
 
-    def fetch(q, k):
-        return pltpu.make_async_copy(emb_ref.at[q], lows[k], sems.at[k])
+    def fetch(q):
+        return pltpu.make_async_copy(emb_ref.at[q], low.at[q], sems.at[q])
 
     def to_table():
         sub = iota((VP, long), 0).astype(F32)
@@ -413,7 +412,6 @@
                 grad[c, at, :] = jnp.where(PLANES * end + m < length, grad[c, at, :], 0.0)
 
     def weight_gradients(q, u):
-        low = lows[u]
         base = pl.multiple_of(q * long, 128)
         for c in range(chans // 128):
             lanes = slice(128 * c, 128 * (c + 1))
@@ -429,7 +427,7 @@
                     if count < 16:
                         back = jnp.concatenate([back, jnp.zeros((16 - count, 128), F32)], axis=0)
                     gemb[pl.ds(base + RP * m + r, 16), lanes] = back.astype(BF16)
-                    e = low[RP * m + r : RP * m + r + 16, lanes].astype(F32)[:count]
+                    e = low[q, RP * m + r : RP * m + r + 16, lanes].astype(F32)[:count]
                     for k in range(4):
                         tap[k] = tap[k] + fold(e * g[m + k])
                     tap[4] = tap[4] + fold(g[m])
@@ -438,7 +436,8 @@
 
     @pl.when(n == 0)
     def _():
-        fetch(0, 0).start()
+        for q in range(seqs):
+            fetch(q).start()
         load_table(table_ref, mine, tail, tab, chans)
         cotf[...] = jnp.zeros(cotf.shape, F32)
         pulls[...] = jnp.zeros(pulls.shape, F32)
@@ -456,14 +455,8 @@
 
     for u in range(2):
         q = 2 * n + u
-        later = jnp.minimum(q + 1, seqs - 1)
-        fetch(q, u).wait()
-
-        @pl.when(q + 1 < seqs)
-        def _():
-            fetch(later, 1 - u).start()
-
         gradients(q, u)
+        fetch(q).wait()
 
         @pl.when(len_ref[q] > 0)
         def _():
@@ -613,9 +606,9 @@
             vmem((chans // 128, long + 8, 128), F32), vmem((384, 128), F32), vmem((VP, chans), F32),
             vmem((5, 8, chans), F32), vmem((total, 128), F32), vmem((5, chans), F32), vmem((groups, chans), F32),
             vmem((6, RP, chans), F32),
-            vmem((seqs * long, chans + 128), BF16), vmem((long, chans), BF16), vmem((long, chans), BF16),
+            vmem((seqs * long, chans + 128), BF16), vmem((seqs, long, chans), BF16),
             vmem((44, RP, 128), F32), vmem((seqs, RP, 128), BF16), vmem((seqs, 8, chans), F32),
-            vmem((44, 16, 128), BF16), pltpu.SemaphoreType.DMA((2,)),
+            vmem((44, 16, 128), BF16), pltpu.SemaphoreType.DMA((seqs,)),
         ],
         BACKWARD_MIB, seqs // 2,
     )

time: 57.1 us -> 56.3 us (0.986)
  Pallas kernels: 32.1 us -> 31.3 us
    pallas_call x4, Pallas kernels: 26.1 us -> 25.4 us  [call(): pl.pallas_call(kernel, grid_spec=pltpu.PrefetchScalarGridSpec(num_scalar_...]
  transfers between devices with their start and end apart: 7 -> 7, of which waited for: 4 -> 5; matrix products, arithmetic and copies ran while one was open for 6% -> 6% of each run, Pallas kernels for 12% -> 12%
where the time goes in v5:
time: 56.3 us; the launch traced here: 56.1 us
  Pallas kernels  31.3 us (56%)
  starting transfers between devices  11.7 us (21%)
  waiting for transfers between devices  6.9 us (12%)
  local copies, waits for them, and re-layouts  5.02 us (9%)
  between operations  0.99 us (2%)
    pallas_call x4, Pallas kernels, call(): pl.pallas_call(kernel, grid_spec=pltpu.PrefetchScalarGridSpec(num_scalar_...  25.4 us
    ppermute x6, starting transfers between devices, swap(): lax.ppermute(x, 'seq', [(i, i ^ (odd_step if i % 2 else step)) for i in r...  8.73 us
    pallas_call x2, Pallas kernels, pooled_two(): pl.pallas_call(functools.partial(pooled_kernel, first), in_specs=[pl.Bloc...  5.98 us
    ppermute x6, waiting for transfers between devices, swap(): lax.ppermute(x, 'seq', [(i, i ^ (odd_step if i % 2 else step)) for i in r...  5.65 us
    transpose x1, local copies, waits for them, and re-layouts, local(): pooled = pooled.transpose(0, 2, 1, 3).reshape(seqs, half_rows, chans)  3.25 us
    ppermute x1, starting transfers between devices, local(): other = lax.ppermute(inner, 'blk', [(0, 1), (1, 0)])  3 us
    reshape x1, local copies, waits for them, and re-layouts, local(): planes = cotangent.reshape(seqs, rows, 6, chans).transpose(0, 2, 1, 3)  1.69 us
    ppermute x1, waiting for transfers between devices, local(): other = lax.ppermute(inner, 'blk', [(0, 1), (1, 0)])  1.25 us
  transfers between devices with their start and end apart: 7, of which 5 were waited for; matrix products, arithmetic and copies ran while one was open for 6% of the time, Pallas kernels for 12%

profile of v5, /device:TPU:0, one launch (start us, length us, event | category | flops | bytes accessed | tf_op | source)
XLA Modules:
  0.0 56.1 jit_solution(137927706095929328)
XLA Ops:
  0.6 0.0 copy-start.4
  0.7 0.0 copy-start.3
  0.7 0.0 copy-start
  0.7 0.0 copy-start.11
  0.7 0.0 copy-start.10
  0.7 1.7 %copy.28 = bf16[4,86,6,384]{3,1,2,0:T(8,128)(2,1)S(1)} copy(bf16[4,86,6,384]{3,0,2,1:T(4,128)(2,1)} %bitcast.20) | data formatting | bytes 3170304 | tf_op jit(solution)/shard_map/reshape | solution.py:553
  2.5 10.4 %forward.1 = (bf16[4,1152,384]{2,1,0:T(8,128)(2,1)}, f32[4,12,88,384]{3,2,1,0:T(8,128)}, f32[4,96,128]{2,1,0:T(8,128)S(1)}, f32[4,32,128]{2,1,0:T(8,128)S(1)}, f32[4,8,1152]{2,1,0:T(8,128)S(1)}) custom-call(s32[1]{0:T(128)} %bitcast.half_ref, s32[4]{0:T(128)S(1)} %copy-done.10, s32[4]{0:T(128)S(1)} %copy-done.11, s32[4,1032]{1,0:T(4,128)S(1)} %copy-done.5, ...), custom_call_target="tpu_custom_call" | custom-call | tf_op jit(solution)/shard_map/forward/pallas_call | solution.py:540
  12.9 3.0 %collective-permute-start = (f32[4,32,128]{2,1,0:T(8,128)S(1)}, f32[4,32,128]{2,1,0:T(8,128)S(1)}, u32[]{:S(2)}, u32[]{:S(2)}) collective-permute-start(f32[4,32,128]{2,1,0:T(8,128)S(1)} %get-tuple-element.41.inner_ref), channel_id=1, source_target_pairs={{0,16},{16,0},{1,17},{17,1},{2,18},{18,2},{3,19},{19,3},{4,20},{20... | collective-permute-start | bytes 196616 | tf_op jit(solution)/shard_map/ppermute | solution.py:582
  15.9 1.0 %scores.1 = (f32[4,48,128]{2,1,0:T(8,128)S(1)}, f32[4,32,128]{2,1,0:T(8,128)S(1)}) custom-call(s32[4]{0:T(128)S(1)} %copy-done.10, s32[4]{0:T(128)S(1)} %copy-done.11, f32[4,96,128]{2,1,0:T(8,128)S(1)} %get-tuple-element.42.look_ref, f32[5,768]{1,0:T(8,128)S(1)} %copy-done.3, f32[8,768]{1,0:T(8,128)S(1)} %copy-done.4), custom_call_target="tpu_custom_call" | custom-call | tf_op jit(solution)/shard_map/scores/pallas_call | solution.py:540
  16.9 1.3 %collective-permute-done.other_ref = f32[4,32,128]{2,1,0:T(8,128)S(1)} collective-permute-done((f32[4,32,128]{2,1,0:T(8,128)S(1)}, f32[4,32,128]{2,1,0:T(8,128)S(1)}, u32[]{:S(2)}, u32[]{:S(2)}) %collective-permute-start) | collective-permute-done | bytes 65568 | tf_op jit(solution)/shard_map/ppermute | solution.py:582
  18.1 11.4 %backward.1 = (f32[416,128]{1,0:T(8,128)S(1)}, f32[416,128]{1,0:T(8,128)S(1)}) custom-call(s32[1]{0:T(128)} %bitcast.half_ref, s32[4]{0:T(128)S(1)} %copy-done.10, s32[4]{0:T(128)S(1)} %copy-done.11, s32[1]{0:T(128)} %bitcast.1.core_ref, f32[4,8,1152]{2,1,0:T(8,128)S(1)} %get-tuple-element.39.rows_ref, bf16[4,6,86,384]{3,2,1,0:T(8,128)(2,1)S(1)} %bitcast.18, ...), custom_call_target="tpu_custom_call" | custom-call | tf_op jit(solution)/shard_map/backward/pallas_call | solution.py:540
  29.5 0.1 collective-permute-start.1
  29.6 1.4 %collective-permute-done.1 = f32[416,128]{1,0:T(8,128)S(1)} collective-permute-done((f32[416,128]{1,0:T(8,128)S(1)}, f32[416,128]{1,0:T(8,128)S(1)}, u32[]{:S(2)}, u32[]{:S(2)}) %collective-permute-start.1) | collective-permute-done | bytes 213024 | tf_op jit(solution)/shard_map/ppermute | solution.py:617
  31.1 2.2 %collective-permute-start.2 = (f32[208,128]{1,0:T(8,128)S(1)}, f32[208,128]{1,0:T(8,128)S(1)}, u32[]{:S(2)}, u32[]{:S(2)}) collective-permute-start(f32[208,128]{1,0:T(8,128)S(1)} %constant_dynamic-slice_fusion), channel_id=1, source_target_pairs={{0,4},{1,3},{2,6},{3,1},{4,0},{5,7},{6,2},{7,5},{8,12},{9,11},{10,... | collective-permute-start | bytes 319496 | tf_op jit(solution)/shard_map/ppermute | solution.py:617
  33.3 3.0 %pooled.2.refs_0_ = bf16[4,6,86,384]{3,2,1,0:T(8,128)(2,1)} custom-call(f32[4,32,128]{2,1,0:T(8,128)S(1)} %get-tuple-element.46.coef_ref.refs_0_.refs_1_, f32[4,12,88,384]{3,2,1,0:T(8,128)} %get-tuple-element.52.refs_1_.refs_2_), custom_call_target="tpu_custom_call" | custom-call | tf_op jit(solution)/shard_map/pooled/pallas_call | solution.py:621
  36.2 0.0 collective-permute-done.2
  36.3 1.7 %collective-permute-start.3 = (f32[208,128]{1,0:T(8,128)S(1)}, f32[208,128]{1,0:T(8,128)S(1)}, u32[]{:S(2)}, u32[]{:S(2)}) collective-permute-start(f32[208,128]{1,0:T(8,128)S(1)} %dynamic-slice_add_fusion), channel_id=1, source_target_pairs={{0,2},{1,9},{2,0},{3,11},{4,6},{5,13},{6,4},{7,15},{8,10},{9,1},{1... | collective-permute-start | bytes 319496 | tf_op jit(solution)/shard_map/ppermute | solution.py:617
  38.0 3.0 %pooled.3 = bf16[4,6,86,384]{3,2,1,0:T(8,128)(2,1)} custom-call(bf16[4,6,86,384]{3,2,1,0:T(8,128)(2,1)} %pooled.2.refs_0_, f32[4,32,128]{2,1,0:T(8,128)S(1)} %get-tuple-element.46.coef_ref.refs_0_.refs_1_, f32[4,12,88,384]{3,2,1,0:T(8,128)} %get-tuple-element.52.refs_1_.refs_2_), custom_call_target="tpu_custom_call", output_to_operand_aliasing={{}: (0, {})} | custom-call | tf_op jit(solution)/shard_map/pooled/pallas_call | solution.py:621
  41.0 0.1 collective-permute-done.3
  41.1 2.8 %collective-permute-start.4 = (f32[208,128]{1,0:T(8,128)S(1)}, f32[208,128]{1,0:T(8,128)S(1)}, u32[]{:S(2)}, u32[]{:S(2)}) collective-permute-start(f32[208,128]{1,0:T(8,128)S(1)} %add.37), channel_id=1, source_target_pairs={{0,8},{1,5},{2,10},{3,7},{4,12},{5,1},{6,14},{7,3},{8,0},{9,13},{1... | collective-permute-start | bytes 319496 | tf_op jit(solution)/shard_map/ppermute | solution.py:617
  43.8 0.0 copy-start.8
  43.9 0.0 copy-start.9
  43.9 0.0 copy-start.12
  43.9 3.2 %copy.26 = bf16[4,86,6,384]{3,0,2,1:T(4,128)(2,1)} copy(bf16[4,86,6,384]{3,1,2,0:T(8,128)(2,1)} %bitcast.19) | data formatting | bytes 3170304 | tf_op jit(solution)/shard_map/transpose | solution.py:656
  47.1 0.0 collective-permute-done.4
  47.1 1.9 %collective-permute-start.5 = (f32[208,128]{1,0:T(8,128)S(1)}, f32[208,128]{1,0:T(8,128)S(1)}, u32[]{:S(2)}, u32[]{:S(2)}) collective-permute-start(f32[208,128]{1,0:T(8,128)S(1)} %add.38), channel_id=1, source_target_pairs={{0,4},{1,3},{2,6},{3,1},{4,0},{5,7},{6,2},{7,5},{8,12},{9,11},{10,... | collective-permute-start | bytes 319496 | tf_op jit(solution)/shard_map/ppermute | solution.py:617
  49.1 2.8 %collective-permute-done.5 = f32[208,128]{1,0:T(8,128)S(1)} collective-permute-done((f32[208,128]{1,0:T(8,128)S(1)}, f32[208,128]{1,0:T(8,128)S(1)}, u32[]{:S(2)}, u32[]{:S(2)}) %collective-permute-start.5) | collective-permute-done | bytes 106528 | tf_op jit(solution)/shard_map/ppermute | solution.py:617
  51.9 0.1 collective-permute-start.6
  52.0 0.1 pad_add_fusion.place_ref
  52.1 1.4 %collective-permute-done.6.other_ref = f32[416,128]{1,0:T(8,128)S(1)} collective-permute-done((f32[416,128]{1,0:T(8,128)S(1)}, f32[416,128]{1,0:T(8,128)S(1)}, u32[]{:S(2)}, u32[]{:S(2)}) %collective-permute-start.6) | collective-permute-done | bytes 213024 | tf_op jit(solution)/shard_map/ppermute | solution.py:617
  53.5 0.0 copy-done.1
  53.5 2.6 %update.1 = (f32[259,1,384]{2,1,0:T(1,128)}, f32[259,1,384]{2,1,0:T(1,128)}, f32[259,1,384]{2,1,0:T(1,128)}, f32[5,1,384]{2,1,0:T(1,128)}, f32[5,1,384]{2,1,0:T(...) custom-call(s32[1]{0:T(128)} %bitcast.half_ref, ...), custom_call_target="tpu_custom_call" | custom-call | tf_op jit(solution)/shard_map/update/pallas_call | solution.py:540
  (23 shorter events, 0.1 us)
Async XLA Ops:
  0.6 1.8 %copy-start.4 = (f32[8,768]{1,0:T(8,128)S(1)}, f32[8,768]{1,0:T(8,128)}, u32[]{:S(2)}) copy-start(f32[8,768]{1,0:T(8,128)} %refs_6_.1) | copy-start | bytes 73732
  0.7 1.8 %copy-start.3 = (f32[5,768]{1,0:T(8,128)S(1)}, f32[5,768]{1,0:T(8,128)}, u32[]{:S(2)}) copy-start(f32[5,768]{1,0:T(8,128)} %refs_3_.1) | copy-start | bytes 46084
  0.7 1.8 %copy-start = (f32[259,768]{1,0:T(8,128)S(1)}, f32[259,768]{1,0:T(8,128)}, u32[]{:S(2)}) copy-start(f32[259,768]{1,0:T(8,128)} %refs_0_.1) | copy-start | bytes 2386948
  0.7 1.8 %copy-start.11 = (s32[4]{0:T(128)S(1)}, s32[4]{0:T(128)}, u32[]{:S(2)}) copy-start(s32[4]{0:T(128)} %lang_ref.5) | copy-start | bytes 52
  0.7 1.8 %copy-start.10 = (s32[4]{0:T(128)S(1)}, s32[4]{0:T(128)}, u32[]{:S(2)}) copy-start(s32[4]{0:T(128)} %len_ref.5) | copy-start | bytes 52
  0.7 1.8 %copy-start.5 = (s32[4,1032]{1,0:T(4,128)S(1)}, s32[4,1032]{1,0:T(4,128)}, u32[]{:S(2)}) copy-start(s32[4,1032]{1,0:T(4,128)} %ids_ref.1) | copy-start | bytes 49540
  12.9 5.2 %collective-permute-start = (f32[4,32,128]{2,1,0:T(8,128)S(1)}, f32[4,32,128]{2,1,0:T(8,128)S(1)}, u32[]{:S(2)}, u32[]{:S(2)}) collective-permute-start(f32[4,32,128]{2,1,0:T(8,128)S(1)} %get-tuple-element.41.inner_ref), channel_id=1, source_target_pairs={{0,16},{16,0},{1,17},{17,1},{2,18},{18,2},{3,19},{19,3},{4,20},{20... | collective-permute-start | bytes 196616 | tf_op jit(solution)/shard_map/ppermute | solution.py:582
  29.5 1.5 %collective-permute-start.1 = (f32[416,128]{1,0:T(8,128)S(1)}, f32[416,128]{1,0:T(8,128)S(1)}, u32[]{:S(2)}, u32[]{:S(2)}) collective-permute-start(f32[416,128]{1,0:T(8,128)S(1)} %get-tuple-element.51), channel_id=1, source_target_pairs={{0,1},{1,0},{2,3},{3,2},{4,5},{5,4},{6,7},{7,6},{8,9},{9,8},{10,11... | collective-permute-start | bytes 638984 | tf_op jit(solution)/shard_map/ppermute | solution.py:617
  31.1 5.2 %collective-permute-start.2 = (f32[208,128]{1,0:T(8,128)S(1)}, f32[208,128]{1,0:T(8,128)S(1)}, u32[]{:S(2)}, u32[]{:S(2)}) collective-permute-start(f32[208,128]{1,0:T(8,128)S(1)} %constant_dynamic-slice_fusion), channel_id=1, source_target_pairs={{0,4},{1,3},{2,6},{3,1},{4,0},{5,7},{6,2},{7,5},{8,12},{9,11},{10,... | collective-permute-start | bytes 319496 | tf_op jit(solution)/shard_map/ppermute | solution.py:617
  36.3 4.8 %collective-permute-start.3 = (f32[208,128]{1,0:T(8,128)S(1)}, f32[208,128]{1,0:T(8,128)S(1)}, u32[]{:S(2)}, u32[]{:S(2)}) collective-permute-start(f32[208,128]{1,0:T(8,128)S(1)} %dynamic-slice_add_fusion), channel_id=1, source_target_pairs={{0,2},{1,9},{2,0},{3,11},{4,6},{5,13},{6,4},{7,15},{8,10},{9,1},{1... | collective-permute-start | bytes 319496 | tf_op jit(solution)/shard_map/ppermute | solution.py:617
  41.1 6.1 %collective-permute-start.4 = (f32[208,128]{1,0:T(8,128)S(1)}, f32[208,128]{1,0:T(8,128)S(1)}, u32[]{:S(2)}, u32[]{:S(2)}) collective-permute-start(f32[208,128]{1,0:T(8,128)S(1)} %add.37), channel_id=1, source_target_pairs={{0,8},{1,5},{2,10},{3,7},{4,12},{5,1},{6,14},{7,3},{8,0},{9,13},{1... | collective-permute-start | bytes 319496 | tf_op jit(solution)/shard_map/ppermute | solution.py:617
  43.8 9.6 %copy-start.1 = (f32[259,384]{1,0:T(8,128)S(1)}, f32[259,384]{1,0:T(8,128)}, u32[]{:S(2)}) copy-start(f32[259,384]{1,0:T(8,128)} %refs_1_.1) | copy-start | bytes 1193476
  43.8 9.6 %copy-start.2 = (f32[259,384]{1,0:T(8,128)S(1)}, f32[259,384]{1,0:T(8,128)}, u32[]{:S(2)}) copy-start(f32[259,384]{1,0:T(8,128)} %refs_2_.1) | copy-start | bytes 1193476
  43.8 9.6 %copy-start.6 = (f32[5,384]{1,0:T(8,128)S(1)}, f32[5,384]{1,0:T(8,128)}, u32[]{:S(2)}) copy-start(f32[5,384]{1,0:T(8,128)} %refs_4_.1) | copy-start | bytes 23044
  43.8 9.6 %copy-start.7 = (f32[5,384]{1,0:T(8,128)S(1)}, f32[5,384]{1,0:T(8,128)}, u32[]{:S(2)}) copy-start(f32[5,384]{1,0:T(8,128)} %refs_5_.1) | copy-start | bytes 23044
  43.8 9.6 %copy-start.8 = (f32[8,384]{1,0:T(8,128)S(1)}, f32[8,384]{1,0:T(8,128)}, u32[]{:S(2)}) copy-start(f32[8,384]{1,0:T(8,128)} %refs_7_.1) | copy-start | bytes 36868
  43.9 9.6 %copy-start.9 = (f32[8,384]{1,0:T(8,128)S(1)}, f32[8,384]{1,0:T(8,128)}, u32[]{:S(2)}) copy-start(f32[8,384]{1,0:T(8,128)} %refs_8_.1) | copy-start | bytes 36868
  43.9 9.6 %copy-start.12 = (s32[3]{0:T(128)S(1)}, s32[3]{0:T(128)}, u32[]{:S(2)}) copy-start(s32[3]{0:T(128)} %owner_ref.1) | copy-start | bytes 40
  47.1 4.8 %collective-permute-start.5 = (f32[208,128]{1,0:T(8,128)S(1)}, f32[208,128]{1,0:T(8,128)S(1)}, u32[]{:S(2)}, u32[]{:S(2)}) collective-permute-start(f32[208,128]{1,0:T(8,128)S(1)} %add.38), channel_id=1, source_target_pairs={{0,4},{1,3},{2,6},{3,1},{4,0},{5,7},{6,2},{7,5},{8,12},{9,11},{10,... | collective-permute-start | bytes 319496 | tf_op jit(solution)/shard_map/ppermute | solution.py:617
  51.9 1.5 %collective-permute-start.6 = (f32[416,128]{1,0:T(8,128)S(1)}, f32[416,128]{1,0:T(8,128)S(1)}, u32[]{:S(2)}, u32[]{:S(2)}) collective-permute-start(f32[416,128]{1,0:T(8,128)S(1)} %pad_maximum_fusion.mine_ref), channel_id=1, source_target_pairs={{0,1},{1,0},{2,3},{3,2},{4,5},{5,4},{6,7},{7,6},{8,9},{9,8},{10,11... | collective-permute-start | bytes 638984 | tf_op jit(solution)/shard_map/ppermute | solution.py:617

commit v6 on v5

--- a/solution.py
+++ b/solution.py
@@ -224,6 +224,7 @@
 
 
 def score_kernel(len_ref, lang_ref, look_ref, convw_ref, score_ref, prob_out, coef_out):
+    prob_out[...] = jnp.zeros(prob_out.shape, F32)
     bias = jnp.sum(convw_ref[4:5, :] * score_ref[...], axis=1, keepdims=True)
     bias = jnp.broadcast_to(bias, (score_ref.shape[0], 128))
     for q in range(look_ref.shape[0]):
@@ -248,7 +249,7 @@
             scale = 1.0 / functools.reduce(jnp.add, grown)
             for b in range(4):
                 prob = grown[b] * scale
-                prob_out[q, PLANES * b + m : PLANES * b + m + 1, :] = prob
+                prob_out[PLANES * b + m, q : q + 1, :] = prob
                 weights[b].append(0.5 * live[m] * prob * inverse[b][m // (b + 1)])
         coef_out[q, 24:32, :] = jnp.zeros((8, 128), F32)
         for k, row in enumerate(coefficients(weights)):
@@ -292,13 +293,14 @@
         both[64:96, :] = coef_ref[first + u] - high
         across = both[...].T[:RP].astype(BF16)
         for k in range(0, 26, 13):
-            spread_columns(across, keep, cols, range(k, k + 13))
+            spread_columns(across, keep, cols.at[u], range(k, k + 13))
+    for u in range(2):
         for c in range(chunks):
             fetches[chunks * u + c].wait()
             for r in range(0, padded, 8):
                 pooled = [0.0] * 6
                 for k, p, x in pair_terms(blocks([conv[u, c, m, r : r + 8, :] for m in range(PLANES)])):
-                    pooled[p] = pooled[p] + cols[k, r : r + 8, :] * x
+                    pooled[p] = pooled[p] + cols[u, k, r : r + 8, :] * x
                 for p in range(6):
                     poolf[p, r : r + 8, :] = pooled[p]
             for p in range(6):
@@ -314,7 +316,7 @@
     emb_ref, prob_ref, coef_ref, inner_ref, other_ref,
     keep_out, send_out,
     tail, tab, pulls, mixed, grad, hist, acc, taps_acc, flat, conv_half, score_half, cotf,
-    gemb, low, cols, across, totals, keep, sems,
+    gemb, low, cols, across, totals, keep, products, sems,
 ):
     n = pl.program_id(0)
     seqs = len_ref.shape[0]
@@ -346,16 +348,21 @@
             total = total + jnp.where(group == lang_ref[q], part, 0.0)
         acc[VP - groups : VP, :] += total
 
-    def prepare(q):
-        both = inner_ref[q] + other_ref[q]
-        live = live_planes(len_ref[q])
+    def prepare():
+        sub, lane = iota((8, 128), 0), iota((8, 128), 1)
+        length = jnp.zeros((8, 128), jnp.int32)
+        for q in range(seqs):
+            both = inner_ref[q] + other_ref[q]
+            for j in range(26):
+                products[j, q : q + 1, :] = both[j : j + 1, :]
+            length = jnp.where(sub == q, len_ref[q], length)
+        live = [jnp.where(PLANES * lane + m < length, 1.0, 0.0).astype(F32) for m in range(PLANES)]
         inverse = inverse_counts(live)
-        row = lambda j: both[j : j + 1, :]
         pull = [[], [], [], []]
         for m in range(PLANES):
             p = m // 2
-            dots = [row(m), row(2 * p) + row(2 * p + 1), row(THIRD[m]), row(12 + p)]
-            prob = [prob_ref[q, PLANES * b + m : PLANES * b + m + 1, :] for b in range(4)]
+            dots = [products[m], products[2 * p] + products[2 * p + 1], products[THIRD[m]], products[12 + p]]
+            prob = [prob_ref[PLANES * b + m] for b in range(4)]
             inv = [inverse[b][m // (b + 1)] for b in range(4)]
             inner = [0.5 * jnp.where(live[m] > 0, d, 0.0) * c for d, c in zip(dots, inv)]
             mean = functools.reduce(jnp.add, [x * y for x, y in zip(prob, inner)])
@@ -364,24 +371,27 @@
         sums = [blocks(pull[b])[b] for b in range(4)]
         pull = [live[m] * (sums[0][m] + sums[1][m // 2] + sums[2][m // 3] + sums[3][m // 4]) for m in range(PLANES)]
         whole = jnp.sum(functools.reduce(jnp.add, pull), axis=1, keepdims=True)
-        totals[q] = jnp.broadcast_to(whole, totals.shape[1:])
-        high = coef_ref[q].astype(BF16).astype(F32)
-        mixed[q, 0:32, :] = high
-        mixed[q, 64:96, :] = coef_ref[q] - high
         for m, x in enumerate(pull + [after_lane(x) for x in pull[:3]]):
             high = x.astype(BF16).astype(F32)
-            pulls[q, m : m + 1, :] = high
-            pulls[q, 64 + m : 65 + m, :] = x - high
-            if m < PLANES:
-                mixed[q, 32 + m : 33 + m, :] = high
-                mixed[q, 96 + m : 97 + m, :] = x - high
-        turned = pulls[q].T
+            low_part = x - high
+            for q in range(seqs):
+                pulls[q, m : m + 1, :] = high[q : q + 1, :]
+                pulls[q, 64 + m : 65 + m, :] = low_part[q : q + 1, :]
+                if m < PLANES:
+                    mixed[q, 32 + m : 33 + m, :] = high[q : q + 1, :]
+                    mixed[q, 96 + m : 97 + m, :] = low_part[q : q + 1, :]
         lane = iota((RP, 128), 1)
-        for m in range(PLANES):
-            x = turned if (4 * q - m) % 128 == 0 else pltpu.roll(turned, (4 * q - m) % 128, 1)
-            x = jnp.where(lane % 64 // 4 == q, x[:RP], 0.0)
-            gemb[long * q + RP * m : long * q + RP * (m + 1), chans:] = x.astype(BF16)
-        across[q] = mixed[q].T[:RP].astype(BF16)
+        for q in range(seqs):
+            totals[q] = jnp.broadcast_to(whole[q : q + 1, :], totals.shape[1:])
+            high = coef_ref[q].astype(BF16).astype(F32)
+            mixed[q, 0:32, :] = high
+            mixed[q, 64:96, :] = coef_ref[q] - high
+            turned = pulls[q].T
+            for m in range(PLANES):
+                x = turned if (4 * q - m) % 128 == 0 else pltpu.roll(turned, (4 * q - m) % 128, 1)
+                x = jnp.where(lane % 64 // 4 == q, x[:RP], 0.0)
+                gemb[long * q + RP * m : long * q + RP * (m + 1), chans:] = x.astype(BF16)
+            across[q] = mixed[q].T[:RP].astype(BF16)
 
     def gradients(q, u):
         length = len_ref[q]
@@ -450,8 +460,8 @@
         conv_half[...] = convw_ref[:, mine]
         score_half[...] = score_ref[:, mine]
         spread_masks(keep)
-        for q in range(seqs):
-            prepare(q)
+        products[...] = jnp.zeros(products.shape, F32)
+        prepare()
 
     for u in range(2):
         q = 2 * n + u
@@ -524,7 +534,7 @@
     half_rows, chans = cotangent.shape[1:]
     groups = score_w.shape[0]
     rows = slot // PLANES
-    assert rows * PLANES == slot and rows <= RP - 2 and seqs % 2 == 0 and seqs <= 16
+    assert rows * PLANES == slot and rows <= RP - 2 and seqs % 2 == 0 and seqs <= 8
     half = lax.axis_index("blk").astype(jnp.int32).reshape(1)
     seq = lax.axis_index("seq").astype(jnp.int32)
     core, far_bit, near_bit = seq % 2, (seq // 4) % 2, (seq // 2) % 2
@@ -584,8 +594,8 @@
         score_kernel, "scores",
         [lengths, lang_ids], [look, conv_w, score_w],
         [whole(seqs, 8 * PLANES, 128), whole(5, full), whole(groups, full)],
-        [shape((seqs, 48, 128), F32), shape((seqs, 32, 128), F32)],
-        [whole(seqs, 48, 128), whole(seqs, 32, 128)], [], 16, 1,
+        [shape((48, 8, 128), F32), shape((seqs, 32, 128), F32)],
+        [whole(48, 8, 128), whole(seqs, 32, 128)], [], 16, 1,
     )
     other, prob, coef = lax.optimization_barrier((other, prob, coef))
     total = -(-VP * (chans // 128) // 32) * 32
@@ -595,7 +605,7 @@
         [id_rows, planes, table, conv_w, score_w, emb, prob, coef, inner, other],
         [
             whole(seqs, 8, long), by_two(6, rows, chans), whole(vocab, full), whole(5, full), whole(groups, full),
-            pl.BlockSpec(memory_space=pltpu.HBM), whole(seqs, 48, 128), whole(seqs, 32, 128),
+            pl.BlockSpec(memory_space=pltpu.HBM), whole(48, 8, 128), whole(seqs, 32, 128),
             whole(seqs, 32, 128), whole(seqs, 32, 128),
         ],
         [shape((total // 2, 128), F32)] * 2,
@@ -608,7 +618,7 @@
             vmem((6, RP, chans), F32),
             vmem((seqs * long, chans + 128), BF16), vmem((seqs, long, chans), BF16),
             vmem((44, RP, 128), F32), vmem((seqs, RP, 128), BF16), vmem((seqs, 8, chans), F32),
-            vmem((44, 16, 128), BF16), pltpu.SemaphoreType.DMA((seqs,)),
+            vmem((44, 16, 128), BF16), vmem((26, 8, 128), F32), pltpu.SemaphoreType.DMA((seqs,)),
         ],
         BACKWARD_MIB, seqs // 2,
     )
@@ -624,7 +634,7 @@
             + [pl.BlockSpec(memory_space=pltpu.VMEM), pl.BlockSpec(memory_space=pltpu.HBM)],
             out_specs=pl.BlockSpec(memory_space=pltpu.HBM),
             scratch_shapes=[
-                vmem((26, RP, 128), F32), vmem((2, chans // 128, PLANES, padded, 128), F32),
+                vmem((2, 26, RP, 128), F32), vmem((2, chans // 128, PLANES, padded, 128), F32),
                 vmem((6, padded, 128), F32), vmem((2, 6, rows, chans), BF16),
                 vmem((32, 16, 128), BF16), vmem((128, 128), F32),
                 pltpu.SemaphoreType.DMA((2 * (chans // 128) + 2,)),

time: 56.3 us -> 56 us (level)
  no operation moved by 1% of the time
where the time goes in v6:
time: 56 us; the launch traced here: 55.8 us
  Pallas kernels  30.8 us (55%)
  starting transfers between devices  11.8 us (21%)
  waiting for transfers between devices  7.02 us (13%)
  local copies, waits for them, and re-layouts  5.02 us (9%)
  between operations  0.99 us (2%)
    pallas_call x4, Pallas kernels, call(): pl.pallas_call(kernel, grid_spec=pltpu.PrefetchScalarGridSpec(num_scalar_...  25 us
    ppermute x6, starting transfers between devices, swap(): lax.ppermute(x, 'seq', [(i, i ^ (odd_step if i % 2 else step)) for i in r...  8.85 us
    ppermute x6, waiting for transfers between devices, swap(): lax.ppermute(x, 'seq', [(i, i ^ (odd_step if i % 2 else step)) for i in r...  5.77 us
    pallas_call x2, Pallas kernels, pooled_two(): pl.pallas_call(functools.partial(pooled_kernel, first), in_specs=[pl.Bloc...  5.74 us
    transpose x1, local copies, waits for them, and re-layouts, local(): pooled = pooled.transpose(0, 2, 1, 3).reshape(seqs, half_rows, chans)  3.25 us
    ppermute x1, starting transfers between devices, local(): other = lax.ppermute(inner, 'blk', [(0, 1), (1, 0)])  3 us
    reshape x1, local copies, waits for them, and re-layouts, local(): planes = cotangent.reshape(seqs, rows, 6, chans).transpose(0, 2, 1, 3)  1.69 us
    ppermute x1, waiting for transfers between devices, local(): other = lax.ppermute(inner, 'blk', [(0, 1), (1, 0)])  1.25 us
  transfers between devices with their start and end apart: 7, of which 5 were waited for; matrix products, arithmetic and copies ran while one was open for 6% of the time, Pallas kernels for 12%

profile of v6, /device:TPU:0, one launch (start us, length us, event | category | flops | bytes accessed | tf_op | source)
XLA Modules:
  0.0 55.8 jit_solution(17038233828478664303)
XLA Ops:
  0.6 0.0 copy-start.4
  0.7 0.0 copy-start.3
  0.7 1.7 %copy.28 = bf16[4,86,6,384]{3,1,2,0:T(8,128)(2,1)S(1)} copy(bf16[4,86,6,384]{3,0,2,1:T(4,128)(2,1)} %bitcast.20) | data formatting | bytes 3170304 | tf_op jit(solution)/shard_map/reshape | solution.py:563
  2.5 10.4 %forward.1 = (bf16[4,1152,384]{2,1,0:T(8,128)(2,1)}, f32[4,12,88,384]{3,2,1,0:T(8,128)}, f32[4,96,128]{2,1,0:T(8,128)S(1)}, f32[4,32,128]{2,1,0:T(8,128)S(1)}, f32[4,8,1152]{2,1,0:T(8,128)S(1)}) custom-call(s32[1]{0:T(128)} %bitcast.half_ref, s32[4]{0:T(128)S(1)} %copy-done.10, s32[4]{0:T(128)S(1)} %copy-done.11, s32[4,1032]{1,0:T(4,128)S(1)} %copy-done.5, ...), custom_call_target="tpu_custom_call" | custom-call | tf_op jit(solution)/shard_map/forward/pallas_call | solution.py:550
  12.9 3.0 %collective-permute-start = (f32[4,32,128]{2,1,0:T(8,128)S(1)}, f32[4,32,128]{2,1,0:T(8,128)S(1)}, u32[]{:S(2)}, u32[]{:S(2)}) collective-permute-start(f32[4,32,128]{2,1,0:T(8,128)S(1)} %get-tuple-element.41.inner_ref), channel_id=1, source_target_pairs={{0,16},{16,0},{1,17},{17,1},{2,18},{18,2},{3,19},{19,3},{4,20},{20... | collective-permute-start | bytes 196616 | tf_op jit(solution)/shard_map/ppermute | solution.py:592
  15.9 1.0 %scores.1 = (f32[48,8,128]{2,1,0:T(8,128)S(1)}, f32[4,32,128]{2,1,0:T(8,128)S(1)}) custom-call(s32[4]{0:T(128)S(1)} %copy-done.10, s32[4]{0:T(128)S(1)} %copy-done.11, f32[4,96,128]{2,1,0:T(8,128)S(1)} %get-tuple-element.42.look_ref, f32[5,768]{1,0:T(8,128)S(1)} %copy-done.3, f32[8,768]{1,0:T(8,128)S(1)} %copy-done.4), custom_call_target="tpu_custom_call" | custom-call | tf_op jit(solution)/shard_map/scores/pallas_call | solution.py:550
  16.9 1.3 %collective-permute-done.other_ref = f32[4,32,128]{2,1,0:T(8,128)S(1)} collective-permute-done((f32[4,32,128]{2,1,0:T(8,128)S(1)}, f32[4,32,128]{2,1,0:T(8,128)S(1)}, u32[]{:S(2)}, u32[]{:S(2)}) %collective-permute-start) | collective-permute-done | bytes 65568 | tf_op jit(solution)/shard_map/ppermute | solution.py:592
  18.1 11.0 %backward.1 = (f32[416,128]{1,0:T(8,128)S(1)}, f32[416,128]{1,0:T(8,128)S(1)}) custom-call(s32[1]{0:T(128)} %bitcast.half_ref, s32[4]{0:T(128)S(1)} %copy-done.10, s32[4]{0:T(128)S(1)} %copy-done.11, s32[1]{0:T(128)} %bitcast.1.core_ref, f32[4,8,1152]{2,1,0:T(8,128)S(1)} %get-tuple-element.39.rows_ref, bf16[4,6,86,384]{3,2,1,0:T(8,128)(2,1)S(1)} %bitcast.18, ...), custom_call_target="tpu_custom_call" | custom-call | tf_op jit(solution)/shard_map/backward/pallas_call | solution.py:550
  29.1 0.1 collective-permute-start.1
  29.3 1.4 %collective-permute-done.1 = f32[416,128]{1,0:T(8,128)S(1)} collective-permute-done((f32[416,128]{1,0:T(8,128)S(1)}, f32[416,128]{1,0:T(8,128)S(1)}, u32[]{:S(2)}, u32[]{:S(2)}) %collective-permute-start.1) | collective-permute-done | bytes 213024 | tf_op jit(solution)/shard_map/ppermute | solution.py:627
  30.7 2.2 %collective-permute-start.2 = (f32[208,128]{1,0:T(8,128)S(1)}, f32[208,128]{1,0:T(8,128)S(1)}, u32[]{:S(2)}, u32[]{:S(2)}) collective-permute-start(f32[208,128]{1,0:T(8,128)S(1)} %constant_dynamic-slice_fusion), channel_id=1, source_target_pairs={{0,4},{1,3},{2,6},{3,1},{4,0},{5,7},{6,2},{7,5},{8,12},{9,11},{10,... | collective-permute-start | bytes 319496 | tf_op jit(solution)/shard_map/ppermute | solution.py:627
  32.9 2.9 %pooled.2.refs_0_ = bf16[4,6,86,384]{3,2,1,0:T(8,128)(2,1)} custom-call(f32[4,32,128]{2,1,0:T(8,128)S(1)} %get-tuple-element.46.coef_ref.refs_0_.refs_1_, f32[4,12,88,384]{3,2,1,0:T(8,128)} %get-tuple-element.52.refs_1_.refs_2_), custom_call_target="tpu_custom_call" | custom-call | tf_op jit(solution)/shard_map/pooled/pallas_call | solution.py:631
  35.8 0.0 collective-permute-done.2
  35.8 1.8 %collective-permute-start.3 = (f32[208,128]{1,0:T(8,128)S(1)}, f32[208,128]{1,0:T(8,128)S(1)}, u32[]{:S(2)}, u32[]{:S(2)}) collective-permute-start(f32[208,128]{1,0:T(8,128)S(1)} %dynamic-slice_add_fusion), channel_id=1, source_target_pairs={{0,2},{1,9},{2,0},{3,11},{4,6},{5,13},{6,4},{7,15},{8,10},{9,1},{1... | collective-permute-start | bytes 319496 | tf_op jit(solution)/shard_map/ppermute | solution.py:627
  37.6 2.9 %pooled.3 = bf16[4,6,86,384]{3,2,1,0:T(8,128)(2,1)} custom-call(bf16[4,6,86,384]{3,2,1,0:T(8,128)(2,1)} %pooled.2.refs_0_, f32[4,32,128]{2,1,0:T(8,128)S(1)} %get-tuple-element.46.coef_ref.refs_0_.refs_1_, f32[4,12,88,384]{3,2,1,0:T(8,128)} %get-tuple-element.52.refs_1_.refs_2_), custom_call_target="tpu_custom_call", output_to_operand_aliasing={{}: (0, {})} | custom-call | tf_op jit(solution)/shard_map/pooled/pallas_call | solution.py:631
  40.5 0.1 collective-permute-done.3
  40.6 2.9 %collective-permute-start.4 = (f32[208,128]{1,0:T(8,128)S(1)}, f32[208,128]{1,0:T(8,128)S(1)}, u32[]{:S(2)}, u32[]{:S(2)}) collective-permute-start(f32[208,128]{1,0:T(8,128)S(1)} %add.37), channel_id=1, source_target_pairs={{0,8},{1,5},{2,10},{3,7},{4,12},{5,1},{6,14},{7,3},{8,0},{9,13},{1... | collective-permute-start | bytes 319496 | tf_op jit(solution)/shard_map/ppermute | solution.py:627
  43.5 0.0 copy-start.8
  43.5 0.0 copy-start.9
  43.5 0.0 copy-start.12
  43.5 3.2 %copy.26 = bf16[4,86,6,384]{3,0,2,1:T(4,128)(2,1)} copy(bf16[4,86,6,384]{3,1,2,0:T(8,128)(2,1)} %bitcast.19) | data formatting | bytes 3170304 | tf_op jit(solution)/shard_map/transpose | solution.py:666
  46.8 0.0 collective-permute-done.4
  46.8 1.8 %collective-permute-start.5 = (f32[208,128]{1,0:T(8,128)S(1)}, f32[208,128]{1,0:T(8,128)S(1)}, u32[]{:S(2)}, u32[]{:S(2)}) collective-permute-start(f32[208,128]{1,0:T(8,128)S(1)} %add.38), channel_id=1, source_target_pairs={{0,4},{1,3},{2,6},{3,1},{4,0},{5,7},{6,2},{7,5},{8,12},{9,11},{10,... | collective-permute-start | bytes 319496 | tf_op jit(solution)/shard_map/ppermute | solution.py:627
  48.6 3.0 %collective-permute-done.5 = f32[208,128]{1,0:T(8,128)S(1)} collective-permute-done((f32[208,128]{1,0:T(8,128)S(1)}, f32[208,128]{1,0:T(8,128)S(1)}, u32[]{:S(2)}, u32[]{:S(2)}) %collective-permute-start.5) | collective-permute-done | bytes 106528 | tf_op jit(solution)/shard_map/ppermute | solution.py:627
  51.6 0.1 collective-permute-start.6
  51.7 0.1 pad_add_fusion.place_ref
  51.8 1.4 %collective-permute-done.6.other_ref = f32[416,128]{1,0:T(8,128)S(1)} collective-permute-done((f32[416,128]{1,0:T(8,128)S(1)}, f32[416,128]{1,0:T(8,128)S(1)}, u32[]{:S(2)}, u32[]{:S(2)}) %collective-permute-start.6) | collective-permute-done | bytes 213024 | tf_op jit(solution)/shard_map/ppermute | solution.py:627
  53.1 0.0 copy-done.7
  53.1 0.0 copy-done.8
  53.2 0.0 copy-done.9
  53.2 0.0 copy-done.12
  53.2 2.6 %update.1 = (f32[259,1,384]{2,1,0:T(1,128)}, f32[259,1,384]{2,1,0:T(1,128)}, f32[259,1,384]{2,1,0:T(1,128)}, f32[5,1,384]{2,1,0:T(1,128)}, f32[5,1,384]{2,1,0:T(...) custom-call(s32[1]{0:T(128)} %bitcast.half_ref, ...), custom_call_target="tpu_custom_call" | custom-call | tf_op jit(solution)/shard_map/update/pallas_call | solution.py:550
  (23 shorter events, 0.1 us)
Async XLA Ops:
  0.6 1.8 %copy-start.4 = (f32[8,768]{1,0:T(8,128)S(1)}, f32[8,768]{1,0:T(8,128)}, u32[]{:S(2)}) copy-start(f32[8,768]{1,0:T(8,128)} %refs_6_.1) | copy-start | bytes 73732
  0.7 1.8 %copy-start.3 = (f32[5,768]{1,0:T(8,128)S(1)}, f32[5,768]{1,0:T(8,128)}, u32[]{:S(2)}) copy-start(f32[5,768]{1,0:T(8,128)} %refs_3_.1) | copy-start | bytes 46084
  0.7 1.8 %copy-start = (f32[259,768]{1,0:T(8,128)S(1)}, f32[259,768]{1,0:T(8,128)}, u32[]{:S(2)}) copy-start(f32[259,768]{1,0:T(8,128)} %refs_0_.1) | copy-start | bytes 2386948
  0.7 1.8 %copy-start.11 = (s32[4]{0:T(128)S(1)}, s32[4]{0:T(128)}, u32[]{:S(2)}) copy-start(s32[4]{0:T(128)} %lang_ref.5) | copy-start | bytes 52
  0.7 1.8 %copy-start.10 = (s32[4]{0:T(128)S(1)}, s32[4]{0:T(128)}, u32[]{:S(2)}) copy-start(s32[4]{0:T(128)} %len_ref.5) | copy-start | bytes 52
  0.7 1.8 %copy-start.5 = (s32[4,1032]{1,0:T(4,128)S(1)}, s32[4,1032]{1,0:T(4,128)}, u32[]{:S(2)}) copy-start(s32[4,1032]{1,0:T(4,128)} %ids_ref.1) | copy-start | bytes 49540
  12.9 5.2 %collective-permute-start = (f32[4,32,128]{2,1,0:T(8,128)S(1)}, f32[4,32,128]{2,1,0:T(8,128)S(1)}, u32[]{:S(2)}, u32[]{:S(2)}) collective-permute-start(f32[4,32,128]{2,1,0:T(8,128)S(1)} %get-tuple-element.41.inner_ref), channel_id=1, source_target_pairs={{0,16},{16,0},{1,17},{17,1},{2,18},{18,2},{3,19},{19,3},{4,20},{20... | collective-permute-start | bytes 196616 | tf_op jit(solution)/shard_map/ppermute | solution.py:592
  29.1 1.5 %collective-permute-start.1 = (f32[416,128]{1,0:T(8,128)S(1)}, f32[416,128]{1,0:T(8,128)S(1)}, u32[]{:S(2)}, u32[]{:S(2)}) collective-permute-start(f32[416,128]{1,0:T(8,128)S(1)} %get-tuple-element.51), channel_id=1, source_target_pairs={{0,1},{1,0},{2,3},{3,2},{4,5},{5,4},{6,7},{7,6},{8,9},{9,8},{10,11... | collective-permute-start | bytes 638984 | tf_op jit(solution)/shard_map/ppermute | solution.py:627
  30.7 5.0 %collective-permute-start.2 = (f32[208,128]{1,0:T(8,128)S(1)}, f32[208,128]{1,0:T(8,128)S(1)}, u32[]{:S(2)}, u32[]{:S(2)}) collective-permute-start(f32[208,128]{1,0:T(8,128)S(1)} %constant_dynamic-slice_fusion), channel_id=1, source_target_pairs={{0,4},{1,3},{2,6},{3,1},{4,0},{5,7},{6,2},{7,5},{8,12},{9,11},{10,... | collective-permute-start | bytes 319496 | tf_op jit(solution)/shard_map/ppermute | solution.py:627
  35.8 4.8 %collective-permute-start.3 = (f32[208,128]{1,0:T(8,128)S(1)}, f32[208,128]{1,0:T(8,128)S(1)}, u32[]{:S(2)}, u32[]{:S(2)}) collective-permute-start(f32[208,128]{1,0:T(8,128)S(1)} %dynamic-slice_add_fusion), channel_id=1, source_target_pairs={{0,2},{1,9},{2,0},{3,11},{4,6},{5,13},{6,4},{7,15},{8,10},{9,1},{1... | collective-permute-start | bytes 319496 | tf_op jit(solution)/shard_map/ppermute | solution.py:627
  40.6 6.2 %collective-permute-start.4 = (f32[208,128]{1,0:T(8,128)S(1)}, f32[208,128]{1,0:T(8,128)S(1)}, u32[]{:S(2)}, u32[]{:S(2)}) collective-permute-start(f32[208,128]{1,0:T(8,128)S(1)} %add.37), channel_id=1, source_target_pairs={{0,8},{1,5},{2,10},{3,7},{4,12},{5,1},{6,14},{7,3},{8,0},{9,13},{1... | collective-permute-start | bytes 319496 | tf_op jit(solution)/shard_map/ppermute | solution.py:627
  43.5 9.6 %copy-start.1 = (f32[259,384]{1,0:T(8,128)S(1)}, f32[259,384]{1,0:T(8,128)}, u32[]{:S(2)}) copy-start(f32[259,384]{1,0:T(8,128)} %refs_1_.1) | copy-start | bytes 1193476
  43.5 9.6 %copy-start.2 = (f32[259,384]{1,0:T(8,128)S(1)}, f32[259,384]{1,0:T(8,128)}, u32[]{:S(2)}) copy-start(f32[259,384]{1,0:T(8,128)} %refs_2_.1) | copy-start | bytes 1193476
  43.5 9.6 %copy-start.6 = (f32[5,384]{1,0:T(8,128)S(1)}, f32[5,384]{1,0:T(8,128)}, u32[]{:S(2)}) copy-start(f32[5,384]{1,0:T(8,128)} %refs_4_.1) | copy-start | bytes 23044
  43.5 9.6 %copy-start.7 = (f32[5,384]{1,0:T(8,128)S(1)}, f32[5,384]{1,0:T(8,128)}, u32[]{:S(2)}) copy-start(f32[5,384]{1,0:T(8,128)} %refs_5_.1) | copy-start | bytes 23044
  43.5 9.6 %copy-start.8 = (f32[8,384]{1,0:T(8,128)S(1)}, f32[8,384]{1,0:T(8,128)}, u32[]{:S(2)}) copy-start(f32[8,384]{1,0:T(8,128)} %refs_7_.1) | copy-start | bytes 36868
  43.5 9.6 %copy-start.9 = (f32[8,384]{1,0:T(8,128)S(1)}, f32[8,384]{1,0:T(8,128)}, u32[]{:S(2)}) copy-start(f32[8,384]{1,0:T(8,128)} %refs_8_.1) | copy-start | bytes 36868
  43.5 9.6 %copy-start.12 = (s32[3]{0:T(128)S(1)}, s32[3]{0:T(128)}, u32[]{:S(2)}) copy-start(s32[3]{0:T(128)} %owner_ref.1) | copy-start | bytes 40
  46.8 4.8 %collective-permute-start.5 = (f32[208,128]{1,0:T(8,128)S(1)}, f32[208,128]{1,0:T(8,128)S(1)}, u32[]{:S(2)}, u32[]{:S(2)}) collective-permute-start(f32[208,128]{1,0:T(8,128)S(1)} %add.38), channel_id=1, source_target_pairs={{0,4},{1,3},{2,6},{3,1},{4,0},{5,7},{6,2},{7,5},{8,12},{9,11},{10,... | collective-permute-start | bytes 319496 | tf_op jit(solution)/shard_map/ppermute | solution.py:627
  51.6 1.5 %collective-permute-start.6 = (f32[416,128]{1,0:T(8,128)S(1)}, f32[416,128]{1,0:T(8,128)S(1)}, u32[]{:S(2)}, u32[]{:S(2)}) collective-permute-start(f32[416,128]{1,0:T(8,128)S(1)} %pad_maximum_fusion.mine_ref), channel_id=1, source_target_pairs={{0,1},{1,0},{2,3},{3,2},{4,5},{5,4},{6,7},{7,6},{8,9},{9,8},{10,11... | collective-permute-start | bytes 638984 | tf_op jit(solution)/shard_map/ppermute | solution.py:627

commit v7 on v6

--- a/solution.py
+++ b/solution.py
@@ -212,8 +212,8 @@
             send_conv(0, u).wait()
 
         look_up(q, u)
+        convolve(q, u)
         send(q, u).start()
-        convolve(q, u)
         send_conv(q, u).start()
 
     @pl.when(n == pl.num_programs(0) - 1)

time: 56 us -> 56 us (level)
  no operation moved by 1% of the time
where the time goes in v7:
time: 56 us; the launch traced here: 55.8 us
  Pallas kernels  30.8 us (55%)
  starting transfers between devices  11.8 us (21%)
  waiting for transfers between devices  7.02 us (13%)
  local copies, waits for them, and re-layouts  5.02 us (9%)
  between operations  0.99 us (2%)
    pallas_call x4, Pallas kernels, call(): pl.pallas_call(kernel, grid_spec=pltpu.PrefetchScalarGridSpec(num_scalar_...  25 us
    ppermute x6, starting transfers between devices, swap(): lax.ppermute(x, 'seq', [(i, i ^ (odd_step if i % 2 else step)) for i in r...  8.85 us
    ppermute x6, waiting for transfers between devices, swap(): lax.ppermute(x, 'seq', [(i, i ^ (odd_step if i % 2 else step)) for i in r...  5.77 us
    pallas_call x2, Pallas kernels, pooled_two(): pl.pallas_call(functools.partial(pooled_kernel, first), in_specs=[pl.Bloc...  5.74 us
    transpose x1, local copies, waits for them, and re-layouts, local(): pooled = pooled.transpose(0, 2, 1, 3).reshape(seqs, half_rows, chans)  3.25 us
    ppermute x1, starting transfers between devices, local(): other = lax.ppermute(inner, 'blk', [(0, 1), (1, 0)])  3 us
    reshape x1, local copies, waits for them, and re-layouts, local(): planes = cotangent.reshape(seqs, rows, 6, chans).transpose(0, 2, 1, 3)  1.69 us
    ppermute x1, waiting for transfers between devices, local(): other = lax.ppermute(inner, 'blk', [(0, 1), (1, 0)])  1.25 us
  transfers between devices with their start and end apart: 7, of which 5 were waited for; matrix products, arithmetic and copies ran while one was open for 6% of the time, Pallas kernels for 12%

profile of v7, /device:TPU:0, one launch (start us, length us, event | category | flops | bytes accessed | tf_op | source)
XLA Modules:
  0.0 55.8 jit_solution(17038233828478664303)
XLA Ops:
  0.6 0.0 copy-start.4
  0.7 0.0 copy-start.3
  0.7 1.7 %copy.28 = bf16[4,86,6,384]{3,1,2,0:T(8,128)(2,1)S(1)} copy(bf16[4,86,6,384]{3,0,2,1:T(4,128)(2,1)} %bitcast.20) | data formatting | bytes 3170304 | tf_op jit(solution)/shard_map/reshape | solution.py:563
  2.5 10.4 %forward.1 = (bf16[4,1152,384]{2,1,0:T(8,128)(2,1)}, f32[4,12,88,384]{3,2,1,0:T(8,128)}, f32[4,96,128]{2,1,0:T(8,128)S(1)}, f32[4,32,128]{2,1,0:T(8,128)S(1)}, f32[4,8,1152]{2,1,0:T(8,128)S(1)}) custom-call(s32[1]{0:T(128)} %bitcast.half_ref, s32[4]{0:T(128)S(1)} %copy-done.10, s32[4]{0:T(128)S(1)} %copy-done.11, s32[4,1032]{1,0:T(4,128)S(1)} %copy-done.5, ...), custom_call_target="tpu_custom_call" | custom-call | tf_op jit(solution)/shard_map/forward/pallas_call | solution.py:550
  12.9 3.0 %collective-permute-start = (f32[4,32,128]{2,1,0:T(8,128)S(1)}, f32[4,32,128]{2,1,0:T(8,128)S(1)}, u32[]{:S(2)}, u32[]{:S(2)}) collective-permute-start(f32[4,32,128]{2,1,0:T(8,128)S(1)} %get-tuple-element.41.inner_ref), channel_id=1, source_target_pairs={{0,16},{16,0},{1,17},{17,1},{2,18},{18,2},{3,19},{19,3},{4,20},{20... | collective-permute-start | bytes 196616 | tf_op jit(solution)/shard_map/ppermute | solution.py:592
  15.9 1.0 %scores.1 = (f32[48,8,128]{2,1,0:T(8,128)S(1)}, f32[4,32,128]{2,1,0:T(8,128)S(1)}) custom-call(s32[4]{0:T(128)S(1)} %copy-done.10, s32[4]{0:T(128)S(1)} %copy-done.11, f32[4,96,128]{2,1,0:T(8,128)S(1)} %get-tuple-element.42.look_ref, f32[5,768]{1,0:T(8,128)S(1)} %copy-done.3, f32[8,768]{1,0:T(8,128)S(1)} %copy-done.4), custom_call_target="tpu_custom_call" | custom-call | tf_op jit(solution)/shard_map/scores/pallas_call | solution.py:550
  16.9 1.3 %collective-permute-done.other_ref = f32[4,32,128]{2,1,0:T(8,128)S(1)} collective-permute-done((f32[4,32,128]{2,1,0:T(8,128)S(1)}, f32[4,32,128]{2,1,0:T(8,128)S(1)}, u32[]{:S(2)}, u32[]{:S(2)}) %collective-permute-start) | collective-permute-done | bytes 65568 | tf_op jit(solution)/shard_map/ppermute | solution.py:592
  18.1 11.0 %backward.1 = (f32[416,128]{1,0:T(8,128)S(1)}, f32[416,128]{1,0:T(8,128)S(1)}) custom-call(s32[1]{0:T(128)} %bitcast.half_ref, s32[4]{0:T(128)S(1)} %copy-done.10, s32[4]{0:T(128)S(1)} %copy-done.11, s32[1]{0:T(128)} %bitcast.1.core_ref, f32[4,8,1152]{2,1,0:T(8,128)S(1)} %get-tuple-element.39.rows_ref, bf16[4,6,86,384]{3,2,1,0:T(8,128)(2,1)S(1)} %bitcast.18, ...), custom_call_target="tpu_custom_call" | custom-call | tf_op jit(solution)/shard_map/backward/pallas_call | solution.py:550
  29.1 0.1 collective-permute-start.1
  29.3 1.4 %collective-permute-done.1 = f32[416,128]{1,0:T(8,128)S(1)} collective-permute-done((f32[416,128]{1,0:T(8,128)S(1)}, f32[416,128]{1,0:T(8,128)S(1)}, u32[]{:S(2)}, u32[]{:S(2)}) %collective-permute-start.1) | collective-permute-done | bytes 213024 | tf_op jit(solution)/shard_map/ppermute | solution.py:627
  30.7 2.2 %collective-permute-start.2 = (f32[208,128]{1,0:T(8,128)S(1)}, f32[208,128]{1,0:T(8,128)S(1)}, u32[]{:S(2)}, u32[]{:S(2)}) collective-permute-start(f32[208,128]{1,0:T(8,128)S(1)} %constant_dynamic-slice_fusion), channel_id=1, source_target_pairs={{0,4},{1,3},{2,6},{3,1},{4,0},{5,7},{6,2},{7,5},{8,12},{9,11},{10,... | collective-permute-start | bytes 319496 | tf_op jit(solution)/shard_map/ppermute | solution.py:627
  32.9 2.9 %pooled.2.refs_0_ = bf16[4,6,86,384]{3,2,1,0:T(8,128)(2,1)} custom-call(f32[4,32,128]{2,1,0:T(8,128)S(1)} %get-tuple-element.46.coef_ref.refs_0_.refs_1_, f32[4,12,88,384]{3,2,1,0:T(8,128)} %get-tuple-element.52.refs_1_.refs_2_), custom_call_target="tpu_custom_call" | custom-call | tf_op jit(solution)/shard_map/pooled/pallas_call | solution.py:631
  35.8 0.0 collective-permute-done.2
  35.8 1.8 %collective-permute-start.3 = (f32[208,128]{1,0:T(8,128)S(1)}, f32[208,128]{1,0:T(8,128)S(1)}, u32[]{:S(2)}, u32[]{:S(2)}) collective-permute-start(f32[208,128]{1,0:T(8,128)S(1)} %dynamic-slice_add_fusion), channel_id=1, source_target_pairs={{0,2},{1,9},{2,0},{3,11},{4,6},{5,13},{6,4},{7,15},{8,10},{9,1},{1... | collective-permute-start | bytes 319496 | tf_op jit(solution)/shard_map/ppermute | solution.py:627
  37.6 2.9 %pooled.3 = bf16[4,6,86,384]{3,2,1,0:T(8,128)(2,1)} custom-call(bf16[4,6,86,384]{3,2,1,0:T(8,128)(2,1)} %pooled.2.refs_0_, f32[4,32,128]{2,1,0:T(8,128)S(1)} %get-tuple-element.46.coef_ref.refs_0_.refs_1_, f32[4,12,88,384]{3,2,1,0:T(8,128)} %get-tuple-element.52.refs_1_.refs_2_), custom_call_target="tpu_custom_call", output_to_operand_aliasing={{}: (0, {})} | custom-call | tf_op jit(solution)/shard_map/pooled/pallas_call | solution.py:631
  40.5 0.1 collective-permute-done.3
  40.6 2.9 %collective-permute-start.4 = (f32[208,128]{1,0:T(8,128)S(1)}, f32[208,128]{1,0:T(8,128)S(1)}, u32[]{:S(2)}, u32[]{:S(2)}) collective-permute-start(f32[208,128]{1,0:T(8,128)S(1)} %add.37), channel_id=1, source_target_pairs={{0,8},{1,5},{2,10},{3,7},{4,12},{5,1},{6,14},{7,3},{8,0},{9,13},{1... | collective-permute-start | bytes 319496 | tf_op jit(solution)/shard_map/ppermute | solution.py:627
  43.5 0.0 copy-start.8
  43.5 0.0 copy-start.9
  43.5 0.0 copy-start.12
  43.5 3.2 %copy.26 = bf16[4,86,6,384]{3,0,2,1:T(4,128)(2,1)} copy(bf16[4,86,6,384]{3,1,2,0:T(8,128)(2,1)} %bitcast.19) | data formatting | bytes 3170304 | tf_op jit(solution)/shard_map/transpose | solution.py:666
  46.8 0.0 collective-permute-done.4
  46.8 1.8 %collective-permute-start.5 = (f32[208,128]{1,0:T(8,128)S(1)}, f32[208,128]{1,0:T(8,128)S(1)}, u32[]{:S(2)}, u32[]{:S(2)}) collective-permute-start(f32[208,128]{1,0:T(8,128)S(1)} %add.38), channel_id=1, source_target_pairs={{0,4},{1,3},{2,6},{3,1},{4,0},{5,7},{6,2},{7,5},{8,12},{9,11},{10,... | collective-permute-start | bytes 319496 | tf_op jit(solution)/shard_map/ppermute | solution.py:627
  48.6 3.0 %collective-permute-done.5 = f32[208,128]{1,0:T(8,128)S(1)} collective-permute-done((f32[208,128]{1,0:T(8,128)S(1)}, f32[208,128]{1,0:T(8,128)S(1)}, u32[]{:S(2)}, u32[]{:S(2)}) %collective-permute-start.5) | collective-permute-done | bytes 106528 | tf_op jit(solution)/shard_map/ppermute | solution.py:627
  51.6 0.1 collective-permute-start.6
  51.7 0.1 pad_add_fusion.place_ref
  51.8 1.4 %collective-permute-done.6.other_ref = f32[416,128]{1,0:T(8,128)S(1)} collective-permute-done((f32[416,128]{1,0:T(8,128)S(1)}, f32[416,128]{1,0:T(8,128)S(1)}, u32[]{:S(2)}, u32[]{:S(2)}) %collective-permute-start.6) | collective-permute-done | bytes 213024 | tf_op jit(solution)/shard_map/ppermute | solution.py:627
  53.1 0.0 copy-done.7
  53.1 0.0 copy-done.8
  53.2 0.0 copy-done.9
  53.2 0.0 copy-done.12
  53.2 2.6 %update.1 = (f32[259,1,384]{2,1,0:T(1,128)}, f32[259,1,384]{2,1,0:T(1,128)}, f32[259,1,384]{2,1,0:T(1,128)}, f32[5,1,384]{2,1,0:T(1,128)}, f32[5,1,384]{2,1,0:T(...) custom-call(s32[1]{0:T(128)} %bitcast.half_ref, ...), custom_call_target="tpu_custom_call" | custom-call | tf_op jit(solution)/shard_map/update/pallas_call | solution.py:550
  (23 shorter events, 0.1 us)
Async XLA Ops:
  0.6 1.8 %copy-start.4 = (f32[8,768]{1,0:T(8,128)S(1)}, f32[8,768]{1,0:T(8,128)}, u32[]{:S(2)}) copy-start(f32[8,768]{1,0:T(8,128)} %refs_6_.1) | copy-start | bytes 73732
  0.7 1.8 %copy-start.3 = (f32[5,768]{1,0:T(8,128)S(1)}, f32[5,768]{1,0:T(8,128)}, u32[]{:S(2)}) copy-start(f32[5,768]{1,0:T(8,128)} %refs_3_.1) | copy-start | bytes 46084
  0.7 1.8 %copy-start = (f32[259,768]{1,0:T(8,128)S(1)}, f32[259,768]{1,0:T(8,128)}, u32[]{:S(2)}) copy-start(f32[259,768]{1,0:T(8,128)} %refs_0_.1) | copy-start | bytes 2386948
  0.7 1.8 %copy-start.11 = (s32[4]{0:T(128)S(1)}, s32[4]{0:T(128)}, u32[]{:S(2)}) copy-start(s32[4]{0:T(128)} %lang_ref.5) | copy-start | bytes 52
  0.7 1.8 %copy-start.10 = (s32[4]{0:T(128)S(1)}, s32[4]{0:T(128)}, u32[]{:S(2)}) copy-start(s32[4]{0:T(128)} %len_ref.5) | copy-start | bytes 52
  0.7 1.8 %copy-start.5 = (s32[4,1032]{1,0:T(4,128)S(1)}, s32[4,1032]{1,0:T(4,128)}, u32[]{:S(2)}) copy-start(s32[4,1032]{1,0:T(4,128)} %ids_ref.1) | copy-start | bytes 49540
  12.9 5.2 %collective-permute-start = (f32[4,32,128]{2,1,0:T(8,128)S(1)}, f32[4,32,128]{2,1,0:T(8,128)S(1)}, u32[]{:S(2)}, u32[]{:S(2)}) collective-permute-start(f32[4,32,128]{2,1,0:T(8,128)S(1)} %get-tuple-element.41.inner_ref), channel_id=1, source_target_pairs={{0,16},{16,0},{1,17},{17,1},{2,18},{18,2},{3,19},{19,3},{4,20},{20... | collective-permute-start | bytes 196616 | tf_op jit(solution)/shard_map/ppermute | solution.py:592
  29.1 1.5 %collective-permute-start.1 = (f32[416,128]{1,0:T(8,128)S(1)}, f32[416,128]{1,0:T(8,128)S(1)}, u32[]{:S(2)}, u32[]{:S(2)}) collective-permute-start(f32[416,128]{1,0:T(8,128)S(1)} %get-tuple-element.51), channel_id=1, source_target_pairs={{0,1},{1,0},{2,3},{3,2},{4,5},{5,4},{6,7},{7,6},{8,9},{9,8},{10,11... | collective-permute-start | bytes 638984 | tf_op jit(solution)/shard_map/ppermute | solution.py:627
  30.7 5.0 %collective-permute-start.2 = (f32[208,128]{1,0:T(8,128)S(1)}, f32[208,128]{1,0:T(8,128)S(1)}, u32[]{:S(2)}, u32[]{:S(2)}) collective-permute-start(f32[208,128]{1,0:T(8,128)S(1)} %constant_dynamic-slice_fusion), channel_id=1, source_target_pairs={{0,4},{1,3},{2,6},{3,1},{4,0},{5,7},{6,2},{7,5},{8,12},{9,11},{10,... | collective-permute-start | bytes 319496 | tf_op jit(solution)/shard_map/ppermute | solution.py:627
  35.8 4.8 %collective-permute-start.3 = (f32[208,128]{1,0:T(8,128)S(1)}, f32[208,128]{1,0:T(8,128)S(1)}, u32[]{:S(2)}, u32[]{:S(2)}) collective-permute-start(f32[208,128]{1,0:T(8,128)S(1)} %dynamic-slice_add_fusion), channel_id=1, source_target_pairs={{0,2},{1,9},{2,0},{3,11},{4,6},{5,13},{6,4},{7,15},{8,10},{9,1},{1... | collective-permute-start | bytes 319496 | tf_op jit(solution)/shard_map/ppermute | solution.py:627
  40.6 6.2 %collective-permute-start.4 = (f32[208,128]{1,0:T(8,128)S(1)}, f32[208,128]{1,0:T(8,128)S(1)}, u32[]{:S(2)}, u32[]{:S(2)}) collective-permute-start(f32[208,128]{1,0:T(8,128)S(1)} %add.37), channel_id=1, source_target_pairs={{0,8},{1,5},{2,10},{3,7},{4,12},{5,1},{6,14},{7,3},{8,0},{9,13},{1... | collective-permute-start | bytes 319496 | tf_op jit(solution)/shard_map/ppermute | solution.py:627
  43.5 9.6 %copy-start.1 = (f32[259,384]{1,0:T(8,128)S(1)}, f32[259,384]{1,0:T(8,128)}, u32[]{:S(2)}) copy-start(f32[259,384]{1,0:T(8,128)} %refs_1_.1) | copy-start | bytes 1193476
  43.5 9.6 %copy-start.2 = (f32[259,384]{1,0:T(8,128)S(1)}, f32[259,384]{1,0:T(8,128)}, u32[]{:S(2)}) copy-start(f32[259,384]{1,0:T(8,128)} %refs_2_.1) | copy-start | bytes 1193476
  43.5 9.6 %copy-start.6 = (f32[5,384]{1,0:T(8,128)S(1)}, f32[5,384]{1,0:T(8,128)}, u32[]{:S(2)}) copy-start(f32[5,384]{1,0:T(8,128)} %refs_4_.1) | copy-start | bytes 23044
  43.5 9.6 %copy-start.7 = (f32[5,384]{1,0:T(8,128)S(1)}, f32[5,384]{1,0:T(8,128)}, u32[]{:S(2)}) copy-start(f32[5,384]{1,0:T(8,128)} %refs_5_.1) | copy-start | bytes 23044
  43.5 9.6 %copy-start.8 = (f32[8,384]{1,0:T(8,128)S(1)}, f32[8,384]{1,0:T(8,128)}, u32[]{:S(2)}) copy-start(f32[8,384]{1,0:T(8,128)} %refs_7_.1) | copy-start | bytes 36868
  43.5 9.6 %copy-start.9 = (f32[8,384]{1,0:T(8,128)S(1)}, f32[8,384]{1,0:T(8,128)}, u32[]{:S(2)}) copy-start(f32[8,384]{1,0:T(8,128)} %refs_8_.1) | copy-start | bytes 36868
  43.5 9.6 %copy-start.12 = (s32[3]{0:T(128)S(1)}, s32[3]{0:T(128)}, u32[]{:S(2)}) copy-start(s32[3]{0:T(128)} %owner_ref.1) | copy-start | bytes 40
  46.8 4.8 %collective-permute-start.5 = (f32[208,128]{1,0:T(8,128)S(1)}, f32[208,128]{1,0:T(8,128)S(1)}, u32[]{:S(2)}, u32[]{:S(2)}) collective-permute-start(f32[208,128]{1,0:T(8,128)S(1)} %add.38), channel_id=1, source_target_pairs={{0,4},{1,3},{2,6},{3,1},{4,0},{5,7},{6,2},{7,5},{8,12},{9,11},{10,... | collective-permute-start | bytes 319496 | tf_op jit(solution)/shard_map/ppermute | solution.py:627
  51.6 1.5 %collective-permute-start.6 = (f32[416,128]{1,0:T(8,128)S(1)}, f32[416,128]{1,0:T(8,128)S(1)}, u32[]{:S(2)}, u32[]{:S(2)}) collective-permute-start(f32[416,128]{1,0:T(8,128)S(1)} %pad_maximum_fusion.mine_ref), channel_id=1, source_target_pairs={{0,1},{1,0},{2,3},{3,2},{4,5},{5,4},{6,7},{7,6},{8,9},{9,8},{10,11... | collective-permute-start | bytes 638984 | tf_op jit(solution)/shard_map/ppermute | solution.py:627
